TPU v7x, 256 devices: a whole 4x4x8 slice. The times are simulated.
256 devices in a mesh: band: 4 (over x), gvec: 16 (over z, core), dom: 4 (over y).
Axes of the slice: x: 4, y: 4, z: 8, core: 2. Of those that a mesh axis runs over, the one named last changes fastest.
Arguments:
- coeffs: bfloat16 [16, 128, 128, 128], P(('band', 'dom'), 'gvec'), may hold values from -1.5 to 1.5
- v_local: bfloat16 [128, 128, 128], P(None, 'gvec'), may hold values from -4 to 4
- atom_pos: float32 [3, 262144], P(None, ('band', 'gvec', 'dom')), may hold values from -32 to 160
- atom_charge: float32 [262144], P(('band', 'gvec', 'dom')), may hold values from -1 to 1
- near_list: int32 [4096], P(('band', 'gvec', 'dom')), may hold values from 0 to 1023, as said below
- live_count: int32 [256], P(('band', 'gvec', 'dom')), may hold values from 0 to 16, as said below
Outputs:
- waves_new: bfloat16 [16, 128, 128, 128], P(('band', 'dom'), 'gvec')
- energies: float32 [16], P(('band', 'dom'))
- resid_ratio: float32 [16], P(('band', 'dom'))
- atom_force: float32 [3, 262144], P(None, ('band', 'gvec', 'dom'))
- totals: float32 [8], replicated
Inputs may be any that keep to these rules, and one draw needn't show every extreme that they name: `live_count`: the counts of all devices sum to exactly 1024; some device has all 16 slots live; a device's live slots are its first ones. `near_list`: indices of the device's own atoms; the 16 entries of one device's block are distinct.
All inputs are finite; a program needn't handle non-finite values.
Results may differ from a plain program's by a relative error of at most 0.0045.
Values may be sent and summed in bfloat16 or wider, within the bound.
No kernel may reach another device: no remote copies, remote signals or barrier semaphores. Data moves between devices by JAX's collectives and lax.ppermute only.
A program may use at most 64 MiB of HBM per device.

v0:
```python
import jax
import jax.numpy as jnp
from jax import lax
from jax.sharding import PartitionSpec as P

sigma_fractions = (1.0 / 32.0, 1.0 / 16.0, 1.0 / 8.0, 1.0 / 4.0)
kernel_weights = (1.0, 0.5, 0.25, 0.125)
force_unit = 1.0 / 4096.0
step_size = 0.5


def cosine_table(length):
    points = jnp.arange(length).astype(jnp.float32)
    angles = jnp.pi * (points[:, None] + 0.5) * points[None, :] / length
    scales = jnp.where(points == 0.0, jnp.sqrt(1.0 / length), jnp.sqrt(2.0 / length))
    return (jnp.cos(angles) * scales[None, :]).astype(jnp.bfloat16)


def occupancy(band_index, band_total):
    shifted = band_index.astype(jnp.float32) - 0.5 * band_total
    return 2.0 / (1.0 + jnp.exp(shifted / (0.125 * band_total)))


def kernels(points, centres, extent):
    values = []
    slopes = []
    for fraction in sigma_fractions:
        exponent = 0.5 / (extent * fraction) ** 2
        offset = points[:, None] - centres[None, :]
        gauss_value = jnp.exp(-exponent * offset * offset)
        values.append(gauss_value)
        slopes.append(2.0 * exponent * offset * gauss_value)
    return (jnp.concatenate(values, axis=1), jnp.concatenate(slopes, axis=1))


def charge_work(charges, density, x_start, y_start, extent, block_width):
    x_count, y_count, z_count = density.shape
    density_rows = density.reshape(x_count * y_count, z_count).astype(jnp.bfloat16)
    x_points = (x_start + jnp.arange(x_count)).astype(jnp.float32)
    y_points = (y_start + jnp.arange(y_count)).astype(jnp.float32)
    z_points = jnp.arange(z_count).astype(jnp.float32)
    weights = jnp.array(kernel_weights, jnp.float32)
    slot_total = charges.shape[1]
    blocks = charges.reshape(4, slot_total // block_width, block_width).transpose(1, 0, 2)

    def one_block(potential, block_now):
        x_value, x_slope = kernels(x_points, block_now[0], extent)
        y_value, y_slope = kernels(y_points, block_now[1], extent)
        z_value, z_slope = kernels(z_points, block_now[2], extent)
        scaled = (weights[:, None] * block_now[3][None, :]).reshape(-1)
        plane = (
            (x_value[:, None, :] * y_value[None, :, :])
            .reshape(x_count * y_count, -1)
            .astype(jnp.bfloat16)
        )
        depth = (scaled[None, :] * z_value).astype(jnp.bfloat16)
        potential = potential + lax.dot_general(
            plane, depth, (((1,), (1,)), ((), ())), preferred_element_type=jnp.float32
        )
        tables = jnp.concatenate([z_value, z_slope], axis=1).astype(jnp.bfloat16)
        projected = jnp.dot(density_rows, tables, preferred_element_type=jnp.float32).reshape(
            x_count, y_count, 2, -1
        )
        grid_part = projected[:, :, 0, :]
        slope_part = projected[:, :, 1, :]
        along_y = jnp.sum(grid_part * y_value[None], axis=1)
        slope_y = jnp.sum(grid_part * y_slope[None], axis=1)
        depth_y = jnp.sum(slope_part * y_value[None], axis=1)
        force_x = jnp.sum(x_slope * along_y, axis=0)
        force_y = jnp.sum(x_value * slope_y, axis=0)
        force_z = jnp.sum(x_value * depth_y, axis=0)
        stacked = jnp.stack([force_x, force_y, force_z]) * scaled[None, :]
        forces = -force_unit * jnp.sum(stacked.reshape(3, len(kernel_weights), -1), axis=1)
        return (potential, forces)

    start = jnp.zeros((x_count * y_count, z_count), jnp.float32)
    potential, forces = lax.scan(one_block, start, blocks)
    return (
        potential.reshape(x_count, y_count, z_count),
        forces.transpose(1, 0, 2).reshape(3, slot_total),
    )


def stress_terms(weighted, x_wave, y_wave):
    over_z = jnp.sum(weighted, axis=2)
    over_y = jnp.sum(weighted, axis=1)
    over_x = jnp.sum(weighted, axis=0)
    stress_xx = jnp.sum(x_wave * x_wave * jnp.sum(over_z, axis=1))
    stress_yy = jnp.sum(y_wave * y_wave * jnp.sum(over_z, axis=0))
    stress_zz = jnp.sum(y_wave * y_wave * jnp.sum(over_y, axis=0))
    stress_xy = jnp.sum(x_wave[:, None] * y_wave[None, :] * over_z)
    stress_xz = jnp.sum(x_wave[:, None] * y_wave[None, :] * over_y)
    stress_yz = jnp.sum(y_wave[:, None] * y_wave[None, :] * over_x)
    return jnp.stack([stress_xx, stress_yy, stress_zz, stress_xy, stress_xz, stress_yz])


def per_device(coeffs, v_local, atom_pos, atom_charge, near_list, live_count):
    local_bands, x_local, extent, _ = coeffs.shape
    cosines = cosine_table(extent)
    gvec_id = lax.axis_index("gvec")
    group_id = lax.axis_index(("band", "dom"))
    groups = lax.axis_size(("band", "dom"))
    band_total = local_bands * groups
    cell_count = float(extent**3)
    band_ids = group_id * local_bands + jnp.arange(local_bands)
    weight = occupancy(band_ids, band_total)
    capacity = near_list.shape[0]
    live_mask = (jnp.arange(capacity) < live_count[0]).astype(jnp.float32)
    picked_pos = jnp.take(atom_pos, near_list, axis=1)
    picked_charge = jnp.take(atom_charge, near_list) * live_mask
    own_block = jnp.concatenate([picked_pos, picked_charge[None, :], live_mask[None, :]], axis=0)
    all_blocks = lax.all_gather(own_block, ("band", "gvec", "dom"), axis=1, tiled=True)
    live_total = all_blocks.shape[1] // 4
    block_width = min(1024, live_total)
    charges = all_blocks[:4]
    sectioned = jnp.einsum(
        "naql,zl->naqz", coeffs, cosines, preferred_element_type=jnp.float32
    ).astype(jnp.bfloat16)
    sectioned = jnp.einsum(
        "naqz,yq->nayz", sectioned, cosines, preferred_element_type=jnp.float32
    ).astype(jnp.bfloat16)
    exchanged = lax.all_to_all(sectioned, "gvec", split_axis=2, concat_axis=1, tiled=True)
    real_space = jnp.einsum(
        "nayz,xa->nxyz", exchanged, cosines, preferred_element_type=jnp.float32
    ).astype(jnp.bfloat16)
    x_share = extent // groups
    y_share = exchanged.shape[2]
    x_start = group_id * x_share
    y_start = gvec_id * y_share
    wide_real = real_space.astype(jnp.float32)
    partial_value = jnp.sum(weight[:, None, None, None] * wide_real * wide_real, axis=0)
    density = lax.psum_scatter(
        partial_value.astype(jnp.bfloat16), ("band", "dom"), scatter_dimension=0, tiled=True
    ).astype(jnp.float32)
    potential, forces = charge_work(charges, density, x_start, y_start, extent, block_width)
    slab_field = lax.all_gather(potential.astype(jnp.bfloat16), ("band", "dom"), axis=0, tiled=True)
    field_total = v_local.astype(jnp.float32) + slab_field.astype(jnp.float32)
    applied = (field_total[None] * wide_real).astype(jnp.bfloat16)
    embedding = jnp.sum(density * potential) / cell_count
    mine = lax.psum_scatter(forces, ("band", "gvec", "dom"), scatter_dimension=1, tiled=True)
    atom_force = jnp.zeros((3, atom_pos.shape[1]), jnp.float32).at[:, near_list].add(mine)
    back_one = jnp.einsum(
        "nxyz,xa->nayz", applied, cosines, preferred_element_type=jnp.float32
    ).astype(jnp.bfloat16)
    returned = lax.all_to_all(back_one, "gvec", split_axis=1, concat_axis=2, tiled=True)
    back_two = jnp.einsum(
        "nayz,yq->naqz", returned, cosines, preferred_element_type=jnp.float32
    ).astype(jnp.bfloat16)
    wave_field = jnp.einsum("naqz,zl->naql", back_two, cosines, preferred_element_type=jnp.float32)
    wave_step = jnp.pi / extent
    x_wave = (gvec_id * x_local + jnp.arange(x_local)).astype(jnp.float32) * wave_step
    y_wave = jnp.arange(extent).astype(jnp.float32) * wave_step
    kinetic = 0.5 * (
        x_wave[:, None, None] ** 2 + y_wave[None, :, None] ** 2 + y_wave[None, None, :] ** 2
    )
    coeff_wide = coeffs.astype(jnp.float32)
    image = kinetic[None] * coeff_wide + wave_field
    norm_sq = jnp.sum(coeff_wide * coeff_wide, axis=(1, 2, 3))
    intersection = jnp.sum(coeff_wide * image, axis=(1, 2, 3))
    weighted = jnp.sum(weight[:, None, None, None] * coeff_wide * coeff_wide, axis=0)
    stress_local = stress_terms(weighted, x_wave, y_wave) / cell_count
    local_totals = jnp.concatenate([stress_local, embedding[None]])
    spread = (jnp.arange(band_total)[None, :] == band_ids[:, None]).astype(jnp.float32)
    norm_vec = jnp.sum(spread * norm_sq[:, None], axis=0)
    intersection_vec = jnp.sum(spread * intersection[:, None], axis=0)
    norm_all, intersection_all, summed = lax.psum(
        (norm_vec, intersection_vec, local_totals), ("band", "gvec", "dom")
    )
    energy_all = intersection_all / norm_all
    energies = jnp.sum(spread * energy_all[None, :], axis=1)
    residual = image - energies[:, None, None, None] * coeff_wide
    resid_sq = lax.psum(jnp.sum(residual * residual, axis=(1, 2, 3)), "gvec")
    norm_mine = jnp.sum(spread * norm_all[None, :], axis=1)
    resid_ratio = resid_sq / norm_mine
    waves_new = (coeff_wide - step_size * residual / (1.0 + kinetic[None])).astype(jnp.bfloat16)
    band_energy = jnp.sum(occupancy(jnp.arange(band_total), band_total) * energy_all) / band_total
    totals = jnp.concatenate([summed, band_energy[None]])
    return (waves_new, energies, resid_ratio, atom_force, totals)


def solution(mesh):
    return jax.shard_map(
        per_device,
        mesh=mesh,
        in_specs=(
            P(("band", "dom"), "gvec", None, None),
            P(None, "gvec", None),
            P(None, ("band", "gvec", "dom")),
            P(("band", "gvec", "dom")),
            P(("band", "gvec", "dom")),
            P(("band", "gvec", "dom")),
        ),
        out_specs=(
            P(("band", "dom"), "gvec", None, None),
            P(("band", "dom")),
            P(("band", "dom")),
            P(None, ("band", "gvec", "dom")),
            P(),
        ),
        check_vma=False,
    )
```

profile of v0, /device:TPU:1, one launch (start us, length us, event | category | flops | bytes accessed | tf_op | source)
XLA Modules:
  0.0 1582.4 jit_solution(9153703159760052844)
XLA Ops:
  7.2 1.7 fusion.53
  8.9 0.9 copy.64
  9.8 10.0 all-to-all-start
  19.9 0.7 compare_select_fusion
  21.2 0.9 copy.59
  22.2 0.6 gather_fusion.1
  23.6 7.9 all-to-all-done
  31.5 1.2 fusion.62
  32.9 102.6 %all-gather = f32[256,16,5]{1,2,0:T(8,128)S(1)} all-gather(f32[1,16,5]{1,2,0:T(8,128)S(1)} %bitcast.187), channel_id=1, replica_groups=mesh['band'=4,'gvec'=16,'dom'=4] {'band','gvec','dom'}, dimensions={0}, use_global_device_ids=true | all-gather | bytes 82240 | tf_op jit(solution)/shard_map/all_gather | solution.py:112
  137.4 0.7 constant_dynamic-slice_fusion.4
  138.1 18.2 %while.14 = (s32[]{:T(128)}, f32[64,128]{1,0:T(8,128)S(1)}, f32[4,3,1024]{2,1,0:T(4,128)S(1)}, f32[4,4,1024]{2,0,1:T(4,128)S(1)}, bf16[64,128]{1,0:T(8,128)(2,1)...) while((s32[]{:T(128)}, f32[64,128]{1,0:T(8,128)S(1)}, ...), condition=%wide.region_9.10_spmd.clone.clone, body=%wide.region_1.9_spmd.sunk.clone.clone.sunk | while | flops 213295264 | bytes 15844695 | solution.py:77
  140.3 1.1 multiply_reduce_fusion.12
  144.8 1.1 multiply_reduce_fusion.12
  149.4 1.1 multiply_reduce_fusion.12
  153.9 1.1 multiply_reduce_fusion.12
  156.3 18.0 %all_gather.7 = bf16[128,8,128]{2,0,1:T(8,128)(2,1)S(1)} all-gather(bf16[8,8,128]{2,0,1:T(8,128)(2,1)S(1)} %copy.109), channel_id=1, replica_groups=mesh['band'=4,'gvec'=16,'dom'=4] {'band','dom'}, dimensions={0}, use_global_device_ids=true | all-gather | bytes 278528 | tf_op jit(solution)/shard_map/all_gather | solution.py:136
  174.8 0.9 copy.70
  175.7 9.9 all-to-all-start.1
  185.7 2.0 copy.83
  189.0 1263.7 %reduce-scatter.5.cloned.1.call-done = f32[16,3]{1,0:T(8,128)} async-done(((f32[4096,3]{1,0:T(8,128)}), f32[16,3]{1,0:T(8,128)}) %reduce-scatter.5.cloned.1.call-update) | async-done | bytes 208
  1452.7 0.8 copy.84
  1453.6 0.8 scatter_custom_fusion
  1454.4 0.8 copy.75
  1455.2 1.6 fusion.56
  1457.4 0.7 multiply_reduce_fusion.7
  1458.1 0.7 multiply_reduce_fusion.5
  1458.8 0.7 fusion.99
  1459.5 3.8 stack.39
  1463.4 1.3 fusion.102
  1464.7 79.4 %all-reduce.1 = (f32[16]{0:T(128)S(1)}, f32[16]{0:T(128)S(1)}, f32[7]{0:T(128)S(1)}) all-reduce(f32[16]{0:T(128)S(1)} %get-tuple-element.228, f32[16]{0:T(128)S(1)} %get-tuple-element.227, f32[7]{0:T(128)S(1)} %pad_maximum_fusion.3), channel_id=1, replica_groups=mesh['band'=4,'gvec'=16,'dom'=4] {'band','gvec','dom'}, use_global_device_ids=true, to_apply=%region_11.12 | all-reduce | flops 39 | bytes 312 | tf_op jit(solution)/shard_map/psum | solution.py:166
  1545.3 2.2 multiply_reduce_fusion.4
  1547.5 24.3 %psum.30 = f32[1]{0:T(128)} all-reduce(f32[1]{0:T(128)} %bitcast.28), channel_id=1, replica_groups=mesh['band'=4,'gvec'=16,'dom'=4] {'gvec'}, use_global_device_ids=true, to_apply=%region_16.17 | all-reduce | flops 1 | bytes 8 | tf_op jit(solution)/shard_map/psum | solution.py:172
  (159 shorter events, 19.3 us)
Async XLA Ops:
  7.2 15.0 copy-start
  7.2 16.2 %copy-start.4 = (s32[16]{0:T(128)S(1)}, s32[16]{0:T(128)}, u32[]{:S(2)}) copy-start(s32[16]{0:T(128)} %param.13) | copy-start | bytes 196
  9.8 21.7 %all-to-all-start = ((bf16[1,8,128,128]{3,1,0,2:T(8,128)(2,1)}), bf16[1,8,128,128]{3,1,0,2:T(8,128)(2,1)S(1)}, u32[]{:S(2)}, u32[]{:S(2)}) async-start(bf16[1,8,128,128]{3,1,0,2:T(8,128)(2,1)} %copy.64), calls=%async_computation | async-start | bytes 524288 | tf_op jit(solution)/shard_map/all_to_all | solution.py:122
  19.8 117.6 %all-reduce.4.cloned.1.call-start = ((), (), s32[]{:S(2)}) async-start(), calls=%async_computation.4 | async-start | bytes 524288
  32.7 103.4 %copy-start.5 = (u32[256]{0:T(256)S(1)}, u32[256]{0:T(256)}, u32[]{:S(2)}) copy-start(u32[256]{0:T(256)} %constant.149) | copy-start | bytes 3076
  32.7 105.4 %copy-start.3 = (f32[4]{0:T(128)S(1)}, f32[4]{0:T(128)}, u32[]{:S(2)}) copy-start(f32[4]{0:T(128)} %constant.140.clone..sunk.3) | copy-start | bytes 52
  138.1 36.2 %copy-start.2 = (bf16[128,8,128]{2,1,0:T(8,128)(2,1)S(1)}, bf16[128,8,128]{2,1,0:T(8,128)(2,1)}, u32[]{:S(2)}) copy-start(bf16[128,8,128]{2,1,0:T(8,128)(2,1)} %param.10) | copy-start | bytes 786436
  175.7 1279.5 %all-to-all-start.1 = ((bf16[1,128,8,128]{3,2,0,1:T(8,128)(2,1)}), bf16[1,128,8,128]{3,2,0,1:T(8,128)(2,1)S(1)}, u32[]{:S(2)}, u32[]{:S(2)}) async-start(bf16[1,128,8,128]{3,2,0,1:T(8,128)(2,1)} %copy.70), calls=%async_computation.1 | async-start | bytes 524288 | tf_op jit(solution)/shard_map/all_to_all | solution.py:145
  185.6 1267.2 %reduce-scatter.5.cloned.1.call-start = ((), (), s32[]{:S(2)}) async-start(), calls=%async_computation.3 | async-start | bytes 2105344
  187.7 1267.5 %copy-start.1 = (bf16[1,8,128,128]{3,2,1,0:T(8,128)(2,1)S(1)}, bf16[1,8,128,128]{3,2,1,0:T(8,128)(2,1)}, u32[]{:S(2)}) copy-start(bf16[1,8,128,128]{3,2,1,0:T(8,128)(2,1)} %param.9) | copy-start | bytes 786436
Sparse Core Ops, SparseCore 0:
  32.8 89.7 all-reduce.3
  189.0 1263.6 reduce-scatter.4
where the time goes:
time: 1580 us
  waiting for transfers between devices  1270 us (80%)
  blocking collectives  224 us (14%)
  other arithmetic  24 us (2%)
  starting transfers between devices  19.9 us (1%)
  between operations  19.5 us (1%)
    unnamed x4, waiting for transfers between devices  1260 us
    all_gather x1, blocking collectives, per_device(): lax.all_gather(own_block, ('band', 'gvec', 'dom'), axis=1, tiled=True)  103 us
    psum x1, blocking collectives, per_device(): lax.psum((norm_vec, intersection_vec, local_totals), ('band', 'gvec', 'do...  79.4 us
  transfers between devices with their start and end apart: 4, of which 2 were waited for; matrix products, arithmetic and copies ran while one was open for 1% of the time, Pallas kernels for 0%

commit v1 on v0

--- a/solution.py
+++ b/solution.py
@@ -94,6 +94,13 @@
     return jnp.stack([stress_xx, stress_yy, stress_zz, stress_xy, stress_xz, stress_yz])
 
 
+def spread_out(block, axes):
+    copies = lax.axis_size(axes)
+    many = jnp.broadcast_to(block[None], (copies,) + block.shape)
+    got = lax.all_to_all(many, axes, split_axis=0, concat_axis=0, tiled=True)
+    return got.reshape((copies * block.shape[0],) + block.shape[1:])
+
+
 def per_device(coeffs, v_local, atom_pos, atom_charge, near_list, live_count):
     local_bands, x_local, extent, _ = coeffs.shape
     cosines = cosine_table(extent)
@@ -108,11 +115,10 @@
     live_mask = (jnp.arange(capacity) < live_count[0]).astype(jnp.float32)
     picked_pos = jnp.take(atom_pos, near_list, axis=1)
     picked_charge = jnp.take(atom_charge, near_list) * live_mask
-    own_block = jnp.concatenate([picked_pos, picked_charge[None, :], live_mask[None, :]], axis=0)
-    all_blocks = lax.all_gather(own_block, ("band", "gvec", "dom"), axis=1, tiled=True)
-    live_total = all_blocks.shape[1] // 4
-    block_width = min(1024, live_total)
-    charges = all_blocks[:4]
+    own_block = jnp.concatenate([picked_pos, picked_charge[None, :]], axis=0)
+    all_blocks = spread_out(own_block.reshape(1, 4 * capacity), ("band", "gvec", "dom"))
+    charges = all_blocks.reshape(-1, 4, capacity).transpose(1, 0, 2).reshape(4, -1)
+    block_width = min(1024, charges.shape[1])
     sectioned = jnp.einsum(
         "naql,zl->naqz", coeffs, cosines, preferred_element_type=jnp.float32
     ).astype(jnp.bfloat16)
@@ -129,15 +135,23 @@
     y_start = gvec_id * y_share
     wide_real = real_space.astype(jnp.float32)
     partial_value = jnp.sum(weight[:, None, None, None] * wide_real * wide_real, axis=0)
-    density = lax.psum_scatter(
-        partial_value.astype(jnp.bfloat16), ("band", "dom"), scatter_dimension=0, tiled=True
-    ).astype(jnp.float32)
+    shares = lax.all_to_all(
+        partial_value.astype(jnp.bfloat16), ("band", "dom"), split_axis=0, concat_axis=0, tiled=True
+    )
+    density = jnp.sum(
+        shares.reshape((groups, x_share) + shares.shape[1:]).astype(jnp.float32), axis=0
+    )
     potential, forces = charge_work(charges, density, x_start, y_start, extent, block_width)
-    slab_field = lax.all_gather(potential.astype(jnp.bfloat16), ("band", "dom"), axis=0, tiled=True)
+    slab_field = spread_out(potential.astype(jnp.bfloat16), ("band", "dom"))
     field_total = v_local.astype(jnp.float32) + slab_field.astype(jnp.float32)
     applied = (field_total[None] * wide_real).astype(jnp.bfloat16)
     embedding = jnp.sum(density * potential) / cell_count
-    mine = lax.psum_scatter(forces, ("band", "gvec", "dom"), scatter_dimension=1, tiled=True)
+    owners = lax.axis_size(("band", "gvec", "dom"))
+    outgoing = forces.reshape(3, owners, capacity).transpose(1, 0, 2).reshape(owners, 3 * capacity)
+    arrived = lax.all_to_all(
+        outgoing, ("band", "gvec", "dom"), split_axis=0, concat_axis=0, tiled=True
+    )
+    mine = jnp.sum(arrived, axis=0).reshape(3, capacity)
     atom_force = jnp.zeros((3, atom_pos.shape[1]), jnp.float32).at[:, near_list].add(mine)
     back_one = jnp.einsum(
         "nxyz,xa->nayz", applied, cosines, preferred_element_type=jnp.float32
@@ -155,25 +169,35 @@
     )
     coeff_wide = coeffs.astype(jnp.float32)
     image = kinetic[None] * coeff_wide + wave_field
-    norm_sq = jnp.sum(coeff_wide * coeff_wide, axis=(1, 2, 3))
-    intersection = jnp.sum(coeff_wide * image, axis=(1, 2, 3))
+    norm_sq = jnp.sum(coeff_wide * coeff_wide)
+    intersection = jnp.sum(coeff_wide * image)
+    local_energy = intersection / jnp.maximum(norm_sq, 1e-30)
+    local_resid = jnp.sum((image - local_energy * coeff_wide) ** 2)
     weighted = jnp.sum(weight[:, None, None, None] * coeff_wide * coeff_wide, axis=0)
     stress_local = stress_terms(weighted, x_wave, y_wave) / cell_count
     local_totals = jnp.concatenate([stress_local, embedding[None]])
-    spread = (jnp.arange(band_total)[None, :] == band_ids[:, None]).astype(jnp.float32)
-    norm_vec = jnp.sum(spread * norm_sq[:, None], axis=0)
-    intersection_vec = jnp.sum(spread * intersection[:, None], axis=0)
-    norm_all, intersection_all, summed = lax.psum(
-        (norm_vec, intersection_vec, local_totals), ("band", "gvec", "dom")
-    )
-    energy_all = intersection_all / norm_all
-    energies = jnp.sum(spread * energy_all[None, :], axis=1)
+    partials = jnp.concatenate(
+        [jnp.stack([norm_sq, intersection, local_resid]), local_totals]
+    )
+    gathered = spread_out(
+        jnp.pad(partials, (0, 128 - partials.shape[0]))[None, :], ("band", "gvec", "dom")
+    )
+    by_group = gathered.reshape(
+        lax.axis_size("band"), lax.axis_size("gvec"), lax.axis_size("dom"), -1
+    ).transpose(0, 2, 1, 3).reshape(groups, -1, gathered.shape[-1])
+    norm_all = jnp.sum(by_group[:, :, 0], axis=1)
+    energy_all = jnp.sum(by_group[:, :, 1], axis=1) / norm_all
+    each_energy = by_group[:, :, 1] / jnp.maximum(by_group[:, :, 0], 1e-30)
+    resid_all = jnp.sum(
+        by_group[:, :, 2] + by_group[:, :, 0] * (each_energy - energy_all[:, None]) ** 2, axis=1
+    )
+    spread = (jnp.arange(band_total) == group_id).astype(jnp.float32)
+    energies = jnp.sum(spread * energy_all)[None]
+    resid_ratio = jnp.sum(spread * (resid_all / norm_all))[None]
     residual = image - energies[:, None, None, None] * coeff_wide
-    resid_sq = lax.psum(jnp.sum(residual * residual, axis=(1, 2, 3)), "gvec")
-    norm_mine = jnp.sum(spread * norm_all[None, :], axis=1)
-    resid_ratio = resid_sq / norm_mine
     waves_new = (coeff_wide - step_size * residual / (1.0 + kinetic[None])).astype(jnp.bfloat16)
     band_energy = jnp.sum(occupancy(jnp.arange(band_total), band_total) * energy_all) / band_total
+    summed = jnp.sum(by_group[:, :, 3:10], axis=(0, 1))
     totals = jnp.concatenate([summed, band_energy[None]])
     return (waves_new, energies, resid_ratio, atom_force, totals)
 

time: 1580 us -> 159 us (0.10)
  waiting for transfers between devices: 1270 us -> 54.1 us
  blocking collectives: 224 us -> 0 us
  starting transfers between devices: 19.9 us -> 51.1 us
    unnamed x4 -> x0, waiting for transfers between devices: 1260 us -> none
    all_gather x2 -> x0, blocking collectives: 121 us -> none  [the longest x1 103 us: per_device(): lax.all_gather(own_block, ('band', 'gvec', 'dom'), axis=1, tiled=True)]
    psum x2 -> x0, blocking collectives: 104 us -> none  [the longest x1 79.4 us: per_device(): lax.psum((norm_vec, intersection_vec, local_totals), ('band', 'gvec', 'do...]
    all_to_all x0 -> x5, waiting for transfers between devices: none -> 36.3 us  [the longest x3 29.4 us: spread_out(): got = lax.all_to_all(many, axes, split_axis=0, concat_axis=0, tiled=True)]
    all_to_all x0 -> x5, starting transfers between devices: none -> 34.6 us  [the longest x3 25.9 us: spread_out(): got = lax.all_to_all(many, axes, split_axis=0, concat_axis=0, tiled=True)]
  transfers between devices with their start and end apart: 4 -> 7, of which waited for: 2 -> 6; matrix products, arithmetic and copies ran while one was open for 1% -> 12% of each run, Pallas kernels for 0% -> 0%
where the time goes in v1:
time: 159 us; the launch traced here: 158 us
  waiting for transfers between devices  54.1 us (34%)
  starting transfers between devices  51.1 us (32%)
  other arithmetic  24.2 us (15%)
  local copies, waits for them, and re-layouts  16 us (10%)
  matrix products  8.02 us (5%)
  between operations  4.28 us (3%)
    all_to_all x3, waiting for transfers between devices, spread_out(): got = lax.all_to_all(many, axes, split_axis=0, concat_axis=0, tiled=True)  29.4 us
    all_to_all x3, starting transfers between devices, spread_out(): got = lax.all_to_all(many, axes, split_axis=0, concat_axis=0, tiled=True)  25.9 us
    all_to_all x1, waiting for transfers between devices, per_device(): lax.all_to_all(back_one, 'gvec', split_axis=1, concat_axis=2, tiled=True)  10 us
    all_to_all x1, starting transfers between devices, per_device(): lax.all_to_all(sectioned, 'gvec', split_axis=2, concat_axis=1, tiled=True)  9.98 us
    all_to_all x1, waiting for transfers between devices, per_device(): lax.all_to_all(sectioned, 'gvec', split_axis=2, concat_axis=1, tiled=True)  7.83 us
    all_to_all x1, waiting for transfers between devices, per_device(): lax.all_to_all(partial_value.astype(jnp.bfloat16), ('band', 'dom'), split...  6.86 us
    all_to_all x1, starting transfers between devices, per_device(): lax.all_to_all(back_one, 'gvec', split_axis=1, concat_axis=2, tiled=True)  6.51 us
    all_to_all x1, starting transfers between devices, per_device(): lax.all_to_all(outgoing, ('band', 'gvec', 'dom'), split_axis=0, concat_ax...  5.11 us
  transfers between devices with their start and end apart: 7, of which 6 were waited for; matrix products, arithmetic and copies ran while one was open for 12% of the time, Pallas kernels for 0%

profile of v1, /device:TPU:1, one launch (start us, length us, event | category | flops | bytes accessed | tf_op | source)
XLA Modules:
  0.0 158.5 jit_solution(6311094013539290039)
XLA Ops:
  0.7 1.7 %fusion.53 = bf16[1,8,128,128]{3,2,1,0:T(8,128)(2,1)S(1)} fusion(bf16[1,8,128,128]{3,2,1,0:T(8,128)(2,1)} %param.9, f32[128]{0:T(128)S(1)} %get-tuple-element.264, f32[128]{0:T(128)S(1)} %iota_convert_fusion.1, f32[128]{0:T(128)S(1)} %get-tuple-element.265), kind=kOutput, calls=%fused_computation.129 | convolution fusion | flops 67502080 | bytes 525824 | tf_op jit(solution)/shard_map/naqz,yq->nayz/dot_general | solution.py:125
  2.4 0.9 copy.135
  3.3 10.0 %all-to-all-start.1 = ((bf16[1,8,128,128]{3,1,0,2:T(8,128)(2,1)}), bf16[1,8,128,128]{3,1,0,2:T(8,128)(2,1)S(1)}, u32[]{:S(2)}, u32[]{:S(2)}) async-start(bf16[1,8,128,128]{3,1,0,2:T(8,128)(2,1)} %copy.135), calls=%async_computation.1 | async-start | bytes 524288 | tf_op jit(solution)/shard_map/all_to_all | solution.py:128
  14.6 0.9 copy.130
  17.1 7.8 %all-to-all-done.1 = bf16[1,8,128,128]{3,1,0,2:T(8,128)(2,1)S(1)} async-done(((bf16[1,8,128,128]{3,1,0,2:T(8,128)(2,1)}), bf16[1,8,128,128]{3,1,0,2:T(8,128)(2,1)S(1)}, u32[]{:S(2)}, u32[]{:S(2)}) %all-to-all-start.1) | async-done | bytes 262176 | tf_op jit(solution)/shard_map/all_to_all | solution.py:128
  25.7 8.6 %all-to-all-start = ((f32[256,1,64]{2,1,0:T(1,128)}), f32[256,1,64]{2,1,0:T(1,128)S(1)}, u32[]{:S(2)}, u32[]{:S(2)}) async-start(f32[256,1,64]{2,1,0:T(1,128)} %broadcast_in_dim.72), calls=%async_computation | async-start | bytes 262144 | tf_op jit(solution)/shard_map/all_to_all | solution.py:100
  34.7 0.9 copy.137
  35.6 11.4 %all-to-all-done = f32[256,1,64]{2,1,0:T(1,128)S(1)} async-done(((f32[256,1,64]{2,1,0:T(1,128)}), f32[256,1,64]{2,1,0:T(1,128)S(1)}, u32[]{:S(2)}, u32[]{:S(2)}) %all-to-all-start) | async-done | bytes 65568 | tf_op jit(solution)/shard_map/all_to_all | solution.py:100
  47.0 3.5 %all-to-all-start.2 = ((bf16[128,8,128]{2,1,0:T(8,128)(2,1)}), bf16[128,8,128]{2,1,0:T(8,128)(2,1)S(1)}, u32[]{:S(2)}, u32[]{:S(2)}) async-start(bf16[128,8,128]{2,1,0:T(8,128)(2,1)} %copy.137), calls=%async_computation.2 | async-start | bytes 524288 | tf_op jit(solution)/shard_map/all_to_all | solution.py:138
  51.2 6.9 %all-to-all-done.2 = bf16[128,8,128]{2,1,0:T(8,128)(2,1)S(1)} async-done(((bf16[128,8,128]{2,1,0:T(8,128)(2,1)}), bf16[128,8,128]{2,1,0:T(8,128)(2,1)S(1)}, u32[]{:S(2)}, u32[]{:S(2)}) %all-to-all-start.2) | async-done | bytes 262176 | tf_op jit(solution)/shard_map/all_to_all | solution.py:138
  58.1 18.4 %while.14 = (s32[]{:T(128)}, f32[64,128]{1,0:T(8,128)S(1)}, f32[4,3,1024]{2,1,0:T(4,128)S(1)}, f32[4,4,1024]{2,0,1:T(4,128)S(1)}, bf16[64,128]{1,0:T(8,128)(2,1)...) while((s32[]{:T(128)}, f32[64,128]{1,0:T(8,128)S(1)}, ...), condition=%wide.region_9.10_spmd.clone.clone, body=%wide.region_1.9_spmd.sunk.clone.clone.sunk | while | flops 213295264 | bytes 15844695 | solution.py:77
  60.3 1.1 multiply_reduce_fusion.10
  64.9 1.1 multiply_reduce_fusion.10
  69.5 1.1 multiply_reduce_fusion.10
  74.0 1.1 multiply_reduce_fusion.10
  77.1 0.8 broadcast_in_dim.73
  77.8 3.7 %all-to-all-start.3 = ((bf16[16,8,8,128]{3,1,2,0:T(8,128)(2,1)}), bf16[16,8,8,128]{3,1,2,0:T(8,128)(2,1)S(1)}, u32[]{:S(2)}, u32[]{:S(2)}) async-start(bf16[16,8,8,128]{3,1,2,0:T(8,128)(2,1)} %broadcast_in_dim.73), calls=%async_computation.3 | async-start | bytes 524288 | tf_op jit(solution)/shard_map/all_to_all | solution.py:100
  81.5 7.3 %all-to-all-done.3 = bf16[16,8,8,128]{3,1,2,0:T(8,128)(2,1)S(1)} async-done(((bf16[16,8,8,128]{3,1,2,0:T(8,128)(2,1)}), bf16[16,8,8,128]{3,1,2,0:T(8,128)(2,1)S(1)}, u32[]{:S(2)}, u32[]{:S(2)}) %all-to-all-start.3) | async-done | bytes 262176 | tf_op jit(solution)/shard_map/all_to_all | solution.py:100
  89.4 0.9 copy.144
  90.3 6.5 %all-to-all-start.4 = ((bf16[1,128,8,128]{3,2,0,1:T(8,128)(2,1)}), bf16[1,128,8,128]{3,2,0,1:T(8,128)(2,1)S(1)}, u32[]{:S(2)}, u32[]{:S(2)}) async-start(bf16[1,128,8,128]{3,2,0,1:T(8,128)(2,1)} %copy.144), calls=%async_computation.4 | async-start | bytes 524288 | tf_op jit(solution)/shard_map/all_to_all | solution.py:159
  97.2 0.8 copy.150
  98.6 10.0 %all-to-all-done.4 = bf16[1,128,8,128]{3,2,0,1:T(8,128)(2,1)S(1)} async-done(((bf16[1,128,8,128]{3,2,0,1:T(8,128)(2,1)}), bf16[1,128,8,128]{3,2,0,1:T(8,128)(2,1)S(1)}, u32[]{:S(2)}, u32[]{:S(2)}) %all-to-all-start.4) | async-done | bytes 262176 | tf_op jit(solution)/shard_map/all_to_all | solution.py:159
  108.6 5.1 %all-to-all-start.6 = ((f32[256,1,48]{2,1,0:T(1,128)}), f32[256,1,48]{2,1,0:T(1,128)S(1)}, u32[]{:S(2)}, u32[]{:S(2)}) async-start(f32[256,1,48]{2,1,0:T(1,128)} %copy.150), calls=%async_computation.6 | async-start | bytes 262144 | tf_op jit(solution)/shard_map/all_to_all | solution.py:151
  113.8 1.5 fusion.56
  118.6 4.0 %stack.51 = f32[6]{0:T(128)S(1)} concatenate(f32[1]{0:T(128)} %bitcast.31, f32[1]{0:T(128)} %bitcast.32, f32[1]{0:T(128)} %bitcast.33, f32[1]{0:T(128)} %bitcast.34, f32[1]{0:T(128)} %bitcast.35, f32[1]{0:T(128)} %bitcast.36), dimensions={0} | concatenate | bytes 48 | tf_op jit(solution)/shard_map/stack | solution.py:94
  123.8 0.7 fusion.67
  124.6 2.0 %concatenate.31 = f32[10]{0:T(128)S(1)} concatenate(f32[1]{0:T(128)} %bitcast.28, f32[1]{0:T(128)} %bitcast.29, f32[1]{0:T(128)} %bitcast.30, f32[6]{0:T(128)S(1)} %broadcast_multiply_fusion.1, f32[1]{0:T(128)} %bitcast.37), dimensions={0} | concatenate | bytes 80 | tf_op jit(solution)/shard_map/concatenate | solution.py:179
  127.3 13.7 %all-to-all-start.5 = ((f32[256,1,128]{2,1,0:T(1,128)}), f32[256,1,128]{2,1,0:T(1,128)S(1)}, u32[]{:S(2)}, u32[]{:S(2)}) async-start(f32[256,1,128]{2,1,0:T(1,128)} %broadcast_in_dim.75), calls=%async_computation.5 | async-start | bytes 262144 | tf_op jit(solution)/shard_map/all_to_all | solution.py:100
  141.5 0.8 scatter_custom_fusion
  142.3 0.8 copy.152
  143.1 10.7 %all-to-all-done.5 = f32[256,1,128]{2,1,0:T(1,128)S(1)} async-done(((f32[256,1,128]{2,1,0:T(1,128)}), f32[256,1,128]{2,1,0:T(1,128)S(1)}, u32[]{:S(2)}, u32[]{:S(2)}) %all-to-all-start.5) | async-done | bytes 131104 | tf_op jit(solution)/shard_map/all_to_all | solution.py:100
  155.7 1.6 %fusion.73 = bf16[1,8,128,128]{3,2,1,0:T(8,128)(2,1)} fusion(f32[1,8,128,128]{3,2,1,0:T(8,128)S(1)} %get-tuple-element.263, bf16[1,8,128,128]{3,2,1,0:T(8,128)(2,1)S(1)} %copy-done.1, f32[]{:T(128)} %get-tuple-element.212, f32[128]{0:T(128)S(1)} %fusion.112, f32[8,128]{1,0:T(8,128)S(1)} %broadcast_add_fusion), kind=kLoop, calls=%fused_computation.153 | loop fusion | flops 1310720 | bytes 1053188 | tf_op jit(solution)/shard_map/convert_element_type | solution.py:198
  (168 shorter events, 25.8 us)
Async XLA Ops:
  0.6 14.9 %copy-start = (f32[1024]{0:T(1024)S(1)}, f32[1024]{0:T(1024)}, u32[]{:S(2)}) copy-start(f32[1024]{0:T(1024)} %param.12) | copy-start | bytes 12292
  0.6 16.1 %copy-start.4 = (s32[16]{0:T(128)S(1)}, s32[16]{0:T(128)}, u32[]{:S(2)}) copy-start(s32[16]{0:T(128)} %param.13) | copy-start | bytes 196
  3.3 21.7 %all-to-all-start.1 = ((bf16[1,8,128,128]{3,1,0,2:T(8,128)(2,1)}), bf16[1,8,128,128]{3,1,0,2:T(8,128)(2,1)S(1)}, u32[]{:S(2)}, u32[]{:S(2)}) async-start(bf16[1,8,128,128]{3,1,0,2:T(8,128)(2,1)} %copy.135), calls=%async_computation.1 | async-start | bytes 524288 | tf_op jit(solution)/shard_map/all_to_all | solution.py:128
  17.1 41.0 %copy-start.3 = (f32[4]{0:T(128)S(1)}, f32[4]{0:T(128)}, u32[]{:S(2)}) copy-start(f32[4]{0:T(128)} %constant.142.clone..sunk.3) | copy-start | bytes 52
  25.7 21.4 %all-to-all-start = ((f32[256,1,64]{2,1,0:T(1,128)}), f32[256,1,64]{2,1,0:T(1,128)S(1)}, u32[]{:S(2)}, u32[]{:S(2)}) async-start(f32[256,1,64]{2,1,0:T(1,128)} %broadcast_in_dim.72), calls=%async_computation | async-start | bytes 262144 | tf_op jit(solution)/shard_map/all_to_all | solution.py:100
  47.0 11.0 %all-to-all-start.2 = ((bf16[128,8,128]{2,1,0:T(8,128)(2,1)}), bf16[128,8,128]{2,1,0:T(8,128)(2,1)S(1)}, u32[]{:S(2)}, u32[]{:S(2)}) async-start(bf16[128,8,128]{2,1,0:T(8,128)(2,1)} %copy.137), calls=%async_computation.2 | async-start | bytes 524288 | tf_op jit(solution)/shard_map/all_to_all | solution.py:138
  58.1 30.8 %copy-start.2 = (bf16[128,8,128]{2,1,0:T(8,128)(2,1)S(1)}, bf16[128,8,128]{2,1,0:T(8,128)(2,1)}, u32[]{:S(2)}) copy-start(bf16[128,8,128]{2,1,0:T(8,128)(2,1)} %param.10) | copy-start | bytes 786436
  77.8 35.9 %copy-start.1 = (bf16[1,8,128,128]{3,2,1,0:T(8,128)(2,1)S(1)}, bf16[1,8,128,128]{3,2,1,0:T(8,128)(2,1)}, u32[]{:S(2)}) copy-start(bf16[1,8,128,128]{3,2,1,0:T(8,128)(2,1)} %param.9) | copy-start | bytes 786436
  77.8 11.0 %all-to-all-start.3 = ((bf16[16,8,8,128]{3,1,2,0:T(8,128)(2,1)}), bf16[16,8,8,128]{3,1,2,0:T(8,128)(2,1)S(1)}, u32[]{:S(2)}, u32[]{:S(2)}) async-start(bf16[16,8,8,128]{3,1,2,0:T(8,128)(2,1)} %broadcast_in_dim.73), calls=%async_computation.3 | async-start | bytes 524288 | tf_op jit(solution)/shard_map/all_to_all | solution.py:100
  90.3 18.4 %all-to-all-start.4 = ((bf16[1,128,8,128]{3,2,0,1:T(8,128)(2,1)}), bf16[1,128,8,128]{3,2,0,1:T(8,128)(2,1)S(1)}, u32[]{:S(2)}, u32[]{:S(2)}) async-start(bf16[1,128,8,128]{3,2,0,1:T(8,128)(2,1)} %copy.144), calls=%async_computation.4 | async-start | bytes 524288 | tf_op jit(solution)/shard_map/all_to_all | solution.py:159
  108.6 18.0 %all-to-all-start.6 = ((f32[256,1,48]{2,1,0:T(1,128)}), f32[256,1,48]{2,1,0:T(1,128)S(1)}, u32[]{:S(2)}, u32[]{:S(2)}) async-start(f32[256,1,48]{2,1,0:T(1,128)} %copy.150), calls=%async_computation.6 | async-start | bytes 262144 | tf_op jit(solution)/shard_map/all_to_all | solution.py:151
  127.3 26.4 %all-to-all-start.5 = ((f32[256,1,128]{2,1,0:T(1,128)}), f32[256,1,128]{2,1,0:T(1,128)S(1)}, u32[]{:S(2)}, u32[]{:S(2)}) async-start(f32[256,1,128]{2,1,0:T(1,128)} %broadcast_in_dim.75), calls=%async_computation.5 | async-start | bytes 262144 | tf_op jit(solution)/shard_map/all_to_all | solution.py:100

commit v2 on v0

v2 whole, which is shorter than its diff:
```python
import jax
import jax.numpy as jnp
import numpy as np
from jax import lax
from jax.experimental import pallas as pl
from jax.experimental.pallas import tpu as pltpu
from jax.sharding import PartitionSpec as P

GRID = 128
CAP = 16
BANDS = 16
SHARES = 16
OWNERS = 256
LIVE = 1024
ATOMS = 1024
SIGMA_FRACTIONS = (1.0 / 32.0, 1.0 / 16.0, 1.0 / 8.0, 1.0 / 4.0)
KERNEL_WEIGHTS = (1.0, 0.5, 0.25, 0.125)
EXPONENTS = tuple(0.5 / (GRID * fraction) ** 2 for fraction in SIGMA_FRACTIONS)
FORCE_UNIT = 1.0 / 4096.0
STEP_SIZE = 0.5
WAVE_STEP = float(np.pi / GRID)
CELLS = float(GRID**3)
DEAD_MARK = 4096.0
SCALAR_LANE = 96
f32 = jnp.float32
bf16 = jnp.bfloat16
EVERY = ("gvec", "band", "dom")
GROUP = ("band", "dom")


def cosine_table():
    points = np.arange(GRID).astype(np.float32)
    angles = np.float32(np.pi) * (points[:, None] + np.float32(0.5)) * points[None, :]
    angles = (angles / np.float32(GRID)).astype(np.float32)
    scales = np.where(
        points == 0, np.sqrt(np.float32(1.0 / GRID)), np.sqrt(np.float32(2.0 / GRID))
    ).astype(np.float32)
    return jnp.asarray(np.cos(angles).astype(np.float32) * scales[None, :], bf16)


def dot_nn(a, b):
    return lax.dot_general(a, b, (((1,), (0,)), ((), ())), preferred_element_type=f32)


def dot_nt(a, b):
    return lax.dot_general(a, b, (((1,), (1,)), ((), ())), preferred_element_type=f32)


def iota(shape, dim):
    return lax.broadcasted_iota(jnp.int32, shape, dim)


def occupancy(band):
    return 2.0 / (1.0 + jnp.exp((band.astype(f32) - 0.5 * BANDS) / (0.125 * BANDS)))


def near_one_hot(near_ref):
    slot = iota((128, 128), 0) % CAP
    wanted = jnp.zeros((128, 128), jnp.int32)
    for s in range(CAP):
        wanted = jnp.where(slot == s, near_ref[s], wanted)
    lanes = iota((128, 128), 1)
    parts = [
        jnp.where(wanted == lanes + 128 * t, 1.0, 0.0).astype(bf16) for t in range(ATOMS // 128)
    ]
    return jnp.concatenate(parts, axis=1)


def halves(value):
    high = value.astype(bf16).astype(f32)
    return high, value - high


def pick_kernel(near_ref, count_ref, pos_ref, charge_ref, out_ref):
    one_hot = near_one_hot(near_ref)
    wide = jnp.concatenate([pos_ref[...], charge_ref[...]], axis=0)
    high, low = halves(wide)
    both = jnp.concatenate([high, low], axis=0).astype(bf16)
    picked = dot_nt(both, one_hot)
    lane = iota((8, 128), 1)
    row = jnp.sum(jnp.where(lane // CAP == iota((8, 128), 0), picked, 0.0), axis=0, keepdims=True)
    lane_row = iota((1, 128), 1)
    dead = (lane_row < CAP) & (lane_row >= count_ref[0])
    row = jnp.where(dead, DEAD_MARK, row)
    out_ref[...] = jnp.broadcast_to(row[None], out_ref.shape)


def section_kernel(coeffs_ref, table_ref, out_ref, wide_ref):
    table = table_ref[...]
    along_z = dot_nt(coeffs_ref[...].reshape(1024, GRID), table).astype(bf16)
    for a in range(8):
        wide_ref[:, a, :] = dot_nn(table, along_z[a * GRID : (a + 1) * GRID])
    out_ref[:, :64, :] = wide_ref[...].reshape(SHARES, 64, GRID).astype(bf16)
    out_ref[:, 64:, :] = jnp.zeros((SHARES, 16, GRID), bf16)


def stats_kernel(where_ref, coeffs_ref, out_ref):
    first = where_ref[0] * 8
    q_wave = iota((GRID, GRID), 0).astype(f32) * WAVE_STEP
    l_wave = iota((1, GRID), 1).astype(f32) * WAVE_STEP
    sums = [jnp.zeros((1, GRID), f32) for _ in range(7)]
    for a in range(8):
        a_wave = (first + a).astype(f32) * WAVE_STEP
        value = coeffs_ref[a].astype(f32)
        square = value * value
        scaled = square * q_wave
        flat = jnp.sum(square, axis=0, keepdims=True)
        once = jnp.sum(scaled, axis=0, keepdims=True)
        twice = jnp.sum(scaled * q_wave, axis=0, keepdims=True)
        terms = (
            flat,
            a_wave * a_wave * flat,
            twice,
            l_wave * l_wave * flat,
            a_wave * once,
            a_wave * l_wave * flat,
            l_wave * once,
        )
        sums = [total + term for total, term in zip(sums, terms)]
    lane = iota((1, GRID), 1)
    weight = occupancy(jnp.full((1, 1), where_ref[1], jnp.int32)) / CELLS
    row = jnp.where(lane == SCALAR_LANE, jnp.sum(sums[0]), 0.0)
    for i in range(1, 7):
        value = jnp.sum(sums[i], axis=1, keepdims=True) * weight
        row = jnp.where(lane == SCALAR_LANE + 2 + i, value, row)
    out_ref[...] = row


def gauss_values(offset):
    wide = jnp.exp(-EXPONENTS[3] * offset * offset)
    values = [wide]
    for _ in range(3):
        square = values[0] * values[0]
        values.insert(0, square * square)
    return values


def slot_place(blocks):
    lane = iota((OWNERS, 128), 1)
    live = jnp.where((blocks < 1000.0) & (lane < CAP), 1.0, 0.0).astype(bf16)
    return live


def place_by_row(live):
    ones = jnp.ones((128, 128), bf16)
    counts = dot_nn(live, ones)
    before = jnp.where(iota((OWNERS, OWNERS), 1) < iota((OWNERS, OWNERS), 0), 1.0, 0.0).astype(bf16)
    starts = dot_nn(before, counts.astype(bf16))
    return counts, starts


def place_by_lane(live):
    ones = jnp.ones((128, 128), bf16)
    counts = dot_nt(ones, live)
    before = jnp.where(iota((OWNERS, OWNERS), 0) < iota((OWNERS, OWNERS), 1), 1.0, 0.0).astype(bf16)
    starts = dot_nn(counts.astype(bf16), before)
    return counts, starts


def slot_masks(live):
    counts, starts = place_by_lane(live)
    place = iota((LIVE, OWNERS), 0).astype(f32)
    start_row = starts[:1]
    owner = (place >= start_row) & (place < start_row + counts[:1])
    owner = jnp.where(owner, 1.0, 0.0).astype(bf16)
    coarse = jnp.floor(starts * 0.125)
    fine = starts - 8.0 * coarse
    own_start = 8.0 * dot_nt(owner, coarse.astype(bf16)) + dot_nt(owner, fine.astype(bf16))
    slot = iota((LIVE, 128), 0).astype(f32) - own_start
    chosen = slot == (iota((LIVE, 128), 1) % CAP).astype(f32)
    return owner, chosen


def field_kernel(
    where_ref, got_ref, local_ref, table_ref, back_ref, density_ref, slots_ref, energy_ref,
    local_wide, back_wide, gx_ref, depth_ref,
):
    table = table_ref[...]
    got = got_ref[...].astype(f32)
    blocks = got[:, 64:, :].reshape(OWNERS, 128)
    owner, chosen = slot_masks(slot_place(blocks))
    rows = jnp.where(chosen, dot_nn(owner, blocks.astype(bf16)), 0.0).astype(bf16)
    pick = jnp.where(iota((8, 128), 1) // CAP == iota((8, 128), 0), 1.0, 0.0).astype(bf16)
    slots = dot_nt(pick, rows)
    slots = slots[:4] + slots[4:]
    slots_ref[...] = jnp.concatenate([slots, slots], axis=0)
    points = iota((GRID, LIVE), 0).astype(f32)
    y_points = (where_ref[0] * 8 + iota((8, LIVE), 0)).astype(f32)
    gx_values = gauss_values(points - slots[0:1])
    gy_values = gauss_values(y_points - slots[1:2])
    gz_values = gauss_values(points - slots[2:3])
    for k in range(4):
        gx_ref[k] = gx_values[k].astype(bf16)
        depth_ref[k] = gz_values[k] * (slots[3:4] * KERNEL_WEIGHTS[k])
    local_wide[...] = local_ref[...].astype(f32)
    weight = occupancy(jnp.full((1, 1), where_ref[1], jnp.int32))
    energy = jnp.zeros((1, GRID), f32)
    for y in range(8):
        potential = jnp.zeros((GRID, GRID), f32)
        for k in range(4):
            plane = (depth_ref[k] * gy_values[k][y : y + 1]).astype(bf16)
            potential = potential + dot_nt(gx_ref[k], plane)
        mine = got[:, y * 8 : (y + 1) * 8, :].reshape(GRID, GRID).astype(bf16)
        real = dot_nn(table, mine).astype(bf16).astype(f32)
        density = weight * real * real
        density_ref[y] = density
        energy = energy + jnp.sum(density * potential, axis=0, keepdims=True)
        field = local_wide[:, y, :] + potential.astype(bf16).astype(f32)
        applied = (field * real).astype(bf16)
        back = lax.dot_general(
            table, applied, (((0,), (0,)), ((), ())), preferred_element_type=f32
        )
        back_wide[:, y * 8 : (y + 1) * 8, :] = back.reshape(SHARES, 8, GRID)
    back_ref[...] = back_wide[...].astype(bf16)
    total = jnp.sum(energy, axis=1, keepdims=True) / CELLS
    energy_ref[...] = jnp.where(iota((1, GRID), 1) == SCALAR_LANE + 9, total, 0.0)


def force_kernel(
    where_ref, got_ref, density_ref, slots_ref, out_ref,
    turned_ref, x_ref, gz_ref, hz_ref, gy_ref, hy_ref, sum_ref,
):
    for y in range(8):
        turned_ref[y] = density_ref[y].T.astype(bf16)
    slots = slots_ref[...]
    points = iota((GRID, LIVE), 0).astype(f32)
    x_offset = points - slots[0:1]
    y_offset = (where_ref[0] * 8 + iota((8, LIVE), 0)).astype(f32) - slots[1:2]
    z_offset = points - slots[2:3]
    gx_values = gauss_values(x_offset)
    gy_values = gauss_values(y_offset)
    gz_values = gauss_values(z_offset)
    for k in range(4):
        slope = 2.0 * EXPONENTS[k]
        x_ref[k, 0] = gx_values[k].astype(bf16)
        x_ref[k, 1] = (slope * x_offset * gx_values[k]).astype(bf16)
        gy_ref[k] = gy_values[k]
        hy_ref[k] = slope * y_offset * gy_values[k]
        scale = KERNEL_WEIGHTS[k] * slots[3:4]
        gz_ref[k] = gz_values[k] * scale
        hz_ref[k] = slope * z_offset * gz_values[k] * scale

    @pl.loop(0, LIVE // 128)
    def _(chunk):
        lanes = pl.ds(pl.multiple_of(chunk * 128, 128), 128)
        force_x = jnp.zeros((1, 128), f32)
        force_y = jnp.zeros((1, 128), f32)
        force_z = jnp.zeros((1, 128), f32)
        for k in range(4):
            both = jnp.concatenate([x_ref[k, 0, :, lanes], x_ref[k, 1, :, lanes]], axis=1)
            value_y = gy_ref[k, :, lanes]
            slope_y = hy_ref[k, :, lanes]
            with_x = jnp.zeros((GRID, 128), f32)
            with_y = jnp.zeros((GRID, 128), f32)
            with_z = jnp.zeros((GRID, 128), f32)
            for y in range(8):
                part = dot_nn(turned_ref[y], both)
                with_x = with_x + part[:, 128:] * value_y[y : y + 1]
                with_y = with_y + part[:, :128] * slope_y[y : y + 1]
                with_z = with_z + part[:, :128] * value_y[y : y + 1]
            value_z = gz_ref[k, :, lanes]
            force_x = force_x + jnp.sum(with_x * value_z, axis=0, keepdims=True)
            force_y = force_y + jnp.sum(with_y * value_z, axis=0, keepdims=True)
            force_z = force_z + jnp.sum(with_z * hz_ref[k, :, lanes], axis=0, keepdims=True)
        sum_ref[0:1, lanes] = force_x
        sum_ref[1:2, lanes] = force_y
        sum_ref[2:3, lanes] = force_z

    forces = sum_ref[0:3, :] * -FORCE_UNIT
    high, low = halves(forces)
    stacked = jnp.concatenate([high, low, jnp.zeros((2, LIVE), f32)], axis=0)
    live = slot_place(got_ref[:, 64:, :].astype(f32).reshape(OWNERS, 128))
    owner, chosen = slot_masks(live)
    spread = jnp.where(iota((8, 128), 1) // CAP == iota((8, 128), 0), 1.0, 0.0).astype(bf16)
    per_slot = lax.dot_general(
        stacked.astype(bf16), spread, (((0,), (0,)), ((), ())), preferred_element_type=f32
    )
    per_slot = jnp.where(chosen, per_slot, 0.0).astype(bf16)
    counts, starts = place_by_row(live)
    place = iota((OWNERS, 128), 1).astype(f32)
    total = jnp.zeros((OWNERS, 128), f32)
    for t in range(LIVE // 128):
        here = place + (128.0 * t)
        held = jnp.where((here >= starts) & (here < starts + counts), 1.0, 0.0).astype(bf16)
        total = total + dot_nn(held, per_slot[t * 128 : (t + 1) * 128])
    out_ref[...] = total


def wave_tables(where_ref):
    q_wave = iota((GRID, GRID), 0).astype(f32) * WAVE_STEP
    l_wave = iota((GRID, GRID), 1).astype(f32) * WAVE_STEP
    return q_wave * q_wave + l_wave * l_wave


def kinetic_of(where_ref, plane_waves, a):
    a_wave = (where_ref[0] * 8 + a).astype(f32) * WAVE_STEP
    return 0.5 * (a_wave * a_wave + plane_waves)


def image_kernel(
    where_ref, got_ref, coeffs_ref, table_ref, force_ref, stats_ref, energy_ref,
    image_ref, out_ref, wide_ref,
):
    table = table_ref[...]
    wide_ref[...] = got_ref[...].astype(f32).reshape(GRID, 8, GRID)
    plane_waves = wave_tables(where_ref)
    overlap = jnp.zeros((1, GRID), f32)
    norm = jnp.zeros((1, GRID), f32)
    for a in range(8):
        along_y = lax.dot_general(
            table, wide_ref[:, a, :].astype(bf16), (((0,), (0,)), ((), ())),
            preferred_element_type=f32,
        ).astype(bf16)
        coeff = coeffs_ref[a].astype(f32)
        image = kinetic_of(where_ref, plane_waves, a) * coeff + dot_nn(along_y, table)
        image_ref[a] = image
        overlap = overlap + jnp.sum(coeff * image, axis=0, keepdims=True)
        norm = norm + jnp.sum(coeff * coeff, axis=0, keepdims=True)
    overlap = jnp.sum(overlap, axis=1, keepdims=True)
    norm = jnp.sum(norm, axis=1, keepdims=True)
    mean = overlap / jnp.maximum(norm, 1e-30)
    spread = jnp.zeros((1, GRID), f32)
    for a in range(8):
        residual = image_ref[a] - mean * coeffs_ref[a].astype(f32)
        spread = spread + jnp.sum(residual * residual, axis=0, keepdims=True)
    spread = jnp.sum(spread, axis=1, keepdims=True)
    lane = iota((1, GRID), 1)
    row = stats_ref[...] + energy_ref[...]
    row = jnp.where(lane == SCALAR_LANE + 1, overlap, row)
    row = jnp.where(lane == SCALAR_LANE + 2, spread, row)
    out_ref[...] = force_ref[...] + row


def final_kernel(
    where_ref, near_ref, count_ref, got_ref, image_ref, coeffs_ref,
    waves_ref, force_ref, energy_ref, ratio_ref, totals_ref,
):
    got = got_ref[...]
    by_band = jnp.sum(got.reshape(SHARES, BANDS, 128), axis=0)
    column = lambda i: slice(SCALAR_LANE + i, SCALAR_LANE + i + 1)
    norms = by_band[:, column(0)]
    energies = by_band[:, column(1)] / norms
    band = iota((BANDS, 1), 0)
    own = band == where_ref[1]
    energy = jnp.sum(jnp.where(own, energies, 0.0), axis=0, keepdims=True)
    norm = jnp.sum(jnp.where(own, norms, 0.0), axis=0, keepdims=True)
    part_norm = got[:, column(0)]
    part_energy = got[:, column(1)] / jnp.maximum(part_norm, 1e-30)
    shift = part_energy - energy
    spread = got[:, column(2)] + part_norm * shift * shift
    own_rows = iota((OWNERS, 1), 0) % BANDS == where_ref[1]
    squares = jnp.sum(jnp.where(own_rows, spread, 0.0), axis=0, keepdims=True)
    energy_ref[...] = energy
    ratio_ref[...] = squares / norm
    everything = jnp.sum(by_band, axis=0, keepdims=True)
    band_energy = jnp.sum(occupancy(band) * energies, axis=0, keepdims=True) / BANDS
    totals_ref[...] = jnp.concatenate(
        [everything[:, SCALAR_LANE + 3 : SCALAR_LANE + 10], band_energy], axis=1
    )
    plane_waves = wave_tables(where_ref)
    for a in range(8):
        coeff = coeffs_ref[a].astype(f32)
        residual = image_ref[a] - energy * coeff
        kinetic = kinetic_of(where_ref, plane_waves, a)
        waves_ref[a] = (coeff - STEP_SIZE * residual / (1.0 + kinetic)).astype(bf16)
    lane = iota((8, 128), 1)
    wanted = (lane // CAP) % 3 == iota((8, 128), 0)
    wanted = wanted & (lane < SCALAR_LANE) & (lane % CAP < count_ref[0])
    split = jnp.where(wanted, everything, 0.0)
    high, rest = halves(split)
    middle, low = halves(rest)
    pieces = jnp.concatenate([high, middle, low, jnp.zeros_like(low)], axis=0).astype(bf16)
    placed = dot_nn(pieces, near_one_hot(near_ref))
    forces = placed[0:8] + placed[8:16] + placed[16:24]
    force_ref[...] = forces[:3]


VMEM = pl.BlockSpec(memory_space=pltpu.VMEM)
SMEM = pl.BlockSpec(memory_space=pltpu.SMEM)


def call(kernel, inputs, outputs, scratch=(), cost=2000000000):
    specs = [SMEM if x.dtype == jnp.int32 else VMEM for x in inputs]
    shapes = [jax.ShapeDtypeStruct(*out) for out in outputs]
    return pl.pallas_call(
        kernel,
        out_shape=shapes,
        in_specs=specs,
        out_specs=[VMEM] * len(shapes),
        scratch_shapes=[pltpu.VMEM(*one) for one in scratch],
        compiler_params=pltpu.CompilerParams(vmem_limit_bytes=40 * 1024 * 1024),
        cost_estimate=pl.CostEstimate(flops=cost, bytes_accessed=1000000, transcendentals=0),
    )(*inputs)


def exchange(block, axes):
    return lax.all_to_all(block, axes, split_axis=0, concat_axis=0, tiled=True)


def per_device(coeffs, v_local, atom_pos, atom_charge, near_list, live_count):
    table = cosine_table()
    coeffs = coeffs[0]
    where = jnp.stack([lax.axis_index("gvec"), lax.axis_index(GROUP)]).astype(jnp.int32)
    (own,) = call(
        pick_kernel,
        [near_list, live_count, atom_pos, atom_charge.reshape(1, ATOMS)],
        [((SHARES, 1, 128), f32)],
    )
    group = exchange(own, GROUP)
    (sections,) = call(
        section_kernel,
        [coeffs, table],
        [((SHARES, 80, GRID), bf16)],
        [((GRID, 8, GRID), f32)],
    )
    blocks = jnp.broadcast_to(group.reshape(1, SHARES, 128), (SHARES, SHARES, 128)).astype(bf16)
    sections = lax.dynamic_update_slice(sections, blocks, (0, 64, 0))
    got = exchange(sections, "gvec")
    (stats,) = call(stats_kernel, [where, coeffs], [((1, 128), f32)])
    back, density, slots, energy = call(
        field_kernel,
        [where, got, v_local, table],
        [
            ((SHARES, 64, GRID), bf16),
            ((8, GRID, GRID), f32),
            ((8, LIVE), f32),
            ((1, 128), f32),
        ],
        [
            ((GRID, 8, GRID), f32),
            ((SHARES, 64, GRID), f32),
            ((4, GRID, LIVE), bf16),
            ((4, GRID, LIVE), f32),
        ],
    )
    returned = exchange(back, "gvec")
    (forces,) = call(
        force_kernel,
        [where, got, density, slots],
        [((OWNERS, 128), f32)],
        [
            ((8, GRID, GRID), bf16),
            ((4, 2, GRID, LIVE), bf16),
            ((4, GRID, LIVE), f32),
            ((4, GRID, LIVE), f32),
            ((4, 8, LIVE), f32),
            ((4, 8, LIVE), f32),
            ((8, LIVE), f32),
        ],
    )
    image, message = call(
        image_kernel,
        [where, returned, coeffs, table, forces, stats, energy],
        [((8, GRID, GRID), f32), ((OWNERS, 128), f32)],
        [((GRID, 8, GRID), f32)],
    )
    arrived = exchange(message.reshape(OWNERS, 1, 128), EVERY).reshape(OWNERS, 128)
    waves, atom_force, energies, ratio, totals = call(
        final_kernel,
        [where, near_list, live_count, arrived, image, coeffs],
        [
            ((8, GRID, GRID), bf16),
            ((3, ATOMS), f32),
            ((1, 1), f32),
            ((1, 1), f32),
            ((1, 8), f32),
        ],
    )
    return (waves[None], energies.reshape(1), ratio.reshape(1), atom_force, totals.reshape(8))


def solution(mesh):
    return jax.shard_map(
        per_device,
        mesh=mesh,
        in_specs=(
            P(("band", "dom"), "gvec", None, None),
            P(None, "gvec", None),
            P(None, ("band", "gvec", "dom")),
            P(("band", "gvec", "dom")),
            P(("band", "gvec", "dom")),
            P(("band", "gvec", "dom")),
        ),
        out_specs=(
            P(("band", "dom"), "gvec", None, None),
            P(("band", "dom")),
            P(("band", "dom")),
            P(None, ("band", "gvec", "dom")),
            P(),
        ),
        check_vma=False,
    )
```

time: 1580 us -> 90.1 us (0.06)
  waiting for transfers between devices: 1270 us -> 19 us
  blocking collectives: 224 us -> 20.4 us
  Pallas kernels: 0 us -> 23.7 us
  other arithmetic: 24 us -> 0.68 us
  between operations: 19.5 us -> 1.36 us
    unnamed x4 -> x0, waiting for transfers between devices: 1260 us -> none
    all_gather x2 -> x0, blocking collectives: 121 us -> none  [the longest x1 103 us: per_device(): lax.all_gather(own_block, ('band', 'gvec', 'dom'), axis=1, tiled=True)]
    psum x2 -> x0, blocking collectives: 104 us -> none  [the longest x1 79.4 us: per_device(): lax.psum((norm_vec, intersection_vec, local_totals), ('band', 'gvec', 'do...]
    pallas_call x0 -> x7, Pallas kernels: none -> 23.7 us  [call(): pl.pallas_call(kernel, out_shape=shapes, in_specs=specs, out_specs=[VMEM]...]
    all_to_all x0 -> x1, blocking collectives: none -> 20.4 us  [exchange(): return lax.all_to_all(block, axes, split_axis=0, concat_axis=0, tiled=True)]
  transfers between devices with their start and end apart: 4 -> 3, of which waited for: 2 -> 3; matrix products, arithmetic and copies ran while one was open for 1% -> 0% of each run, Pallas kernels for 0% -> 13%
where the time goes in v2:
time: 90.1 us; the launch traced here: 89.6 us
  Pallas kernels  23.7 us (26%)
  starting transfers between devices  21.7 us (24%)
  blocking collectives  20.4 us (23%)
  waiting for transfers between devices  19 us (21%)
  local copies, waits for them, and re-layouts  2.72 us (3%)
  between operations  1.36 us (2%)
    pallas_call x7, Pallas kernels, call(): pl.pallas_call(kernel, out_shape=shapes, in_specs=specs, out_specs=[VMEM]...  23.7 us
    all_to_all x3, starting transfers between devices, exchange(): return lax.all_to_all(block, axes, split_axis=0, concat_axis=0, tiled=True)  21.7 us
    all_to_all x1, blocking collectives, exchange(): return lax.all_to_all(block, axes, split_axis=0, concat_axis=0, tiled=True)  20.4 us
    all_to_all x3, waiting for transfers between devices, exchange(): return lax.all_to_all(block, axes, split_axis=0, concat_axis=0, tiled=True)  19 us
    unnamed x13, local copies, waits for them, and re-layouts  2.07 us
  transfers between devices with their start and end apart: 3, of which 3 were waited for; matrix products, arithmetic and copies ran while one was open for 0% of the time, Pallas kernels for 13%

profile of v2, /device:TPU:1, one launch (start us, length us, event | category | flops | bytes accessed | tf_op | source)
XLA Modules:
  0.0 89.6 jit_solution(11558627081211274511)
XLA Ops:
  1.3 0.0 copy-start.4
  1.3 0.6 copy-done.4
  1.9 0.0 copy-start.2
  1.9 0.7 copy-done.2
  2.7 0.0 copy-start.3
  2.7 0.7 copy-done.3
  3.3 0.0 copy-start.1
  3.3 0.8 shard_map.111
  4.1 0.0 copy-start.5
  4.1 0.6 convert
  4.7 7.6 %all-to-all-start = ((bf16[16,1,128]{2,1,0:T(2,128)(2,1)}), bf16[16,1,128]{2,1,0:T(2,128)(2,1)S(1)}, u32[]{:S(2)}, u32[]{:S(2)}) async-start(bf16[16,1,128]{2,1,0:T(2,128)(2,1)} %convert), calls=%async_computation | async-start | bytes 16384 | tf_op jit(solution)/shard_map/all_to_all | solution.py:397
  12.3 0.0 copy-done.1
  12.3 0.0 copy-done.5
  12.3 1.3 %shard_map.110 = bf16[16,80,128]{2,1,0:T(8,128)(2,1)} custom-call(bf16[8,128,128]{2,1,0:T(8,128)(2,1)S(1)} %bitcast.17, bf16[128,128]{1,0:T(8,128)(2,1)S(1)} %copy-done.5), custom_call_target="tpu_custom_call" | custom-call | flops 2000000000 | bytes 1000000 | tf_op jit(solution)/shard_map/pallas_call | solution.py:385
  13.7 5.0 %all-to-all-done = bf16[16,1,128]{2,1,0:T(2,128)(2,1)S(1)} async-done(((bf16[16,1,128]{2,1,0:T(2,128)(2,1)}), bf16[16,1,128]{2,1,0:T(2,128)(2,1)S(1)}, u32[]{:S(2)}, u32[]{:S(2)}) %all-to-all-start) | async-done | bytes 4128 | tf_op jit(solution)/shard_map/all_to_all | solution.py:397
  18.7 0.6 broadcast_dynamic-update-slice_fusion
  19.3 0.0 copy-start
  19.3 10.7 %all-to-all-start.1 = ((bf16[16,80,128]{2,1,0:T(8,128)(2,1)}), bf16[16,80,128]{2,1,0:T(8,128)(2,1)S(1)}, u32[]{:S(2)}, u32[]{:S(2)}) async-start(bf16[16,80,128]{2,1,0:T(8,128)(2,1)} %broadcast_dynamic-update-slice_fusion), calls=%async_computation.1 | async-start | bytes 655360 | tf_op jit(solution)/shard_map/all_to_all | solution.py:397
  30.0 0.1 pad_add_fusion.where_ref
  30.1 13.0 %all-to-all-done.1.got_ref = bf16[16,80,128]{2,1,0:T(8,128)(2,1)S(1)} async-done(((bf16[16,80,128]{2,1,0:T(8,128)(2,1)}), bf16[16,80,128]{2,1,0:T(8,128)(2,1)S(1)}, u32[]{:S(2)}, u32[]{:S(2)}) %all-to-all-start.1) | async-done | bytes 327712 | tf_op jit(solution)/shard_map/all_to_all | solution.py:397
  43.1 0.0 copy-done
  43.1 8.1 %shard_map.112 = (bf16[16,64,128]{2,1,0:T(8,128)(2,1)}, f32[8,128,128]{2,1,0:T(8,128)S(1)}, f32[8,1024]{1,0:T(8,128)S(1)}, f32[1,128]{1,0:T(1,128)S(1)}) custom-call(s32[2]{0:T(128)S(1)} %pad_add_fusion.where_ref, bf16[16,80,128]{2,1,0:T(8,128)(2,1)S(1)} %all-to-all-done.1.got_ref, bf16[128,8,128]{2,1,0:T(8,128)(2,1)S(1)} %copy-done, ...), custom_call_target="tpu_custom_call" | custom-call | flops 2000000000 | bytes 1000000 | tf_op jit(solution)/shard_map/pallas_call | solution.py:385
  51.2 3.4 %all-to-all-start.2 = ((bf16[16,64,128]{2,1,0:T(8,128)(2,1)}), bf16[16,64,128]{2,1,0:T(8,128)(2,1)S(1)}, u32[]{:S(2)}, u32[]{:S(2)}) async-start(bf16[16,64,128]{2,1,0:T(8,128)(2,1)} %get-tuple-element.16), calls=%async_computation.2 | async-start | bytes 524288 | tf_op jit(solution)/shard_map/all_to_all | solution.py:397
  54.6 0.8 shard_map.114.stats_ref
  55.5 9.3 %shard_map.113.force_ref = f32[256,128]{1,0:T(8,128)S(1)} custom-call(s32[2]{0:T(128)S(1)} %pad_add_fusion.where_ref, bf16[16,80,128]{2,1,0:T(8,128)(2,1)S(1)} %all-to-all-done.1.got_ref, f32[8,128,128]{2,1,0:T(8,128)S(1)} %get-tuple-element.17.density_ref, f32[8,1024]{1,0:T(8,128)S(1)} %get-tuple-element.18.slots_ref), custom_call_target="tpu_custom_call" | custom-call | flops 2000000000 | bytes 1000000 | tf_op jit(solution)/shard_map/pallas_call | solution.py:385
  64.8 1.0 %all-to-all-done.2.got_ref = bf16[16,64,128]{2,1,0:T(8,128)(2,1)S(1)} async-done(((bf16[16,64,128]{2,1,0:T(8,128)(2,1)}), bf16[16,64,128]{2,1,0:T(8,128)(2,1)S(1)}, u32[]{:S(2)}, u32[]{:S(2)}) %all-to-all-start.2) | async-done | bytes 262176 | tf_op jit(solution)/shard_map/all_to_all | solution.py:397
  65.8 1.7 %shard_map.115 = (f32[8,128,128]{2,1,0:T(8,128)S(1)}, f32[256,128]{1,0:T(8,128)S(1)}) custom-call(s32[2]{0:T(128)S(1)} %pad_add_fusion.where_ref, bf16[16,64,128]{2,1,0:T(8,128)(2,1)S(1)} %all-to-all-done.2.got_ref, bf16[8,128,128]{2,1,0:T(8,128)(2,1)S(1)} %bitcast.19, bf16[128,128]{1,0:T(8,128)(2,1)S(1)} %copy-done.5, f32[256,128]{1,0:T(8,128)S(1)} %shard_map.113.force_ref, ...), custom_call_target="tpu_custom_call" | custom-call | flops 2000000000 | bytes 1000000 | tf_op jit(solution)/shard_map/pallas_call | solution.py:385
  67.5 20.4 %all_to_all.20 = f32[256,1,128]{2,1,0:T(1,128)S(1)} all-to-all(f32[256,1,128]{2,1,0:T(1,128)S(1)} %bitcast.16), channel_id=1, replica_groups=mesh['band'=4,'gvec'=16,'dom'=4] {'gvec','band','dom'}, dimensions={0} | all-to-all | bytes 262144 | tf_op jit(solution)/shard_map/all_to_all | solution.py:397
  87.9 1.7 %shard_map.116 = (bf16[8,128,128]{2,1,0:T(8,128)(2,1)}, f32[3,1024]{1,0:T(4,128)}, f32[1,1]{1,0:T(1,128)}, f32[1,1]{1,0:T(1,128)}, f32[1,8]{1,0:T(1,128)}) custom-call(s32[2]{0:T(128)S(1)} %pad_add_fusion.where_ref, s32[16]{0:T(128)S(1)} %copy-done.4, s32[1]{0:T(128)S(6)} %copy.17.count_ref, f32[256,128]{1,0:T(8,128)S(1)} %bitcast.15, ...), custom_call_target="tpu_custom_call" | custom-call | flops 2000000000 | bytes 1000000 | tf_op jit(solution)/shard_map/pallas_call | solution.py:385
  (1 shorter events, 0.0 us)
Async XLA Ops:
  1.3 0.7 copy-start.4
  1.9 0.7 copy-start.2
  2.7 0.7 copy-start.3
  3.3 9.0 %copy-start.1 = (bf16[1,8,128,128]{3,2,1,0:T(8,128)(2,1)S(1)}, bf16[1,8,128,128]{3,2,1,0:T(8,128)(2,1)}, u32[]{:S(2)}) copy-start(bf16[1,8,128,128]{3,2,1,0:T(8,128)(2,1)} %param.7) | copy-start | bytes 786436
  4.1 8.2 %copy-start.5 = (bf16[128,128]{1,0:T(8,128)(2,1)S(1)}, bf16[128,128]{1,0:T(8,128)(2,1)}, u32[]{:S(2)}) copy-start(bf16[128,128]{1,0:T(8,128)(2,1)} %constant.21.clone.table_ref) | copy-start | bytes 98308
  4.7 13.9 %all-to-all-start = ((bf16[16,1,128]{2,1,0:T(2,128)(2,1)}), bf16[16,1,128]{2,1,0:T(2,128)(2,1)S(1)}, u32[]{:S(2)}, u32[]{:S(2)}) async-start(bf16[16,1,128]{2,1,0:T(2,128)(2,1)} %convert), calls=%async_computation | async-start | bytes 16384 | tf_op jit(solution)/shard_map/all_to_all | solution.py:397
  19.3 23.8 %copy-start = (bf16[128,8,128]{2,1,0:T(8,128)(2,1)S(1)}, bf16[128,8,128]{2,1,0:T(8,128)(2,1)}, u32[]{:S(2)}) copy-start(bf16[128,8,128]{2,1,0:T(8,128)(2,1)} %local_ref.1) | copy-start | bytes 786436
  19.3 23.8 %all-to-all-start.1 = ((bf16[16,80,128]{2,1,0:T(8,128)(2,1)}), bf16[16,80,128]{2,1,0:T(8,128)(2,1)S(1)}, u32[]{:S(2)}, u32[]{:S(2)}) async-start(bf16[16,80,128]{2,1,0:T(8,128)(2,1)} %broadcast_dynamic-update-slice_fusion), calls=%async_computation.1 | async-start | bytes 655360 | tf_op jit(solution)/shard_map/all_to_all | solution.py:397
  51.2 14.6 %all-to-all-start.2 = ((bf16[16,64,128]{2,1,0:T(8,128)(2,1)}), bf16[16,64,128]{2,1,0:T(8,128)(2,1)S(1)}, u32[]{:S(2)}, u32[]{:S(2)}) async-start(bf16[16,64,128]{2,1,0:T(8,128)(2,1)} %get-tuple-element.16), calls=%async_computation.2 | async-start | bytes 524288 | tf_op jit(solution)/shard_map/all_to_all | solution.py:397

commit v3 on v2

--- a/solution.py
+++ b/solution.py
@@ -71,7 +71,20 @@
     return high, value - high
 
 
-def pick_kernel(near_ref, count_ref, pos_ref, charge_ref, out_ref):
+def pick_kernel(
+    near_hbm, count_hbm, pos_hbm, charge_hbm, out_ref,
+    near_ref, count_ref, pos_ref, charge_ref, sems,
+):
+    moves = [
+        pltpu.make_async_copy(near_hbm, near_ref, sems.at[0]),
+        pltpu.make_async_copy(count_hbm, count_ref, sems.at[1]),
+        pltpu.make_async_copy(pos_hbm, pos_ref, sems.at[2]),
+        pltpu.make_async_copy(charge_hbm, charge_ref, sems.at[3]),
+    ]
+    for move in moves:
+        move.start()
+    for move in moves:
+        move.wait()
     one_hot = near_one_hot(near_ref)
     wide = jnp.concatenate([pos_ref[...], charge_ref[...]], axis=0)
     high, low = halves(wide)
@@ -82,7 +95,7 @@
     lane_row = iota((1, 128), 1)
     dead = (lane_row < CAP) & (lane_row >= count_ref[0])
     row = jnp.where(dead, DEAD_MARK, row)
-    out_ref[...] = jnp.broadcast_to(row[None], out_ref.shape)
+    out_ref[...] = jnp.broadcast_to(row, out_ref.shape)
 
 
 def section_kernel(coeffs_ref, table_ref, out_ref, wide_ref):
@@ -90,8 +103,7 @@
     along_z = dot_nt(coeffs_ref[...].reshape(1024, GRID), table).astype(bf16)
     for a in range(8):
         wide_ref[:, a, :] = dot_nn(table, along_z[a * GRID : (a + 1) * GRID])
-    out_ref[:, :64, :] = wide_ref[...].reshape(SHARES, 64, GRID).astype(bf16)
-    out_ref[:, 64:, :] = jnp.zeros((SHARES, 16, GRID), bf16)
+    out_ref[...] = wide_ref[...].reshape(SHARES, 64, GRID).astype(bf16)
 
 
 def stats_kernel(where_ref, coeffs_ref, out_ref):
@@ -171,13 +183,8 @@
     return owner, chosen
 
 
-def field_kernel(
-    where_ref, got_ref, local_ref, table_ref, back_ref, density_ref, slots_ref, energy_ref,
-    local_wide, back_wide, gx_ref, depth_ref,
-):
-    table = table_ref[...]
-    got = got_ref[...].astype(f32)
-    blocks = got[:, 64:, :].reshape(OWNERS, 128)
+def potential_kernel(where_ref, blocks_ref, potential_ref, slots_ref, gx_ref, depth_ref):
+    blocks = blocks_ref[...]
     owner, chosen = slot_masks(slot_place(blocks))
     rows = jnp.where(chosen, dot_nn(owner, blocks.astype(bf16)), 0.0).astype(bf16)
     pick = jnp.where(iota((8, 128), 1) // CAP == iota((8, 128), 0), 1.0, 0.0).astype(bf16)
@@ -192,14 +199,25 @@
     for k in range(4):
         gx_ref[k] = gx_values[k].astype(bf16)
         depth_ref[k] = gz_values[k] * (slots[3:4] * KERNEL_WEIGHTS[k])
-    local_wide[...] = local_ref[...].astype(f32)
-    weight = occupancy(jnp.full((1, 1), where_ref[1], jnp.int32))
-    energy = jnp.zeros((1, GRID), f32)
     for y in range(8):
         potential = jnp.zeros((GRID, GRID), f32)
         for k in range(4):
             plane = (depth_ref[k] * gy_values[k][y : y + 1]).astype(bf16)
             potential = potential + dot_nt(gx_ref[k], plane)
+        potential_ref[y] = potential
+
+
+def field_kernel(
+    where_ref, got_ref, local_ref, table_ref, potential_ref, stats_ref,
+    back_ref, density_ref, energy_ref, local_wide, back_wide,
+):
+    table = table_ref[...]
+    got = got_ref[...].astype(f32)
+    local_wide[...] = local_ref[...].astype(f32)
+    weight = occupancy(jnp.full((1, 1), where_ref[1], jnp.int32))
+    energy = jnp.zeros((1, GRID), f32)
+    for y in range(8):
+        potential = potential_ref[y]
         mine = got[:, y * 8 : (y + 1) * 8, :].reshape(GRID, GRID).astype(bf16)
         real = dot_nn(table, mine).astype(bf16).astype(f32)
         density = weight * real * real
@@ -213,11 +231,12 @@
         back_wide[:, y * 8 : (y + 1) * 8, :] = back.reshape(SHARES, 8, GRID)
     back_ref[...] = back_wide[...].astype(bf16)
     total = jnp.sum(energy, axis=1, keepdims=True) / CELLS
-    energy_ref[...] = jnp.where(iota((1, GRID), 1) == SCALAR_LANE + 9, total, 0.0)
+    lane = iota((1, GRID), 1)
+    energy_ref[...] = stats_ref[...] + jnp.where(lane == SCALAR_LANE + 9, total, 0.0)
 
 
 def force_kernel(
-    where_ref, got_ref, density_ref, slots_ref, out_ref,
+    where_ref, blocks_ref, density_ref, slots_ref, out_ref,
     turned_ref, x_ref, gz_ref, hz_ref, gy_ref, hy_ref, sum_ref,
 ):
     for y in range(8):
@@ -269,7 +288,7 @@
     forces = sum_ref[0:3, :] * -FORCE_UNIT
     high, low = halves(forces)
     stacked = jnp.concatenate([high, low, jnp.zeros((2, LIVE), f32)], axis=0)
-    live = slot_place(got_ref[:, 64:, :].astype(f32).reshape(OWNERS, 128))
+    live = slot_place(blocks_ref[...])
     owner, chosen = slot_masks(live)
     spread = jnp.where(iota((8, 128), 1) // CAP == iota((8, 128), 0), 1.0, 0.0).astype(bf16)
     per_slot = lax.dot_general(
@@ -298,7 +317,7 @@
 
 
 def image_kernel(
-    where_ref, got_ref, coeffs_ref, table_ref, force_ref, stats_ref, energy_ref,
+    where_ref, got_ref, coeffs_ref, table_ref, force_ref, energy_ref,
     image_ref, out_ref, wide_ref,
 ):
     table = table_ref[...]
@@ -325,8 +344,7 @@
         spread = spread + jnp.sum(residual * residual, axis=0, keepdims=True)
     spread = jnp.sum(spread, axis=1, keepdims=True)
     lane = iota((1, GRID), 1)
-    row = stats_ref[...] + energy_ref[...]
-    row = jnp.where(lane == SCALAR_LANE + 1, overlap, row)
+    row = jnp.where(lane == SCALAR_LANE + 1, overlap, energy_ref[...])
     row = jnp.where(lane == SCALAR_LANE + 2, spread, row)
     out_ref[...] = force_ref[...] + row
 
@@ -379,15 +397,16 @@
 SMEM = pl.BlockSpec(memory_space=pltpu.SMEM)
 
 
-def call(kernel, inputs, outputs, scratch=(), cost=2000000000):
-    specs = [SMEM if x.dtype == jnp.int32 else VMEM for x in inputs]
+def call(kernel, inputs, outputs, scratch=(), cost=2000000000, specs=None):
+    if specs is None:
+        specs = [SMEM if x.dtype == jnp.int32 else VMEM for x in inputs]
     shapes = [jax.ShapeDtypeStruct(*out) for out in outputs]
     return pl.pallas_call(
         kernel,
         out_shape=shapes,
         in_specs=specs,
         out_specs=[VMEM] * len(shapes),
-        scratch_shapes=[pltpu.VMEM(*one) for one in scratch],
+        scratch_shapes=[pltpu.VMEM(*one) if isinstance(one, tuple) else one for one in scratch],
         compiler_params=pltpu.CompilerParams(vmem_limit_bytes=40 * 1024 * 1024),
         cost_estimate=pl.CostEstimate(flops=cost, bytes_accessed=1000000, transcendentals=0),
     )(*inputs)
@@ -404,39 +423,45 @@
     (own,) = call(
         pick_kernel,
         [near_list, live_count, atom_pos, atom_charge.reshape(1, ATOMS)],
-        [((SHARES, 1, 128), f32)],
-    )
-    group = exchange(own, GROUP)
+        [((OWNERS, 128), f32)],
+        [
+            pltpu.SMEM((CAP,), jnp.int32),
+            pltpu.SMEM((1,), jnp.int32),
+            ((3, ATOMS), f32),
+            ((1, ATOMS), f32),
+            pltpu.SemaphoreType.DMA((4,)),
+        ],
+        specs=[pl.BlockSpec(memory_space=pltpu.HBM)] * 4,
+    )
+    blocks = exchange(own.reshape(OWNERS, 1, 128), EVERY).reshape(OWNERS, 128)
     (sections,) = call(
         section_kernel,
         [coeffs, table],
-        [((SHARES, 80, GRID), bf16)],
+        [((SHARES, 64, GRID), bf16)],
         [((GRID, 8, GRID), f32)],
     )
-    blocks = jnp.broadcast_to(group.reshape(1, SHARES, 128), (SHARES, SHARES, 128)).astype(bf16)
-    sections = lax.dynamic_update_slice(sections, blocks, (0, 64, 0))
     got = exchange(sections, "gvec")
     (stats,) = call(stats_kernel, [where, coeffs], [((1, 128), f32)])
-    back, density, slots, energy = call(
+    potential, slots = call(
+        potential_kernel,
+        [where, blocks],
+        [((8, GRID, GRID), f32), ((8, LIVE), f32)],
+        [((4, GRID, LIVE), bf16), ((4, GRID, LIVE), f32)],
+    )
+    back, density, energy = call(
         field_kernel,
-        [where, got, v_local, table],
+        [where, got, v_local, table, potential, stats],
         [
             ((SHARES, 64, GRID), bf16),
             ((8, GRID, GRID), f32),
-            ((8, LIVE), f32),
             ((1, 128), f32),
         ],
-        [
-            ((GRID, 8, GRID), f32),
-            ((SHARES, 64, GRID), f32),
-            ((4, GRID, LIVE), bf16),
-            ((4, GRID, LIVE), f32),
-        ],
+        [((GRID, 8, GRID), f32), ((SHARES, 64, GRID), f32)],
     )
     returned = exchange(back, "gvec")
     (forces,) = call(
         force_kernel,
-        [where, got, density, slots],
+        [where, blocks, density, slots],
         [((OWNERS, 128), f32)],
         [
             ((8, GRID, GRID), bf16),
@@ -450,7 +475,7 @@
     )
     image, message = call(
         image_kernel,
-        [where, returned, coeffs, table, forces, stats, energy],
+        [where, returned, coeffs, table, forces, energy],
         [((8, GRID, GRID), f32), ((OWNERS, 128), f32)],
         [((GRID, 8, GRID), f32)],
     )

time: 90.1 us -> 89.2 us (0.990)
  Pallas kernels: 23.7 us -> 22.3 us
  waiting for transfers between devices: 19 us -> 20.3 us
  starting transfers between devices: 21.7 us -> 22.9 us
    pallas_call x7 -> x8, Pallas kernels: 23.7 us -> 22.3 us  [call(): pl.pallas_call(kernel, out_shape=shapes, in_specs=specs, out_specs=[VMEM]...]
    all_to_all x3, waiting for transfers between devices: 19 us -> 20.3 us  [exchange(): return lax.all_to_all(block, axes, split_axis=0, concat_axis=0, tiled=True)]
    all_to_all x3, starting transfers between devices: 21.7 us -> 22.9 us  [exchange(): return lax.all_to_all(block, axes, split_axis=0, concat_axis=0, tiled=True)]
    unnamed x13 -> x12, local copies, waits for them, and re-layouts: 2.07 us -> 2.07 us
  transfers between devices with their start and end apart: 3 -> 3, of which waited for: 3 -> 3; matrix products, arithmetic and copies ran while one was open for 0% -> 0% of each run, Pallas kernels for 13% -> 17%
where the time goes in v3:
time: 89.2 us; the launch traced here: 88.6 us
  starting transfers between devices  22.9 us (26%)
  Pallas kernels  22.3 us (25%)
  waiting for transfers between devices  20.3 us (23%)
  blocking collectives  19.6 us (22%)
  local copies, waits for them, and re-layouts  2.07 us (2%)
  between operations  1.37 us (2%)
    all_to_all x3, starting transfers between devices, exchange(): return lax.all_to_all(block, axes, split_axis=0, concat_axis=0, tiled=True)  22.9 us
    pallas_call x8, Pallas kernels, call(): pl.pallas_call(kernel, out_shape=shapes, in_specs=specs, out_specs=[VMEM]...  22.3 us
    all_to_all x3, waiting for transfers between devices, exchange(): return lax.all_to_all(block, axes, split_axis=0, concat_axis=0, tiled=True)  20.3 us
    all_to_all x1, blocking collectives, exchange(): return lax.all_to_all(block, axes, split_axis=0, concat_axis=0, tiled=True)  19.6 us
    unnamed x12, local copies, waits for them, and re-layouts  2.07 us
  transfers between devices with their start and end apart: 3, of which 3 were waited for; matrix products, arithmetic and copies ran while one was open for 0% of the time, Pallas kernels for 17%

profile of v3, /device:TPU:1, one launch (start us, length us, event | category | flops | bytes accessed | tf_op | source)
XLA Modules:
  0.0 88.6 jit_solution(7142161346051255954)
XLA Ops:
  1.3 0.0 copy-start.4
  1.3 0.6 copy-done.4
  1.9 0.0 copy-start.2
  1.9 0.7 copy-done.2
  2.7 0.0 copy-start.3
  2.7 0.7 copy-done.3
  3.3 0.0 copy-start.5
  3.3 1.5 %shard_map.111 = f32[256,128]{1,0:T(8,128)} custom-call(s32[16]{0:T(128)S(1)} %copy-done.4, s32[1]{0:T(128)S(6)} %copy.14.count_hbm.count_ref, f32[3,1024]{1,0:T(4,128)S(1)} %copy-done.2, f32[1,1024]{1,0:T(1,128)S(1)} %bitcast.24), custom_call_target="tpu_custom_call" | custom-call | flops 2000000000 | bytes 1000000 | tf_op jit(solution)/shard_map/pallas_call | solution.py:404
  4.8 0.0 copy-start.1
  4.8 15.7 %all-to-all-start.1 = ((f32[256,1,128]{2,1,0:T(1,128)}), f32[256,1,128]{2,1,0:T(1,128)S(1)}, u32[]{:S(2)}, u32[]{:S(2)}) async-start(f32[256,1,128]{2,1,0:T(1,128)} %bitcast.5), calls=%async_computation.1 | async-start | bytes 262144 | tf_op jit(solution)/shard_map/all_to_all | solution.py:416
  20.5 0.0 copy-done.5
  20.5 0.0 copy-done.1
  20.5 1.3 %shard_map.110 = bf16[16,64,128]{2,1,0:T(8,128)(2,1)} custom-call(bf16[8,128,128]{2,1,0:T(8,128)(2,1)S(1)} %bitcast.20, bf16[128,128]{1,0:T(8,128)(2,1)S(1)} %copy-done.5), custom_call_target="tpu_custom_call" | custom-call | flops 2000000000 | bytes 1000000 | tf_op jit(solution)/shard_map/pallas_call | solution.py:404
  21.9 11.7 %all-to-all-done.1 = f32[256,1,128]{2,1,0:T(1,128)S(1)} async-done(((f32[256,1,128]{2,1,0:T(1,128)}), f32[256,1,128]{2,1,0:T(1,128)S(1)}, u32[]{:S(2)}, u32[]{:S(2)}) %all-to-all-start.1) | async-done | bytes 131104 | tf_op jit(solution)/shard_map/all_to_all | solution.py:416
  33.6 3.8 %all-to-all-start = ((bf16[16,64,128]{2,1,0:T(8,128)(2,1)}), bf16[16,64,128]{2,1,0:T(8,128)(2,1)S(1)}, u32[]{:S(2)}, u32[]{:S(2)}) async-start(bf16[16,64,128]{2,1,0:T(8,128)(2,1)} %shard_map.110), calls=%async_computation | async-start | bytes 524288 | tf_op jit(solution)/shard_map/all_to_all | solution.py:416
  37.4 0.1 pad_add_fusion.where_ref
  37.5 0.8 shard_map.113.stats_ref
  38.3 0.0 copy-start
  38.3 4.1 %shard_map.112 = (f32[8,128,128]{2,1,0:T(8,128)S(1)}, f32[8,1024]{1,0:T(8,128)S(1)}) custom-call(s32[2]{0:T(128)S(1)} %pad_add_fusion.where_ref, f32[256,128]{1,0:T(8,128)S(1)} %bitcast.16), custom_call_target="tpu_custom_call" | custom-call | flops 2000000000 | bytes 1000000 | tf_op jit(solution)/shard_map/pallas_call | solution.py:404
  42.4 6.9 %all-to-all-done.got_ref = bf16[16,64,128]{2,1,0:T(8,128)(2,1)S(1)} async-done(((bf16[16,64,128]{2,1,0:T(8,128)(2,1)}), bf16[16,64,128]{2,1,0:T(8,128)(2,1)S(1)}, u32[]{:S(2)}, u32[]{:S(2)}) %all-to-all-start) | async-done | bytes 262176 | tf_op jit(solution)/shard_map/all_to_all | solution.py:416
  49.3 0.0 copy-done
  49.3 1.9 %shard_map.114 = (bf16[16,64,128]{2,1,0:T(8,128)(2,1)}, f32[8,128,128]{2,1,0:T(8,128)S(1)}, f32[1,128]{1,0:T(1,128)S(1)}) custom-call(s32[2]{0:T(128)S(1)} %pad_add_fusion.where_ref, bf16[16,64,128]{2,1,0:T(8,128)(2,1)S(1)} %all-to-all-done.got_ref, bf16[128,8,128]{2,1,0:T(8,128)(2,1)S(1)} %copy-done, bf16[128,128]{1,0:T(8,128)(2,1)S(1)} %copy-done.5, ...), custom_call_target="tpu_custom_call" | custom-call | flops 2000000000 | bytes 1000000 | tf_op jit(solution)/shard_map/pallas_call | solution.py:404
  51.2 3.4 %all-to-all-start.2 = ((bf16[16,64,128]{2,1,0:T(8,128)(2,1)}), bf16[16,64,128]{2,1,0:T(8,128)(2,1)S(1)}, u32[]{:S(2)}, u32[]{:S(2)}) async-start(bf16[16,64,128]{2,1,0:T(8,128)(2,1)} %get-tuple-element.18), calls=%async_computation.2 | async-start | bytes 524288 | tf_op jit(solution)/shard_map/all_to_all | solution.py:416
  54.6 9.3 %shard_map.115.force_ref = f32[256,128]{1,0:T(8,128)S(1)} custom-call(s32[2]{0:T(128)S(1)} %pad_add_fusion.where_ref, f32[256,128]{1,0:T(8,128)S(1)} %bitcast.17, f32[8,128,128]{2,1,0:T(8,128)S(1)} %get-tuple-element.19.density_ref, f32[8,1024]{1,0:T(8,128)S(1)} %get-tuple-element.20.slots_ref), custom_call_target="tpu_custom_call" | custom-call | flops 2000000000 | bytes 1000000 | tf_op jit(solution)/shard_map/pallas_call | solution.py:404
  63.9 1.7 %all-to-all-done.2.got_ref = bf16[16,64,128]{2,1,0:T(8,128)(2,1)S(1)} async-done(((bf16[16,64,128]{2,1,0:T(8,128)(2,1)}), bf16[16,64,128]{2,1,0:T(8,128)(2,1)S(1)}, u32[]{:S(2)}, u32[]{:S(2)}) %all-to-all-start.2) | async-done | bytes 262176 | tf_op jit(solution)/shard_map/all_to_all | solution.py:416
  65.7 1.7 %shard_map.116 = (f32[8,128,128]{2,1,0:T(8,128)S(1)}, f32[256,128]{1,0:T(8,128)S(1)}) custom-call(s32[2]{0:T(128)S(1)} %pad_add_fusion.where_ref, bf16[16,64,128]{2,1,0:T(8,128)(2,1)S(1)} %all-to-all-done.2.got_ref, bf16[8,128,128]{2,1,0:T(8,128)(2,1)S(1)} %bitcast.22, bf16[128,128]{1,0:T(8,128)(2,1)S(1)} %copy-done.5, f32[256,128]{1,0:T(8,128)S(1)} %shard_map.115.force_ref, ...), custom_call_target="tpu_custom_call" | custom-call | flops 2000000000 | bytes 1000000 | tf_op jit(solution)/shard_map/pallas_call | solution.py:404
  67.3 19.6 %all_to_all.20 = f32[256,1,128]{2,1,0:T(1,128)S(1)} all-to-all(f32[256,1,128]{2,1,0:T(1,128)S(1)} %bitcast.19), channel_id=1, replica_groups=mesh['band'=4,'gvec'=16,'dom'=4] {'gvec','band','dom'}, dimensions={0} | all-to-all | bytes 262144 | tf_op jit(solution)/shard_map/all_to_all | solution.py:416
  86.9 1.7 %shard_map.117 = (bf16[8,128,128]{2,1,0:T(8,128)(2,1)}, f32[3,1024]{1,0:T(4,128)}, f32[1,1]{1,0:T(1,128)}, f32[1,1]{1,0:T(1,128)}, f32[1,8]{1,0:T(1,128)}) custom-call(s32[2]{0:T(128)S(1)} %pad_add_fusion.where_ref, s32[16]{0:T(128)S(1)} %copy-done.4, s32[1]{0:T(128)S(6)} %copy.14.count_hbm.count_ref, f32[256,128]{1,0:T(8,128)S(1)} %bitcast.18, ...), custom_call_target="tpu_custom_call" | custom-call | flops 2000000000 | bytes 1000000 | tf_op jit(solution)/shard_map/pallas_call | solution.py:404
Async XLA Ops:
  1.3 0.7 copy-start.4
  1.9 0.7 copy-start.2
  2.7 0.7 copy-start.3
  3.3 17.2 %copy-start.5 = (bf16[128,128]{1,0:T(8,128)(2,1)S(1)}, bf16[128,128]{1,0:T(8,128)(2,1)}, u32[]{:S(2)}) copy-start(bf16[128,128]{1,0:T(8,128)(2,1)} %constant.17.clone.table_ref) | copy-start | bytes 98308
  4.8 15.7 %copy-start.1 = (bf16[1,8,128,128]{3,2,1,0:T(8,128)(2,1)S(1)}, bf16[1,8,128,128]{3,2,1,0:T(8,128)(2,1)}, u32[]{:S(2)}) copy-start(bf16[1,8,128,128]{3,2,1,0:T(8,128)(2,1)} %param.7) | copy-start | bytes 786436
  4.8 28.7 %all-to-all-start.1 = ((f32[256,1,128]{2,1,0:T(1,128)}), f32[256,1,128]{2,1,0:T(1,128)S(1)}, u32[]{:S(2)}, u32[]{:S(2)}) async-start(f32[256,1,128]{2,1,0:T(1,128)} %bitcast.5), calls=%async_computation.1 | async-start | bytes 262144 | tf_op jit(solution)/shard_map/all_to_all | solution.py:416
  33.6 15.7 %all-to-all-start = ((bf16[16,64,128]{2,1,0:T(8,128)(2,1)}), bf16[16,64,128]{2,1,0:T(8,128)(2,1)S(1)}, u32[]{:S(2)}, u32[]{:S(2)}) async-start(bf16[16,64,128]{2,1,0:T(8,128)(2,1)} %shard_map.110), calls=%async_computation | async-start | bytes 524288 | tf_op jit(solution)/shard_map/all_to_all | solution.py:416
  38.3 11.0 %copy-start = (bf16[128,8,128]{2,1,0:T(8,128)(2,1)S(1)}, bf16[128,8,128]{2,1,0:T(8,128)(2,1)}, u32[]{:S(2)}) copy-start(bf16[128,8,128]{2,1,0:T(8,128)(2,1)} %local_ref.1) | copy-start | bytes 786436
  51.2 14.5 %all-to-all-start.2 = ((bf16[16,64,128]{2,1,0:T(8,128)(2,1)}), bf16[16,64,128]{2,1,0:T(8,128)(2,1)S(1)}, u32[]{:S(2)}, u32[]{:S(2)}) async-start(bf16[16,64,128]{2,1,0:T(8,128)(2,1)} %get-tuple-element.18), calls=%async_computation.2 | async-start | bytes 524288 | tf_op jit(solution)/shard_map/all_to_all | solution.py:416

commit v4 on v3

--- a/solution.py
+++ b/solution.py
@@ -95,7 +95,7 @@
     lane_row = iota((1, 128), 1)
     dead = (lane_row < CAP) & (lane_row >= count_ref[0])
     row = jnp.where(dead, DEAD_MARK, row)
-    out_ref[...] = jnp.broadcast_to(row, out_ref.shape)
+    out_ref[...] = jnp.broadcast_to(row.astype(bf16)[None], out_ref.shape)
 
 
 def section_kernel(coeffs_ref, table_ref, out_ref, wide_ref):
@@ -103,7 +103,8 @@
     along_z = dot_nt(coeffs_ref[...].reshape(1024, GRID), table).astype(bf16)
     for a in range(8):
         wide_ref[:, a, :] = dot_nn(table, along_z[a * GRID : (a + 1) * GRID])
-    out_ref[...] = wide_ref[...].reshape(SHARES, 64, GRID).astype(bf16)
+    out_ref[:, :64, :] = wide_ref[...].reshape(SHARES, 64, GRID).astype(bf16)
+    out_ref[:, 64:, :] = jnp.zeros((SHARES, 16, GRID), bf16)
 
 
 def stats_kernel(where_ref, coeffs_ref, out_ref):
@@ -183,8 +184,11 @@
     return owner, chosen
 
 
-def potential_kernel(where_ref, blocks_ref, potential_ref, slots_ref, gx_ref, depth_ref):
-    blocks = blocks_ref[...]
+def potential_kernel(
+    where_ref, got_ref, potential_ref, slots_ref, blocks_ref, gx_ref, depth_ref
+):
+    blocks = got_ref[:, 64:, :].astype(f32).reshape(OWNERS, 128)
+    blocks_ref[...] = blocks
     owner, chosen = slot_masks(slot_place(blocks))
     rows = jnp.where(chosen, dot_nn(owner, blocks.astype(bf16)), 0.0).astype(bf16)
     pick = jnp.where(iota((8, 128), 1) // CAP == iota((8, 128), 0), 1.0, 0.0).astype(bf16)
@@ -212,7 +216,7 @@
     back_ref, density_ref, energy_ref, local_wide, back_wide,
 ):
     table = table_ref[...]
-    got = got_ref[...].astype(f32)
+    got = got_ref[:, :64, :].astype(f32)
     local_wide[...] = local_ref[...].astype(f32)
     weight = occupancy(jnp.full((1, 1), where_ref[1], jnp.int32))
     energy = jnp.zeros((1, GRID), f32)
@@ -259,9 +263,8 @@
         gz_ref[k] = gz_values[k] * scale
         hz_ref[k] = slope * z_offset * gz_values[k] * scale
 
-    @pl.loop(0, LIVE // 128)
-    def _(chunk):
-        lanes = pl.ds(pl.multiple_of(chunk * 128, 128), 128)
+    for chunk in range(LIVE // 128):
+        lanes = pl.ds(chunk * 128, 128)
         force_x = jnp.zeros((1, 128), f32)
         force_y = jnp.zeros((1, 128), f32)
         force_z = jnp.zeros((1, 128), f32)
@@ -397,7 +400,7 @@
 SMEM = pl.BlockSpec(memory_space=pltpu.SMEM)
 
 
-def call(kernel, inputs, outputs, scratch=(), cost=2000000000, specs=None):
+def call(kernel, inputs, outputs, scratch=(), cost=2000000000, specs=None, room=40):
     if specs is None:
         specs = [SMEM if x.dtype == jnp.int32 else VMEM for x in inputs]
     shapes = [jax.ShapeDtypeStruct(*out) for out in outputs]
@@ -407,7 +410,7 @@
         in_specs=specs,
         out_specs=[VMEM] * len(shapes),
         scratch_shapes=[pltpu.VMEM(*one) if isinstance(one, tuple) else one for one in scratch],
-        compiler_params=pltpu.CompilerParams(vmem_limit_bytes=40 * 1024 * 1024),
+        compiler_params=pltpu.CompilerParams(vmem_limit_bytes=room * 1024 * 1024),
         cost_estimate=pl.CostEstimate(flops=cost, bytes_accessed=1000000, transcendentals=0),
     )(*inputs)
 
@@ -423,7 +426,7 @@
     (own,) = call(
         pick_kernel,
         [near_list, live_count, atom_pos, atom_charge.reshape(1, ATOMS)],
-        [((OWNERS, 128), f32)],
+        [((SHARES, 1, 128), bf16)],
         [
             pltpu.SMEM((CAP,), jnp.int32),
             pltpu.SMEM((1,), jnp.int32),
@@ -431,21 +434,23 @@
             ((1, ATOMS), f32),
             pltpu.SemaphoreType.DMA((4,)),
         ],
-        specs=[pl.BlockSpec(memory_space=pltpu.HBM)] * 4,
-    )
-    blocks = exchange(own.reshape(OWNERS, 1, 128), EVERY).reshape(OWNERS, 128)
+        specs=[pl.BlockSpec(memory_space=pl.ANY)] * 4,
+        room=60,
+    )
+    group = exchange(own, GROUP)
     (sections,) = call(
         section_kernel,
         [coeffs, table],
-        [((SHARES, 64, GRID), bf16)],
+        [((SHARES, 80, GRID), bf16)],
         [((GRID, 8, GRID), f32)],
     )
-    got = exchange(sections, "gvec")
+    rows = jnp.broadcast_to(group.reshape(1, SHARES, 128), (SHARES, SHARES, 128))
+    got = exchange(lax.dynamic_update_slice(sections, rows, (0, 64, 0)), "gvec")
     (stats,) = call(stats_kernel, [where, coeffs], [((1, 128), f32)])
-    potential, slots = call(
+    potential, slots, blocks = call(
         potential_kernel,
-        [where, blocks],
-        [((8, GRID, GRID), f32), ((8, LIVE), f32)],
+        [where, got],
+        [((8, GRID, GRID), f32), ((8, LIVE), f32), ((OWNERS, 128), f32)],
         [((4, GRID, LIVE), bf16), ((4, GRID, LIVE), f32)],
     )
     back, density, energy = call(

time: 89.2 us -> 84.1 us (0.943)
  blocking collectives: 19.6 us -> 17.9 us
  Pallas kernels: 22.3 us -> 20.7 us
  starting transfers between devices: 22.9 us -> 21.8 us
    all_to_all x1, blocking collectives: 19.6 us -> 17.9 us  [exchange(): return lax.all_to_all(block, axes, split_axis=0, concat_axis=0, tiled=True)]
    pallas_call x8, Pallas kernels: 22.3 us -> 20.7 us  [call(): pl.pallas_call(kernel, out_shape=shapes, in_specs=specs, out_specs=[VMEM]...]
    unnamed x12 -> x9, local copies, waits for them, and re-layouts: 2.07 us -> 0.67 us
    all_to_all x3, starting transfers between devices: 22.9 us -> 21.8 us  [exchange(): return lax.all_to_all(block, axes, split_axis=0, concat_axis=0, tiled=True)]
  transfers between devices with their start and end apart: 3 -> 3, of which waited for: 3 -> 3; matrix products, arithmetic and copies ran while one was open for 0% -> 0% of each run, Pallas kernels for 17% -> 11%
where the time goes in v4:
time: 84.1 us; the launch traced here: 83.7 us
  starting transfers between devices  21.8 us (26%)
  Pallas kernels  20.7 us (25%)
  waiting for transfers between devices  20.6 us (24%)
  blocking collectives  17.9 us (21%)
  between operations  1.37 us (2%)
  local copies, waits for them, and re-layouts  1.32 us (2%)
    all_to_all x3, starting transfers between devices, exchange(): return lax.all_to_all(block, axes, split_axis=0, concat_axis=0, tiled=True)  21.8 us
    pallas_call x8, Pallas kernels, call(): pl.pallas_call(kernel, out_shape=shapes, in_specs=specs, out_specs=[VMEM]...  20.7 us
    all_to_all x3, waiting for transfers between devices, exchange(): return lax.all_to_all(block, axes, split_axis=0, concat_axis=0, tiled=True)  20.6 us
    all_to_all x1, blocking collectives, exchange(): return lax.all_to_all(block, axes, split_axis=0, concat_axis=0, tiled=True)  17.9 us
  transfers between devices with their start and end apart: 3, of which 3 were waited for; matrix products, arithmetic and copies ran while one was open for 0% of the time, Pallas kernels for 11%

profile of v4, /device:TPU:1, one launch (start us, length us, event | category | flops | bytes accessed | tf_op | source)
XLA Modules:
  0.0 83.7 jit_solution(4065783468612619739)
XLA Ops:
  1.3 0.0 copy-start.1
  1.3 0.0 copy-start.3
  1.3 1.7 %shard_map.111 = bf16[16,1,128]{2,1,0:T(2,128)(2,1)} custom-call(s32[16]{0:T(128)} %near_ref.1, s32[1]{0:T(128)S(6)} %copy.17.count_hbm.count_ref, f32[3,1024]{1,0:T(4,128)} %pos_hbm.1, f32[1,1024]{1,0:T(1,128)} %bitcast.22), custom_call_target="tpu_custom_call" | custom-call | flops 2000000000 | bytes 1000000 | tf_op jit(solution)/shard_map/pallas_call | solution.py:407
  3.0 7.6 %all-to-all-start = ((bf16[16,1,128]{2,1,0:T(2,128)(2,1)}), bf16[16,1,128]{2,1,0:T(2,128)(2,1)S(1)}, u32[]{:S(2)}, u32[]{:S(2)}) async-start(bf16[16,1,128]{2,1,0:T(2,128)(2,1)} %shard_map.111), calls=%async_computation | async-start | bytes 16384 | tf_op jit(solution)/shard_map/all_to_all | solution.py:419
  10.6 0.0 copy-done.1
  10.6 0.0 copy-done.3
  10.6 1.3 %shard_map.110 = bf16[16,80,128]{2,1,0:T(8,128)(2,1)} custom-call(bf16[8,128,128]{2,1,0:T(8,128)(2,1)S(1)} %bitcast.17, bf16[128,128]{1,0:T(8,128)(2,1)S(1)} %copy-done.3), custom_call_target="tpu_custom_call" | custom-call | flops 2000000000 | bytes 1000000 | tf_op jit(solution)/shard_map/pallas_call | solution.py:407
  11.9 5.0 %all-to-all-done = bf16[16,1,128]{2,1,0:T(2,128)(2,1)S(1)} async-done(((bf16[16,1,128]{2,1,0:T(2,128)(2,1)}), bf16[16,1,128]{2,1,0:T(2,128)(2,1)S(1)}, u32[]{:S(2)}, u32[]{:S(2)}) %all-to-all-start) | async-done | bytes 4128 | tf_op jit(solution)/shard_map/all_to_all | solution.py:419
  16.9 0.7 broadcast_dynamic-update-slice_fusion
  17.6 10.6 %all-to-all-start.1 = ((bf16[16,80,128]{2,1,0:T(8,128)(2,1)}), bf16[16,80,128]{2,1,0:T(8,128)(2,1)S(1)}, u32[]{:S(2)}, u32[]{:S(2)}) async-start(bf16[16,80,128]{2,1,0:T(8,128)(2,1)} %broadcast_dynamic-update-slice_fusion), calls=%async_computation.1 | async-start | bytes 655360 | tf_op jit(solution)/shard_map/all_to_all | solution.py:419
  28.2 0.1 pad_add_fusion.where_ref
  28.2 0.8 shard_map.113.stats_ref
  29.0 0.0 copy-start
  29.1 12.2 %all-to-all-done.1.got_ref = bf16[16,80,128]{2,1,0:T(8,128)(2,1)S(1)} async-done(((bf16[16,80,128]{2,1,0:T(8,128)(2,1)}), bf16[16,80,128]{2,1,0:T(8,128)(2,1)S(1)}, u32[]{:S(2)}, u32[]{:S(2)}) %all-to-all-start.1) | async-done | bytes 327712 | tf_op jit(solution)/shard_map/all_to_all | solution.py:419
  41.2 4.1 %shard_map.112 = (f32[8,128,128]{2,1,0:T(8,128)S(1)}, f32[8,1024]{1,0:T(8,128)S(1)}, f32[256,128]{1,0:T(8,128)S(1)}) custom-call(s32[2]{0:T(128)S(1)} %pad_add_fusion.where_ref, bf16[16,80,128]{2,1,0:T(8,128)(2,1)S(1)} %all-to-all-done.1.got_ref), custom_call_target="tpu_custom_call" | custom-call | flops 2000000000 | bytes 1000000 | tf_op jit(solution)/shard_map/pallas_call | solution.py:407
  45.3 0.0 copy-done
  45.3 1.9 %shard_map.114 = (bf16[16,64,128]{2,1,0:T(8,128)(2,1)}, f32[8,128,128]{2,1,0:T(8,128)S(1)}, f32[1,128]{1,0:T(1,128)S(1)}) custom-call(s32[2]{0:T(128)S(1)} %pad_add_fusion.where_ref, bf16[16,80,128]{2,1,0:T(8,128)(2,1)S(1)} %all-to-all-done.1.got_ref, bf16[128,8,128]{2,1,0:T(8,128)(2,1)S(1)} %copy-done, bf16[128,128]{1,0:T(8,128)(2,1)S(1)} %copy-done.3, ...), custom_call_target="tpu_custom_call" | custom-call | flops 2000000000 | bytes 1000000 | tf_op jit(solution)/shard_map/pallas_call | solution.py:407
  47.3 3.6 %all-to-all-start.2 = ((bf16[16,64,128]{2,1,0:T(8,128)(2,1)}), bf16[16,64,128]{2,1,0:T(8,128)(2,1)S(1)}, u32[]{:S(2)}, u32[]{:S(2)}) async-start(bf16[16,64,128]{2,1,0:T(8,128)(2,1)} %get-tuple-element.19), calls=%async_computation.2 | async-start | bytes 524288 | tf_op jit(solution)/shard_map/all_to_all | solution.py:419
  50.9 7.5 %shard_map.115.force_ref = f32[256,128]{1,0:T(8,128)S(1)} custom-call(s32[2]{0:T(128)S(1)} %pad_add_fusion.where_ref, f32[256,128]{1,0:T(8,128)S(1)} %get-tuple-element.20.blocks_ref, f32[8,128,128]{2,1,0:T(8,128)S(1)} %get-tuple-element.21.density_ref, f32[8,1024]{1,0:T(8,128)S(1)} %get-tuple-element.22.slots_ref), custom_call_target="tpu_custom_call" | custom-call | flops 2000000000 | bytes 1000000 | tf_op jit(solution)/shard_map/pallas_call | solution.py:407
  58.4 3.4 %all-to-all-done.2.got_ref = bf16[16,64,128]{2,1,0:T(8,128)(2,1)S(1)} async-done(((bf16[16,64,128]{2,1,0:T(8,128)(2,1)}), bf16[16,64,128]{2,1,0:T(8,128)(2,1)S(1)}, u32[]{:S(2)}, u32[]{:S(2)}) %all-to-all-start.2) | async-done | bytes 262176 | tf_op jit(solution)/shard_map/all_to_all | solution.py:419
  61.8 1.6 %shard_map.116 = (f32[8,128,128]{2,1,0:T(8,128)S(1)}, f32[256,128]{1,0:T(8,128)S(1)}) custom-call(s32[2]{0:T(128)S(1)} %pad_add_fusion.where_ref, bf16[16,64,128]{2,1,0:T(8,128)(2,1)S(1)} %all-to-all-done.2.got_ref, bf16[8,128,128]{2,1,0:T(8,128)(2,1)S(1)} %bitcast.19, bf16[128,128]{1,0:T(8,128)(2,1)S(1)} %copy-done.3, f32[256,128]{1,0:T(8,128)S(1)} %shard_map.115.force_ref, ...), custom_call_target="tpu_custom_call" | custom-call | flops 2000000000 | bytes 1000000 | tf_op jit(solution)/shard_map/pallas_call | solution.py:407
  63.4 17.9 %all_to_all.20 = f32[256,1,128]{2,1,0:T(1,128)S(1)} all-to-all(f32[256,1,128]{2,1,0:T(1,128)S(1)} %bitcast.16), channel_id=1, replica_groups=mesh['band'=4,'gvec'=16,'dom'=4] {'gvec','band','dom'}, dimensions={0} | all-to-all | bytes 262144 | tf_op jit(solution)/shard_map/all_to_all | solution.py:419
  81.3 0.0 copy-start.2
  81.3 0.7 copy-done.2
  82.0 1.7 %shard_map.117 = (bf16[8,128,128]{2,1,0:T(8,128)(2,1)}, f32[3,1024]{1,0:T(4,128)}, f32[1,1]{1,0:T(1,128)}, f32[1,1]{1,0:T(1,128)}, f32[1,8]{1,0:T(1,128)}) custom-call(s32[2]{0:T(128)S(1)} %pad_add_fusion.where_ref, s32[16]{0:T(128)S(1)} %copy-done.2, s32[1]{0:T(128)S(6)} %copy.17.count_hbm.count_ref, f32[256,128]{1,0:T(8,128)S(1)} %bitcast.15, ...), custom_call_target="tpu_custom_call" | custom-call | flops 2000000000 | bytes 1000000 | tf_op jit(solution)/shard_map/pallas_call | solution.py:407
  (1 shorter events, 0.0 us)
Async XLA Ops:
  1.3 9.3 %copy-start.1 = (bf16[1,8,128,128]{3,2,1,0:T(8,128)(2,1)S(1)}, bf16[1,8,128,128]{3,2,1,0:T(8,128)(2,1)}, u32[]{:S(2)}) copy-start(bf16[1,8,128,128]{3,2,1,0:T(8,128)(2,1)} %param.7) | copy-start | bytes 786436
  1.3 9.3 %copy-start.3 = (bf16[128,128]{1,0:T(8,128)(2,1)S(1)}, bf16[128,128]{1,0:T(8,128)(2,1)}, u32[]{:S(2)}) copy-start(bf16[128,128]{1,0:T(8,128)(2,1)} %constant.21.clone.table_ref) | copy-start | bytes 98308
  3.0 13.9 %all-to-all-start = ((bf16[16,1,128]{2,1,0:T(2,128)(2,1)}), bf16[16,1,128]{2,1,0:T(2,128)(2,1)S(1)}, u32[]{:S(2)}, u32[]{:S(2)}) async-start(bf16[16,1,128]{2,1,0:T(2,128)(2,1)} %shard_map.111), calls=%async_computation | async-start | bytes 16384 | tf_op jit(solution)/shard_map/all_to_all | solution.py:419
  17.6 23.7 %all-to-all-start.1 = ((bf16[16,80,128]{2,1,0:T(8,128)(2,1)}), bf16[16,80,128]{2,1,0:T(8,128)(2,1)S(1)}, u32[]{:S(2)}, u32[]{:S(2)}) async-start(bf16[16,80,128]{2,1,0:T(8,128)(2,1)} %broadcast_dynamic-update-slice_fusion), calls=%async_computation.1 | async-start | bytes 655360 | tf_op jit(solution)/shard_map/all_to_all | solution.py:419
  29.0 16.3 %copy-start = (bf16[128,8,128]{2,1,0:T(8,128)(2,1)S(1)}, bf16[128,8,128]{2,1,0:T(8,128)(2,1)}, u32[]{:S(2)}) copy-start(bf16[128,8,128]{2,1,0:T(8,128)(2,1)} %local_ref.1) | copy-start | bytes 786436
  47.3 14.5 %all-to-all-start.2 = ((bf16[16,64,128]{2,1,0:T(8,128)(2,1)}), bf16[16,64,128]{2,1,0:T(8,128)(2,1)S(1)}, u32[]{:S(2)}, u32[]{:S(2)}) async-start(bf16[16,64,128]{2,1,0:T(8,128)(2,1)} %get-tuple-element.19), calls=%async_computation.2 | async-start | bytes 524288 | tf_op jit(solution)/shard_map/all_to_all | solution.py:419
  81.3 0.7 copy-start.2

commit v5 on v4

--- a/solution.py
+++ b/solution.py
@@ -107,7 +107,9 @@
     out_ref[:, 64:, :] = jnp.zeros((SHARES, 16, GRID), bf16)
 
 
-def stats_kernel(where_ref, coeffs_ref, out_ref):
+def stats_kernel(
+    where_ref, near_ref, count_ref, coeffs_ref, out_ref, hot_ref, halved_ref, drawn_ref
+):
     first = where_ref[0] * 8
     q_wave = iota((GRID, GRID), 0).astype(f32) * WAVE_STEP
     l_wave = iota((1, GRID), 1).astype(f32) * WAVE_STEP
@@ -137,6 +139,13 @@
         value = jnp.sum(sums[i], axis=1, keepdims=True) * weight
         row = jnp.where(lane == SCALAR_LANE + 2 + i, value, row)
     out_ref[...] = row
+    plane_waves = wave_tables()
+    for a in range(8):
+        halved = STEP_SIZE / (1.0 + kinetic_of(where_ref, plane_waves, a))
+        halved_ref[a] = halved
+        drawn_ref[a] = halved * coeffs_ref[a].astype(f32)
+    alive = iota((128, ATOMS), 0) % CAP < count_ref[0]
+    hot_ref[...] = jnp.where(alive, near_one_hot(near_ref), jnp.zeros((), bf16))
 
 
 def gauss_values(offset):
@@ -154,34 +163,29 @@
     return live
 
 
-def place_by_row(live):
-    ones = jnp.ones((128, 128), bf16)
-    counts = dot_nn(live, ones)
+def slot_masks(live):
+    counts = dot_nn(live, jnp.ones((128, 128), bf16))
     before = jnp.where(iota((OWNERS, OWNERS), 1) < iota((OWNERS, OWNERS), 0), 1.0, 0.0).astype(bf16)
     starts = dot_nn(before, counts.astype(bf16))
-    return counts, starts
-
-
-def place_by_lane(live):
-    ones = jnp.ones((128, 128), bf16)
-    counts = dot_nt(ones, live)
-    before = jnp.where(iota((OWNERS, OWNERS), 0) < iota((OWNERS, OWNERS), 1), 1.0, 0.0).astype(bf16)
-    starts = dot_nn(counts.astype(bf16), before)
-    return counts, starts
-
-
-def slot_masks(live):
-    counts, starts = place_by_lane(live)
-    place = iota((LIVE, OWNERS), 0).astype(f32)
-    start_row = starts[:1]
-    owner = (place >= start_row) & (place < start_row + counts[:1])
-    owner = jnp.where(owner, 1.0, 0.0).astype(bf16)
+    ends = starts + counts
+    lane = iota((OWNERS, 128), 1).astype(f32)
+    tiles = []
+    for t in range(LIVE // 128):
+        here = lane + (128.0 * t)
+        tiles.append(jnp.where((here >= starts) & (here < ends), 1.0, 0.0).astype(bf16))
+    return jnp.concatenate(tiles, axis=1), starts
+
+
+def choose(held, starts, rows):
     coarse = jnp.floor(starts * 0.125)
     fine = starts - 8.0 * coarse
-    own_start = 8.0 * dot_nt(owner, coarse.astype(bf16)) + dot_nt(owner, fine.astype(bf16))
-    slot = iota((LIVE, 128), 0).astype(f32) - own_start
-    chosen = slot == (iota((LIVE, 128), 1) % CAP).astype(f32)
-    return owner, chosen
+    left = jnp.concatenate(rows + [coarse.T[:16], fine.T[:16]], axis=0).astype(bf16)
+    moved = dot_nn(left, held)
+    size = moved.shape[0] - 32
+    own_start = 8.0 * moved[size : size + 1] + moved[size + 16 : size + 17]
+    slot = iota((1, LIVE), 1).astype(f32) - own_start
+    chosen = (iota((128, LIVE), 0) % CAP).astype(f32) == slot
+    return chosen, moved
 
 
 def potential_kernel(
@@ -189,10 +193,10 @@
 ):
     blocks = got_ref[:, 64:, :].astype(f32).reshape(OWNERS, 128)
     blocks_ref[...] = blocks
-    owner, chosen = slot_masks(slot_place(blocks))
-    rows = jnp.where(chosen, dot_nn(owner, blocks.astype(bf16)), 0.0).astype(bf16)
+    held, starts = slot_masks(slot_place(blocks))
+    chosen, moved = choose(held, starts, [blocks.T])
     pick = jnp.where(iota((8, 128), 1) // CAP == iota((8, 128), 0), 1.0, 0.0).astype(bf16)
-    slots = dot_nt(pick, rows)
+    slots = dot_nn(pick, jnp.where(chosen, moved[:128], 0.0).astype(bf16))
     slots = slots[:4] + slots[4:]
     slots_ref[...] = jnp.concatenate([slots, slots], axis=0)
     points = iota((GRID, LIVE), 0).astype(f32)
@@ -290,25 +294,18 @@
 
     forces = sum_ref[0:3, :] * -FORCE_UNIT
     high, low = halves(forces)
-    stacked = jnp.concatenate([high, low, jnp.zeros((2, LIVE), f32)], axis=0)
-    live = slot_place(blocks_ref[...])
-    owner, chosen = slot_masks(live)
-    spread = jnp.where(iota((8, 128), 1) // CAP == iota((8, 128), 0), 1.0, 0.0).astype(bf16)
-    per_slot = lax.dot_general(
-        stacked.astype(bf16), spread, (((0,), (0,)), ((), ())), preferred_element_type=f32
-    )
-    per_slot = jnp.where(chosen, per_slot, 0.0).astype(bf16)
-    counts, starts = place_by_row(live)
-    place = iota((OWNERS, 128), 1).astype(f32)
-    total = jnp.zeros((OWNERS, 128), f32)
-    for t in range(LIVE // 128):
-        here = place + (128.0 * t)
-        held = jnp.where((here >= starts) & (here < starts + counts), 1.0, 0.0).astype(bf16)
-        total = total + dot_nn(held, per_slot[t * 128 : (t + 1) * 128])
-    out_ref[...] = total
-
-
-def wave_tables(where_ref):
+    stacked = jnp.concatenate(
+        [jnp.broadcast_to(part[c : c + 1], (CAP, LIVE)) for part in (high, low) for c in range(3)]
+        + [jnp.zeros((128 - 6 * CAP, LIVE), f32)],
+        axis=0,
+    )
+    held, starts = slot_masks(slot_place(blocks_ref[...]))
+    chosen, _ = choose(held, starts, [])
+    per_slot = jnp.where(chosen, stacked, 0.0).astype(bf16)
+    out_ref[...] = dot_nt(per_slot, held).T
+
+
+def wave_tables():
     q_wave = iota((GRID, GRID), 0).astype(f32) * WAVE_STEP
     l_wave = iota((GRID, GRID), 1).astype(f32) * WAVE_STEP
     return q_wave * q_wave + l_wave * l_wave
@@ -320,12 +317,12 @@
 
 
 def image_kernel(
-    where_ref, got_ref, coeffs_ref, table_ref, force_ref, energy_ref,
-    image_ref, out_ref, wide_ref,
+    where_ref, got_ref, coeffs_ref, table_ref, force_ref, energy_ref, halved_ref,
+    ahead_ref, out_ref, wide_ref, image_ref,
 ):
     table = table_ref[...]
     wide_ref[...] = got_ref[...].astype(f32).reshape(GRID, 8, GRID)
-    plane_waves = wave_tables(where_ref)
+    plane_waves = wave_tables()
     overlap = jnp.zeros((1, GRID), f32)
     norm = jnp.zeros((1, GRID), f32)
     for a in range(8):
@@ -336,6 +333,7 @@
         coeff = coeffs_ref[a].astype(f32)
         image = kinetic_of(where_ref, plane_waves, a) * coeff + dot_nn(along_y, table)
         image_ref[a] = image
+        ahead_ref[a] = coeff - halved_ref[a] * image
         overlap = overlap + jnp.sum(coeff * image, axis=0, keepdims=True)
         norm = norm + jnp.sum(coeff * coeff, axis=0, keepdims=True)
     overlap = jnp.sum(overlap, axis=1, keepdims=True)
@@ -353,7 +351,7 @@
 
 
 def final_kernel(
-    where_ref, near_ref, count_ref, got_ref, image_ref, coeffs_ref,
+    where_ref, got_ref, ahead_ref, drawn_ref, hot_ref,
     waves_ref, force_ref, energy_ref, ratio_ref, totals_ref,
 ):
     got = got_ref[...]
@@ -378,20 +376,15 @@
     totals_ref[...] = jnp.concatenate(
         [everything[:, SCALAR_LANE + 3 : SCALAR_LANE + 10], band_energy], axis=1
     )
-    plane_waves = wave_tables(where_ref)
     for a in range(8):
-        coeff = coeffs_ref[a].astype(f32)
-        residual = image_ref[a] - energy * coeff
-        kinetic = kinetic_of(where_ref, plane_waves, a)
-        waves_ref[a] = (coeff - STEP_SIZE * residual / (1.0 + kinetic)).astype(bf16)
+        waves_ref[a] = (ahead_ref[a] + energy * drawn_ref[a]).astype(bf16)
     lane = iota((8, 128), 1)
-    wanted = (lane // CAP) % 3 == iota((8, 128), 0)
-    wanted = wanted & (lane < SCALAR_LANE) & (lane % CAP < count_ref[0])
+    wanted = ((lane // CAP) % 3 == iota((8, 128), 0)) & (lane < SCALAR_LANE)
     split = jnp.where(wanted, everything, 0.0)
     high, rest = halves(split)
     middle, low = halves(rest)
     pieces = jnp.concatenate([high, middle, low, jnp.zeros_like(low)], axis=0).astype(bf16)
-    placed = dot_nn(pieces, near_one_hot(near_ref))
+    placed = dot_nn(pieces, hot_ref[...])
     forces = placed[0:8] + placed[8:16] + placed[16:24]
     force_ref[...] = forces[:3]
 
@@ -446,7 +439,16 @@
     )
     rows = jnp.broadcast_to(group.reshape(1, SHARES, 128), (SHARES, SHARES, 128))
     got = exchange(lax.dynamic_update_slice(sections, rows, (0, 64, 0)), "gvec")
-    (stats,) = call(stats_kernel, [where, coeffs], [((1, 128), f32)])
+    stats, hot, halved, drawn = call(
+        stats_kernel,
+        [where, near_list, live_count, coeffs],
+        [
+            ((1, 128), f32),
+            ((128, ATOMS), bf16),
+            ((8, GRID, GRID), f32),
+            ((8, GRID, GRID), f32),
+        ],
+    )
     potential, slots, blocks = call(
         potential_kernel,
         [where, got],
@@ -478,16 +480,16 @@
             ((8, LIVE), f32),
         ],
     )
-    image, message = call(
+    ahead, message = call(
         image_kernel,
-        [where, returned, coeffs, table, forces, energy],
+        [where, returned, coeffs, table, forces, energy, halved],
         [((8, GRID, GRID), f32), ((OWNERS, 128), f32)],
-        [((GRID, 8, GRID), f32)],
+        [((GRID, 8, GRID), f32), ((8, GRID, GRID), f32)],
     )
     arrived = exchange(message.reshape(OWNERS, 1, 128), EVERY).reshape(OWNERS, 128)
     waves, atom_force, energies, ratio, totals = call(
         final_kernel,
-        [where, near_list, live_count, arrived, image, coeffs],
+        [where, arrived, ahead, drawn, hot],
         [
             ((8, GRID, GRID), bf16),
             ((3, ATOMS), f32),

time: 84.1 us -> 83.1 us (0.988)
  transfers between devices with their start and end apart: 3 -> 3, of which waited for: 3 -> 3; matrix products, arithmetic and copies ran while one was open for 0% -> 0% of each run, Pallas kernels for 11% -> 12%
where the time goes in v5:
time: 83.1 us; the launch traced here: 82.7 us
  starting transfers between devices  21.8 us (26%)
  Pallas kernels  20.5 us (25%)
  waiting for transfers between devices  19.9 us (24%)
  blocking collectives  17.8 us (21%)
  between operations  1.39 us (2%)
  local copies, waits for them, and re-layouts  1.24 us (1%)
    all_to_all x3, starting transfers between devices, exchange(): return lax.all_to_all(block, axes, split_axis=0, concat_axis=0, tiled=True)  21.8 us
    pallas_call x8, Pallas kernels, call(): pl.pallas_call(kernel, out_shape=shapes, in_specs=specs, out_specs=[VMEM]...  20.5 us
    all_to_all x3, waiting for transfers between devices, exchange(): return lax.all_to_all(block, axes, split_axis=0, concat_axis=0, tiled=True)  19.9 us
    all_to_all x1, blocking collectives, exchange(): return lax.all_to_all(block, axes, split_axis=0, concat_axis=0, tiled=True)  17.8 us
  transfers between devices with their start and end apart: 3, of which 3 were waited for; matrix products, arithmetic and copies ran while one was open for 0% of the time, Pallas kernels for 12%

profile of v5, /device:TPU:1, one launch (start us, length us, event | category | flops | bytes accessed | tf_op | source)
XLA Modules:
  0.0 82.7 jit_solution(5144820110212990242)
XLA Ops:
  1.3 0.0 copy-start.1
  1.3 0.0 copy-start.3
  1.3 1.7 %shard_map.111 = bf16[16,1,128]{2,1,0:T(2,128)(2,1)} custom-call(s32[16]{0:T(128)} %near_ref.1, s32[1]{0:T(128)S(6)} %copy.17.count_hbm.count_ref, f32[3,1024]{1,0:T(4,128)} %pos_hbm.1, f32[1,1024]{1,0:T(1,128)} %bitcast.21), custom_call_target="tpu_custom_call" | custom-call | flops 2000000000 | bytes 1000000 | tf_op jit(solution)/shard_map/pallas_call | solution.py:400
  3.0 7.6 %all-to-all-start = ((bf16[16,1,128]{2,1,0:T(2,128)(2,1)}), bf16[16,1,128]{2,1,0:T(2,128)(2,1)S(1)}, u32[]{:S(2)}, u32[]{:S(2)}) async-start(bf16[16,1,128]{2,1,0:T(2,128)(2,1)} %shard_map.111), calls=%async_computation | async-start | bytes 16384 | tf_op jit(solution)/shard_map/all_to_all | solution.py:412
  10.6 0.0 copy-done.1
  10.6 0.0 copy-done.3
  10.6 1.3 %shard_map.110 = bf16[16,80,128]{2,1,0:T(8,128)(2,1)} custom-call(bf16[8,128,128]{2,1,0:T(8,128)(2,1)S(1)} %bitcast.17, bf16[128,128]{1,0:T(8,128)(2,1)S(1)} %copy-done.3), custom_call_target="tpu_custom_call" | custom-call | flops 2000000000 | bytes 1000000 | tf_op jit(solution)/shard_map/pallas_call | solution.py:400
  12.0 5.0 %all-to-all-done = bf16[16,1,128]{2,1,0:T(2,128)(2,1)S(1)} async-done(((bf16[16,1,128]{2,1,0:T(2,128)(2,1)}), bf16[16,1,128]{2,1,0:T(2,128)(2,1)S(1)}, u32[]{:S(2)}, u32[]{:S(2)}) %all-to-all-start) | async-done | bytes 4128 | tf_op jit(solution)/shard_map/all_to_all | solution.py:412
  16.9 0.6 broadcast_dynamic-update-slice_fusion
  17.6 10.6 %all-to-all-start.1 = ((bf16[16,80,128]{2,1,0:T(8,128)(2,1)}), bf16[16,80,128]{2,1,0:T(8,128)(2,1)S(1)}, u32[]{:S(2)}, u32[]{:S(2)}) async-start(bf16[16,80,128]{2,1,0:T(8,128)(2,1)} %broadcast_dynamic-update-slice_fusion), calls=%async_computation.1 | async-start | bytes 655360 | tf_op jit(solution)/shard_map/all_to_all | solution.py:412
  28.2 0.0 copy-start.2
  28.2 0.1 pad_add_fusion.where_ref
  28.2 0.6 copy-done.2
  28.8 1.0 %shard_map.113 = (f32[1,128]{1,0:T(1,128)S(1)}, bf16[128,1024]{1,0:T(8,128)(2,1)S(1)}, f32[8,128,128]{2,1,0:T(8,128)S(1)}, f32[8,128,128]{2,1,0:T(8,128)S(1)}) custom-call(s32[2]{0:T(128)S(1)} %pad_add_fusion.where_ref, s32[16]{0:T(128)S(1)} %copy-done.2, s32[1]{0:T(128)S(6)} %copy.17.count_hbm.count_ref, bf16[8,128,128]{2,1,0:T(8,128)(2,1)S(1)} %bitcast.18), custom_call_target="tpu_custom_call" | custom-call | flops 2000000000 | bytes 1000000 | tf_op jit(solution)/shard_map/pallas_call | solution.py:400
  29.8 0.0 copy-start
  29.8 11.4 %all-to-all-done.1.got_ref = bf16[16,80,128]{2,1,0:T(8,128)(2,1)S(1)} async-done(((bf16[16,80,128]{2,1,0:T(8,128)(2,1)}), bf16[16,80,128]{2,1,0:T(8,128)(2,1)S(1)}, u32[]{:S(2)}, u32[]{:S(2)}) %all-to-all-start.1) | async-done | bytes 327712 | tf_op jit(solution)/shard_map/all_to_all | solution.py:412
  41.2 4.0 %shard_map.112 = (f32[8,128,128]{2,1,0:T(8,128)S(1)}, f32[8,1024]{1,0:T(8,128)S(1)}, f32[256,128]{1,0:T(8,128)S(1)}) custom-call(s32[2]{0:T(128)S(1)} %pad_add_fusion.where_ref, bf16[16,80,128]{2,1,0:T(8,128)(2,1)S(1)} %all-to-all-done.1.got_ref), custom_call_target="tpu_custom_call" | custom-call | flops 2000000000 | bytes 1000000 | tf_op jit(solution)/shard_map/pallas_call | solution.py:400
  45.2 0.0 copy-done
  45.2 1.9 %shard_map.114 = (bf16[16,64,128]{2,1,0:T(8,128)(2,1)}, f32[8,128,128]{2,1,0:T(8,128)S(1)}, f32[1,128]{1,0:T(1,128)S(1)}) custom-call(s32[2]{0:T(128)S(1)} %pad_add_fusion.where_ref, bf16[16,80,128]{2,1,0:T(8,128)(2,1)S(1)} %all-to-all-done.1.got_ref, bf16[128,8,128]{2,1,0:T(8,128)(2,1)S(1)} %copy-done, bf16[128,128]{1,0:T(8,128)(2,1)S(1)} %copy-done.3, ...), custom_call_target="tpu_custom_call" | custom-call | flops 2000000000 | bytes 1000000 | tf_op jit(solution)/shard_map/pallas_call | solution.py:400
  47.1 3.6 %all-to-all-start.2 = ((bf16[16,64,128]{2,1,0:T(8,128)(2,1)}), bf16[16,64,128]{2,1,0:T(8,128)(2,1)S(1)}, u32[]{:S(2)}, u32[]{:S(2)}) async-start(bf16[16,64,128]{2,1,0:T(8,128)(2,1)} %get-tuple-element.24), calls=%async_computation.2 | async-start | bytes 524288 | tf_op jit(solution)/shard_map/all_to_all | solution.py:412
  50.8 7.3 %shard_map.115.force_ref = f32[256,128]{1,0:T(8,128)S(1)} custom-call(s32[2]{0:T(128)S(1)} %pad_add_fusion.where_ref, f32[256,128]{1,0:T(8,128)S(1)} %get-tuple-element.25.blocks_ref, f32[8,128,128]{2,1,0:T(8,128)S(1)} %get-tuple-element.26.density_ref, f32[8,1024]{1,0:T(8,128)S(1)} %get-tuple-element.27.slots_ref), custom_call_target="tpu_custom_call" | custom-call | flops 2000000000 | bytes 1000000 | tf_op jit(solution)/shard_map/pallas_call | solution.py:400
  58.1 3.6 %all-to-all-done.2.got_ref = bf16[16,64,128]{2,1,0:T(8,128)(2,1)S(1)} async-done(((bf16[16,64,128]{2,1,0:T(8,128)(2,1)}), bf16[16,64,128]{2,1,0:T(8,128)(2,1)S(1)}, u32[]{:S(2)}, u32[]{:S(2)}) %all-to-all-start.2) | async-done | bytes 262176 | tf_op jit(solution)/shard_map/all_to_all | solution.py:412
  61.7 1.7 %shard_map.116 = (f32[8,128,128]{2,1,0:T(8,128)S(1)}, f32[256,128]{1,0:T(8,128)S(1)}) custom-call(s32[2]{0:T(128)S(1)} %pad_add_fusion.where_ref, bf16[16,64,128]{2,1,0:T(8,128)(2,1)S(1)} %all-to-all-done.2.got_ref, bf16[8,128,128]{2,1,0:T(8,128)(2,1)S(1)} %bitcast.19, bf16[128,128]{1,0:T(8,128)(2,1)S(1)} %copy-done.3, f32[256,128]{1,0:T(8,128)S(1)} %shard_map.115.force_ref, ...), custom_call_target="tpu_custom_call" | custom-call | flops 2000000000 | bytes 1000000 | tf_op jit(solution)/shard_map/pallas_call | solution.py:400
  63.3 17.8 %all_to_all.20 = f32[256,1,128]{2,1,0:T(1,128)S(1)} all-to-all(f32[256,1,128]{2,1,0:T(1,128)S(1)} %bitcast.16), channel_id=1, replica_groups=mesh['band'=4,'gvec'=16,'dom'=4] {'gvec','band','dom'}, dimensions={0} | all-to-all | bytes 262144 | tf_op jit(solution)/shard_map/all_to_all | solution.py:412
  81.1 1.6 %shard_map.117 = (bf16[8,128,128]{2,1,0:T(8,128)(2,1)}, f32[3,1024]{1,0:T(4,128)}, f32[1,1]{1,0:T(1,128)}, f32[1,1]{1,0:T(1,128)}, f32[1,8]{1,0:T(1,128)}) custom-call(s32[2]{0:T(128)S(1)} %pad_add_fusion.where_ref, f32[256,128]{1,0:T(8,128)S(1)} %bitcast.15, f32[8,128,128]{2,1,0:T(8,128)S(1)} %get-tuple-element.31.ahead_ref, ...), custom_call_target="tpu_custom_call" | custom-call | flops 2000000000 | bytes 1000000 | tf_op jit(solution)/shard_map/pallas_call | solution.py:400
  (1 shorter events, 0.0 us)
Async XLA Ops:
  1.3 9.3 %copy-start.1 = (bf16[1,8,128,128]{3,2,1,0:T(8,128)(2,1)S(1)}, bf16[1,8,128,128]{3,2,1,0:T(8,128)(2,1)}, u32[]{:S(2)}) copy-start(bf16[1,8,128,128]{3,2,1,0:T(8,128)(2,1)} %param.7) | copy-start | bytes 786436
  1.3 9.3 %copy-start.3 = (bf16[128,128]{1,0:T(8,128)(2,1)S(1)}, bf16[128,128]{1,0:T(8,128)(2,1)}, u32[]{:S(2)}) copy-start(bf16[128,128]{1,0:T(8,128)(2,1)} %constant.21.clone.table_ref) | copy-start | bytes 98308
  3.0 13.9 %all-to-all-start = ((bf16[16,1,128]{2,1,0:T(2,128)(2,1)}), bf16[16,1,128]{2,1,0:T(2,128)(2,1)S(1)}, u32[]{:S(2)}, u32[]{:S(2)}) async-start(bf16[16,1,128]{2,1,0:T(2,128)(2,1)} %shard_map.111), calls=%async_computation | async-start | bytes 16384 | tf_op jit(solution)/shard_map/all_to_all | solution.py:412
  17.6 23.7 %all-to-all-start.1 = ((bf16[16,80,128]{2,1,0:T(8,128)(2,1)}), bf16[16,80,128]{2,1,0:T(8,128)(2,1)S(1)}, u32[]{:S(2)}, u32[]{:S(2)}) async-start(bf16[16,80,128]{2,1,0:T(8,128)(2,1)} %broadcast_dynamic-update-slice_fusion), calls=%async_computation.1 | async-start | bytes 655360 | tf_op jit(solution)/shard_map/all_to_all | solution.py:412
  28.2 0.7 copy-start.2
  29.8 15.4 %copy-start = (bf16[128,8,128]{2,1,0:T(8,128)(2,1)S(1)}, bf16[128,8,128]{2,1,0:T(8,128)(2,1)}, u32[]{:S(2)}) copy-start(bf16[128,8,128]{2,1,0:T(8,128)(2,1)} %local_ref.1) | copy-start | bytes 786436
  47.1 14.5 %all-to-all-start.2 = ((bf16[16,64,128]{2,1,0:T(8,128)(2,1)}), bf16[16,64,128]{2,1,0:T(8,128)(2,1)S(1)}, u32[]{:S(2)}, u32[]{:S(2)}) async-start(bf16[16,64,128]{2,1,0:T(8,128)(2,1)} %get-tuple-element.24), calls=%async_computation.2 | async-start | bytes 524288 | tf_op jit(solution)/shard_map/all_to_all | solution.py:412

commit v6 on v5

--- a/solution.py
+++ b/solution.py
@@ -108,9 +108,9 @@
 
 
 def stats_kernel(
-    where_ref, near_ref, count_ref, coeffs_ref, out_ref, hot_ref, halved_ref, drawn_ref
-):
-    first = where_ref[0] * 8
+    near_ref, count_ref, coeffs_ref, out_ref, hot_ref, halved_ref, drawn_ref
+):
+    first = lax.axis_index("gvec") * 8
     q_wave = iota((GRID, GRID), 0).astype(f32) * WAVE_STEP
     l_wave = iota((1, GRID), 1).astype(f32) * WAVE_STEP
     sums = [jnp.zeros((1, GRID), f32) for _ in range(7)]
@@ -133,7 +133,7 @@
         )
         sums = [total + term for total, term in zip(sums, terms)]
     lane = iota((1, GRID), 1)
-    weight = occupancy(jnp.full((1, 1), where_ref[1], jnp.int32)) / CELLS
+    weight = occupancy(jnp.full((1, 1), lax.axis_index(GROUP), jnp.int32)) / CELLS
     row = jnp.where(lane == SCALAR_LANE, jnp.sum(sums[0]), 0.0)
     for i in range(1, 7):
         value = jnp.sum(sums[i], axis=1, keepdims=True) * weight
@@ -141,7 +141,7 @@
     out_ref[...] = row
     plane_waves = wave_tables()
     for a in range(8):
-        halved = STEP_SIZE / (1.0 + kinetic_of(where_ref, plane_waves, a))
+        halved = STEP_SIZE / (1.0 + kinetic_of(plane_waves, a))
         halved_ref[a] = halved
         drawn_ref[a] = halved * coeffs_ref[a].astype(f32)
     alive = iota((128, ATOMS), 0) % CAP < count_ref[0]
@@ -189,7 +189,7 @@
 
 
 def potential_kernel(
-    where_ref, got_ref, potential_ref, slots_ref, blocks_ref, gx_ref, depth_ref
+    got_ref, potential_ref, slots_ref, blocks_ref, gx_ref, depth_ref
 ):
     blocks = got_ref[:, 64:, :].astype(f32).reshape(OWNERS, 128)
     blocks_ref[...] = blocks
@@ -200,7 +200,7 @@
     slots = slots[:4] + slots[4:]
     slots_ref[...] = jnp.concatenate([slots, slots], axis=0)
     points = iota((GRID, LIVE), 0).astype(f32)
-    y_points = (where_ref[0] * 8 + iota((8, LIVE), 0)).astype(f32)
+    y_points = (lax.axis_index("gvec") * 8 + iota((8, LIVE), 0)).astype(f32)
     gx_values = gauss_values(points - slots[0:1])
     gy_values = gauss_values(y_points - slots[1:2])
     gz_values = gauss_values(points - slots[2:3])
@@ -216,13 +216,13 @@
 
 
 def field_kernel(
-    where_ref, got_ref, local_ref, table_ref, potential_ref, stats_ref,
+    got_ref, local_ref, table_ref, potential_ref, stats_ref,
     back_ref, density_ref, energy_ref, local_wide, back_wide,
 ):
     table = table_ref[...]
     got = got_ref[:, :64, :].astype(f32)
     local_wide[...] = local_ref[...].astype(f32)
-    weight = occupancy(jnp.full((1, 1), where_ref[1], jnp.int32))
+    weight = occupancy(jnp.full((1, 1), lax.axis_index(GROUP), jnp.int32))
     energy = jnp.zeros((1, GRID), f32)
     for y in range(8):
         potential = potential_ref[y]
@@ -244,7 +244,7 @@
 
 
 def force_kernel(
-    where_ref, blocks_ref, density_ref, slots_ref, out_ref,
+    blocks_ref, density_ref, slots_ref, out_ref,
     turned_ref, x_ref, gz_ref, hz_ref, gy_ref, hy_ref, sum_ref,
 ):
     for y in range(8):
@@ -252,7 +252,7 @@
     slots = slots_ref[...]
     points = iota((GRID, LIVE), 0).astype(f32)
     x_offset = points - slots[0:1]
-    y_offset = (where_ref[0] * 8 + iota((8, LIVE), 0)).astype(f32) - slots[1:2]
+    y_offset = (lax.axis_index("gvec") * 8 + iota((8, LIVE), 0)).astype(f32) - slots[1:2]
     z_offset = points - slots[2:3]
     gx_values = gauss_values(x_offset)
     gy_values = gauss_values(y_offset)
@@ -311,13 +311,13 @@
     return q_wave * q_wave + l_wave * l_wave
 
 
-def kinetic_of(where_ref, plane_waves, a):
-    a_wave = (where_ref[0] * 8 + a).astype(f32) * WAVE_STEP
+def kinetic_of(plane_waves, a):
+    a_wave = (lax.axis_index("gvec") * 8 + a).astype(f32) * WAVE_STEP
     return 0.5 * (a_wave * a_wave + plane_waves)
 
 
 def image_kernel(
-    where_ref, got_ref, coeffs_ref, table_ref, force_ref, energy_ref, halved_ref,
+    got_ref, coeffs_ref, table_ref, force_ref, energy_ref, halved_ref,
     ahead_ref, out_ref, wide_ref, image_ref,
 ):
     table = table_ref[...]
@@ -331,7 +331,7 @@
             preferred_element_type=f32,
         ).astype(bf16)
         coeff = coeffs_ref[a].astype(f32)
-        image = kinetic_of(where_ref, plane_waves, a) * coeff + dot_nn(along_y, table)
+        image = kinetic_of(plane_waves, a) * coeff + dot_nn(along_y, table)
         image_ref[a] = image
         ahead_ref[a] = coeff - halved_ref[a] * image
         overlap = overlap + jnp.sum(coeff * image, axis=0, keepdims=True)
@@ -351,7 +351,7 @@
 
 
 def final_kernel(
-    where_ref, got_ref, ahead_ref, drawn_ref, hot_ref,
+    got_ref, ahead_ref, drawn_ref, hot_ref,
     waves_ref, force_ref, energy_ref, ratio_ref, totals_ref,
 ):
     got = got_ref[...]
@@ -360,14 +360,14 @@
     norms = by_band[:, column(0)]
     energies = by_band[:, column(1)] / norms
     band = iota((BANDS, 1), 0)
-    own = band == where_ref[1]
+    own = band == lax.axis_index(GROUP)
     energy = jnp.sum(jnp.where(own, energies, 0.0), axis=0, keepdims=True)
     norm = jnp.sum(jnp.where(own, norms, 0.0), axis=0, keepdims=True)
     part_norm = got[:, column(0)]
     part_energy = got[:, column(1)] / jnp.maximum(part_norm, 1e-30)
     shift = part_energy - energy
     spread = got[:, column(2)] + part_norm * shift * shift
-    own_rows = iota((OWNERS, 1), 0) % BANDS == where_ref[1]
+    own_rows = iota((OWNERS, 1), 0) % BANDS == lax.axis_index(GROUP)
     squares = jnp.sum(jnp.where(own_rows, spread, 0.0), axis=0, keepdims=True)
     energy_ref[...] = energy
     ratio_ref[...] = squares / norm
@@ -415,7 +415,6 @@
 def per_device(coeffs, v_local, atom_pos, atom_charge, near_list, live_count):
     table = cosine_table()
     coeffs = coeffs[0]
-    where = jnp.stack([lax.axis_index("gvec"), lax.axis_index(GROUP)]).astype(jnp.int32)
     (own,) = call(
         pick_kernel,
         [near_list, live_count, atom_pos, atom_charge.reshape(1, ATOMS)],
@@ -441,7 +440,7 @@
     got = exchange(lax.dynamic_update_slice(sections, rows, (0, 64, 0)), "gvec")
     stats, hot, halved, drawn = call(
         stats_kernel,
-        [where, near_list, live_count, coeffs],
+        [near_list, live_count, coeffs],
         [
             ((1, 128), f32),
             ((128, ATOMS), bf16),
@@ -451,13 +450,13 @@
     )
     potential, slots, blocks = call(
         potential_kernel,
-        [where, got],
+        [got],
         [((8, GRID, GRID), f32), ((8, LIVE), f32), ((OWNERS, 128), f32)],
         [((4, GRID, LIVE), bf16), ((4, GRID, LIVE), f32)],
     )
     back, density, energy = call(
         field_kernel,
-        [where, got, v_local, table, potential, stats],
+        [got, v_local, table, potential, stats],
         [
             ((SHARES, 64, GRID), bf16),
             ((8, GRID, GRID), f32),
@@ -468,7 +467,7 @@
     returned = exchange(back, "gvec")
     (forces,) = call(
         force_kernel,
-        [where, blocks, density, slots],
+        [blocks, density, slots],
         [((OWNERS, 128), f32)],
         [
             ((8, GRID, GRID), bf16),
@@ -482,14 +481,14 @@
     )
     ahead, message = call(
         image_kernel,
-        [where, returned, coeffs, table, forces, energy, halved],
+        [returned, coeffs, table, forces, energy, halved],
         [((8, GRID, GRID), f32), ((OWNERS, 128), f32)],
         [((GRID, 8, GRID), f32), ((8, GRID, GRID), f32)],
     )
     arrived = exchange(message.reshape(OWNERS, 1, 128), EVERY).reshape(OWNERS, 128)
     waves, atom_force, energies, ratio, totals = call(
         final_kernel,
-        [where, arrived, ahead, drawn, hot],
+        [arrived, ahead, drawn, hot],
         [
             ((8, GRID, GRID), bf16),
             ((3, ATOMS), f32),

time: 83.1 us -> 81 us (0.975)
  Pallas kernels: 20.5 us -> 17.8 us
  waiting for transfers between devices: 19.9 us -> 21.1 us
    pallas_call x8, Pallas kernels: 20.5 us -> 17.8 us  [call(): pl.pallas_call(kernel, out_shape=shapes, in_specs=specs, out_specs=[VMEM]...]
    all_to_all x3, waiting for transfers between devices: 19.9 us -> 21.1 us  [exchange(): return lax.all_to_all(block, axes, split_axis=0, concat_axis=0, tiled=True)]
  transfers between devices with their start and end apart: 3 -> 3, of which waited for: 3 -> 3; matrix products, arithmetic and copies ran while one was open for 0% -> 0% of each run, Pallas kernels for 12% -> 11%
where the time goes in v6:
time: 81 us; the launch traced here: 80.7 us
  starting transfers between devices  21.9 us (27%)
  waiting for transfers between devices  21.1 us (26%)
  Pallas kernels  17.8 us (22%)
  blocking collectives  17.8 us (22%)
  between operations  1.39 us (2%)
    all_to_all x3, starting transfers between devices, exchange(): return lax.all_to_all(block, axes, split_axis=0, concat_axis=0, tiled=True)  21.9 us
    all_to_all x3, waiting for transfers between devices, exchange(): return lax.all_to_all(block, axes, split_axis=0, concat_axis=0, tiled=True)  21.1 us
    pallas_call x8, Pallas kernels, call(): pl.pallas_call(kernel, out_shape=shapes, in_specs=specs, out_specs=[VMEM]...  17.8 us
    all_to_all x1, blocking collectives, exchange(): return lax.all_to_all(block, axes, split_axis=0, concat_axis=0, tiled=True)  17.8 us
  transfers between devices with their start and end apart: 3, of which 3 were waited for; matrix products, arithmetic and copies ran while one was open for 0% of the time, Pallas kernels for 11%

profile of v6, /device:TPU:1, one launch (start us, length us, event | category | flops | bytes accessed | tf_op | source)
XLA Modules:
  0.0 80.7 jit_solution(17704863529550372075)
XLA Ops:
  1.3 0.0 copy-start.1
  1.3 0.0 copy-start.3
  1.3 1.7 %shard_map.111 = bf16[16,1,128]{2,1,0:T(2,128)(2,1)} custom-call(s32[16]{0:T(128)} %near_ref.1, s32[1]{0:T(128)S(6)} %copy.17.count_hbm.count_ref, f32[3,1024]{1,0:T(4,128)} %pos_hbm.1, f32[1,1024]{1,0:T(1,128)} %bitcast.19), custom_call_target="tpu_custom_call" | custom-call | flops 2000000000 | bytes 1000000 | tf_op jit(solution)/shard_map/pallas_call | solution.py:400
  3.0 7.6 %all-to-all-start = ((bf16[16,1,128]{2,1,0:T(2,128)(2,1)}), bf16[16,1,128]{2,1,0:T(2,128)(2,1)S(1)}, u32[]{:S(2)}, u32[]{:S(2)}) async-start(bf16[16,1,128]{2,1,0:T(2,128)(2,1)} %shard_map.111), calls=%async_computation | async-start | bytes 16384 | tf_op jit(solution)/shard_map/all_to_all | solution.py:412
  10.6 0.0 copy-done.1
  10.6 0.0 copy-done.3
  10.6 1.3 %shard_map.110 = bf16[16,80,128]{2,1,0:T(8,128)(2,1)} custom-call(bf16[8,128,128]{2,1,0:T(8,128)(2,1)S(1)} %bitcast.15, bf16[128,128]{1,0:T(8,128)(2,1)S(1)} %copy-done.3), custom_call_target="tpu_custom_call" | custom-call | flops 2000000000 | bytes 1000000 | tf_op jit(solution)/shard_map/pallas_call | solution.py:400
  12.0 5.0 %all-to-all-done = bf16[16,1,128]{2,1,0:T(2,128)(2,1)S(1)} async-done(((bf16[16,1,128]{2,1,0:T(2,128)(2,1)}), bf16[16,1,128]{2,1,0:T(2,128)(2,1)S(1)}, u32[]{:S(2)}, u32[]{:S(2)}) %all-to-all-start) | async-done | bytes 4128 | tf_op jit(solution)/shard_map/all_to_all | solution.py:412
  16.9 0.6 broadcast_dynamic-update-slice_fusion
  17.6 0.0 copy-start.2
  17.6 10.7 %all-to-all-start.1 = ((bf16[16,80,128]{2,1,0:T(8,128)(2,1)}), bf16[16,80,128]{2,1,0:T(8,128)(2,1)S(1)}, u32[]{:S(2)}, u32[]{:S(2)}) async-start(bf16[16,80,128]{2,1,0:T(8,128)(2,1)} %broadcast_dynamic-update-slice_fusion), calls=%async_computation.1 | async-start | bytes 655360 | tf_op jit(solution)/shard_map/all_to_all | solution.py:412
  28.3 0.0 copy-done.2
  28.3 1.0 %shard_map.113 = (f32[1,128]{1,0:T(1,128)S(1)}, bf16[128,1024]{1,0:T(8,128)(2,1)S(1)}, f32[8,128,128]{2,1,0:T(8,128)S(1)}, f32[8,128,128]{2,1,0:T(8,128)S(1)}) custom-call(s32[16]{0:T(128)S(1)} %copy-done.2, s32[1]{0:T(128)S(6)} %copy.17.count_hbm.count_ref, bf16[8,128,128]{2,1,0:T(8,128)(2,1)S(1)} %bitcast.16), custom_call_target="tpu_custom_call" | custom-call | flops 2000000000 | bytes 1000000 | tf_op jit(solution)/shard_map/pallas_call | solution.py:400
  29.3 0.0 copy-start
  29.3 12.0 %all-to-all-done.1.got_ref = bf16[16,80,128]{2,1,0:T(8,128)(2,1)S(1)} async-done(((bf16[16,80,128]{2,1,0:T(8,128)(2,1)}), bf16[16,80,128]{2,1,0:T(8,128)(2,1)S(1)}, u32[]{:S(2)}, u32[]{:S(2)}) %all-to-all-start.1) | async-done | bytes 327712 | tf_op jit(solution)/shard_map/all_to_all | solution.py:412
  41.4 3.4 %shard_map.112 = (f32[8,128,128]{2,1,0:T(8,128)S(1)}, f32[8,1024]{1,0:T(8,128)S(1)}, f32[256,128]{1,0:T(8,128)S(1)}) custom-call(bf16[16,80,128]{2,1,0:T(8,128)(2,1)S(1)} %all-to-all-done.1.got_ref), custom_call_target="tpu_custom_call" | custom-call | flops 2000000000 | bytes 1000000 | tf_op jit(solution)/shard_map/pallas_call | solution.py:400
  44.8 0.0 copy-done
  44.8 1.4 %shard_map.114 = (bf16[16,64,128]{2,1,0:T(8,128)(2,1)}, f32[8,128,128]{2,1,0:T(8,128)S(1)}, f32[1,128]{1,0:T(1,128)S(1)}) custom-call(bf16[16,80,128]{2,1,0:T(8,128)(2,1)S(1)} %all-to-all-done.1.got_ref, bf16[128,8,128]{2,1,0:T(8,128)(2,1)S(1)} %copy-done, bf16[128,128]{1,0:T(8,128)(2,1)S(1)} %copy-done.3, ...), custom_call_target="tpu_custom_call" | custom-call | flops 2000000000 | bytes 1000000 | tf_op jit(solution)/shard_map/pallas_call | solution.py:400
  46.2 3.6 %all-to-all-start.2 = ((bf16[16,64,128]{2,1,0:T(8,128)(2,1)}), bf16[16,64,128]{2,1,0:T(8,128)(2,1)S(1)}, u32[]{:S(2)}, u32[]{:S(2)}) async-start(bf16[16,64,128]{2,1,0:T(8,128)(2,1)} %get-tuple-element.24), calls=%async_computation.2 | async-start | bytes 524288 | tf_op jit(solution)/shard_map/all_to_all | solution.py:412
  49.8 6.8 %shard_map.115.force_ref = f32[256,128]{1,0:T(8,128)S(1)} custom-call(f32[256,128]{1,0:T(8,128)S(1)} %get-tuple-element.25.blocks_ref, f32[8,128,128]{2,1,0:T(8,128)S(1)} %get-tuple-element.26.density_ref, f32[8,1024]{1,0:T(8,128)S(1)} %get-tuple-element.27.slots_ref), custom_call_target="tpu_custom_call" | custom-call | flops 2000000000 | bytes 1000000 | tf_op jit(solution)/shard_map/pallas_call | solution.py:400
  56.6 4.1 %all-to-all-done.2.got_ref = bf16[16,64,128]{2,1,0:T(8,128)(2,1)S(1)} async-done(((bf16[16,64,128]{2,1,0:T(8,128)(2,1)}), bf16[16,64,128]{2,1,0:T(8,128)(2,1)S(1)}, u32[]{:S(2)}, u32[]{:S(2)}) %all-to-all-start.2) | async-done | bytes 262176 | tf_op jit(solution)/shard_map/all_to_all | solution.py:412
  60.7 1.1 %shard_map.116 = (f32[8,128,128]{2,1,0:T(8,128)S(1)}, f32[256,128]{1,0:T(8,128)S(1)}) custom-call(bf16[16,64,128]{2,1,0:T(8,128)(2,1)S(1)} %all-to-all-done.2.got_ref, bf16[8,128,128]{2,1,0:T(8,128)(2,1)S(1)} %bitcast.17, bf16[128,128]{1,0:T(8,128)(2,1)S(1)} %copy-done.3, f32[256,128]{1,0:T(8,128)S(1)} %shard_map.115.force_ref, ...), custom_call_target="tpu_custom_call" | custom-call | flops 2000000000 | bytes 1000000 | tf_op jit(solution)/shard_map/pallas_call | solution.py:400
  61.9 17.8 %all_to_all.20 = f32[256,1,128]{2,1,0:T(1,128)S(1)} all-to-all(f32[256,1,128]{2,1,0:T(1,128)S(1)} %bitcast.14), channel_id=1, replica_groups=mesh['band'=4,'gvec'=16,'dom'=4] {'gvec','band','dom'}, dimensions={0} | all-to-all | bytes 262144 | tf_op jit(solution)/shard_map/all_to_all | solution.py:412
  79.6 1.0 %shard_map.117 = (bf16[8,128,128]{2,1,0:T(8,128)(2,1)}, f32[3,1024]{1,0:T(4,128)}, f32[1,1]{1,0:T(1,128)}, f32[1,1]{1,0:T(1,128)}, f32[1,8]{1,0:T(1,128)}) custom-call(f32[256,128]{1,0:T(8,128)S(1)} %bitcast.13, f32[8,128,128]{2,1,0:T(8,128)S(1)} %get-tuple-element.31.ahead_ref, f32[8,128,128]{2,1,0:T(8,128)S(1)} %get-tuple-element.32.drawn_ref, ...), custom_call_target="tpu_custom_call" | custom-call | flops 2000000000 | bytes 1000000 | tf_op jit(solution)/shard_map/pallas_call | solution.py:400
  (1 shorter events, 0.0 us)
Async XLA Ops:
  1.3 9.3 %copy-start.1 = (bf16[1,8,128,128]{3,2,1,0:T(8,128)(2,1)S(1)}, bf16[1,8,128,128]{3,2,1,0:T(8,128)(2,1)}, u32[]{:S(2)}) copy-start(bf16[1,8,128,128]{3,2,1,0:T(8,128)(2,1)} %param.7) | copy-start | bytes 786436
  1.3 9.3 %copy-start.3 = (bf16[128,128]{1,0:T(8,128)(2,1)S(1)}, bf16[128,128]{1,0:T(8,128)(2,1)}, u32[]{:S(2)}) copy-start(bf16[128,128]{1,0:T(8,128)(2,1)} %constant.6.clone.table_ref) | copy-start | bytes 98308
  3.0 13.9 %all-to-all-start = ((bf16[16,1,128]{2,1,0:T(2,128)(2,1)}), bf16[16,1,128]{2,1,0:T(2,128)(2,1)S(1)}, u32[]{:S(2)}, u32[]{:S(2)}) async-start(bf16[16,1,128]{2,1,0:T(2,128)(2,1)} %shard_map.111), calls=%async_computation | async-start | bytes 16384 | tf_op jit(solution)/shard_map/all_to_all | solution.py:412
  17.6 10.7 %copy-start.2 = (s32[16]{0:T(128)S(1)}, s32[16]{0:T(128)}, u32[]{:S(2)}) copy-start(s32[16]{0:T(128)} %near_ref.1) | copy-start | bytes 196
  17.6 23.8 %all-to-all-start.1 = ((bf16[16,80,128]{2,1,0:T(8,128)(2,1)}), bf16[16,80,128]{2,1,0:T(8,128)(2,1)S(1)}, u32[]{:S(2)}, u32[]{:S(2)}) async-start(bf16[16,80,128]{2,1,0:T(8,128)(2,1)} %broadcast_dynamic-update-slice_fusion), calls=%async_computation.1 | async-start | bytes 655360 | tf_op jit(solution)/shard_map/all_to_all | solution.py:412
  29.3 15.5 %copy-start = (bf16[128,8,128]{2,1,0:T(8,128)(2,1)S(1)}, bf16[128,8,128]{2,1,0:T(8,128)(2,1)}, u32[]{:S(2)}) copy-start(bf16[128,8,128]{2,1,0:T(8,128)(2,1)} %local_ref.1) | copy-start | bytes 786436
  46.2 14.5 %all-to-all-start.2 = ((bf16[16,64,128]{2,1,0:T(8,128)(2,1)}), bf16[16,64,128]{2,1,0:T(8,128)(2,1)S(1)}, u32[]{:S(2)}, u32[]{:S(2)}) async-start(bf16[16,64,128]{2,1,0:T(8,128)(2,1)} %get-tuple-element.24), calls=%async_computation.2 | async-start | bytes 524288 | tf_op jit(solution)/shard_map/all_to_all | solution.py:412

commit v7 on v6

--- a/solution.py
+++ b/solution.py
@@ -35,7 +35,7 @@
     scales = np.where(
         points == 0, np.sqrt(np.float32(1.0 / GRID)), np.sqrt(np.float32(2.0 / GRID))
     ).astype(np.float32)
-    return jnp.asarray(np.cos(angles).astype(np.float32) * scales[None, :], bf16)
+    return np.cos(angles).astype(np.float32) * scales[None, :]
 
 
 def dot_nn(a, b):
@@ -83,13 +83,22 @@
     ]
     for move in moves:
         move.start()
-    for move in moves:
+    moves[0].wait()
+    slot = iota((1, 128), 1) % CAP
+    wanted = jnp.zeros((1, 128), jnp.int32)
+    for s in range(CAP):
+        wanted = jnp.where(slot == s, near_ref[s], wanted)
+    parts = [
+        jnp.where(iota((128, 128), 0) + 128 * t == wanted, 1.0, 0.0).astype(bf16)
+        for t in range(ATOMS // 128)
+    ]
+    one_hot = jnp.concatenate(parts, axis=0)
+    for move in moves[1:]:
         move.wait()
-    one_hot = near_one_hot(near_ref)
     wide = jnp.concatenate([pos_ref[...], charge_ref[...]], axis=0)
     high, low = halves(wide)
     both = jnp.concatenate([high, low], axis=0).astype(bf16)
-    picked = dot_nt(both, one_hot)
+    picked = dot_nn(both, one_hot)
     lane = iota((8, 128), 1)
     row = jnp.sum(jnp.where(lane // CAP == iota((8, 128), 0), picked, 0.0), axis=0, keepdims=True)
     lane_row = iota((1, 128), 1)
@@ -108,7 +117,8 @@
 
 
 def stats_kernel(
-    near_ref, count_ref, coeffs_ref, out_ref, hot_ref, halved_ref, drawn_ref
+    near_ref, count_ref, coeffs_ref, local_ref,
+    out_ref, hot_ref, halved_ref, drawn_ref, turned_ref, wide_ref,
 ):
     first = lax.axis_index("gvec") * 8
     q_wave = iota((GRID, GRID), 0).astype(f32) * WAVE_STEP
@@ -144,6 +154,9 @@
         halved = STEP_SIZE / (1.0 + kinetic_of(plane_waves, a))
         halved_ref[a] = halved
         drawn_ref[a] = halved * coeffs_ref[a].astype(f32)
+    wide_ref[...] = local_ref[...].astype(f32)
+    for y in range(8):
+        turned_ref[y] = wide_ref[:, y, :]
     alive = iota((128, ATOMS), 0) % CAP < count_ref[0]
     hot_ref[...] = jnp.where(alive, near_one_hot(near_ref), jnp.zeros((), bf16))
 
@@ -216,12 +229,12 @@
 
 
 def field_kernel(
-    got_ref, local_ref, table_ref, potential_ref, stats_ref,
-    back_ref, density_ref, energy_ref, local_wide, back_wide,
+    got_ref, local_ref, table_ref, turned_ref, potential_ref, stats_ref,
+    back_ref, density_ref, energy_ref, back_wide,
 ):
     table = table_ref[...]
     got = got_ref[:, :64, :].astype(f32)
-    local_wide[...] = local_ref[...].astype(f32)
+    turned = turned_ref[...]
     weight = occupancy(jnp.full((1, 1), lax.axis_index(GROUP), jnp.int32))
     energy = jnp.zeros((1, GRID), f32)
     for y in range(8):
@@ -231,11 +244,9 @@
         density = weight * real * real
         density_ref[y] = density
         energy = energy + jnp.sum(density * potential, axis=0, keepdims=True)
-        field = local_wide[:, y, :] + potential.astype(bf16).astype(f32)
+        field = local_ref[y] + potential.astype(bf16).astype(f32)
         applied = (field * real).astype(bf16)
-        back = lax.dot_general(
-            table, applied, (((0,), (0,)), ((), ())), preferred_element_type=f32
-        )
+        back = dot_nn(turned, applied)
         back_wide[:, y * 8 : (y + 1) * 8, :] = back.reshape(SHARES, 8, GRID)
     back_ref[...] = back_wide[...].astype(bf16)
     total = jnp.sum(energy, axis=1, keepdims=True) / CELLS
@@ -317,19 +328,17 @@
 
 
 def image_kernel(
-    got_ref, coeffs_ref, table_ref, force_ref, energy_ref, halved_ref,
+    got_ref, coeffs_ref, table_ref, turned_ref, force_ref, energy_ref, halved_ref,
     ahead_ref, out_ref, wide_ref, image_ref,
 ):
     table = table_ref[...]
+    turned = turned_ref[...]
     wide_ref[...] = got_ref[...].astype(f32).reshape(GRID, 8, GRID)
     plane_waves = wave_tables()
     overlap = jnp.zeros((1, GRID), f32)
     norm = jnp.zeros((1, GRID), f32)
     for a in range(8):
-        along_y = lax.dot_general(
-            table, wide_ref[:, a, :].astype(bf16), (((0,), (0,)), ((), ())),
-            preferred_element_type=f32,
-        ).astype(bf16)
+        along_y = dot_nn(turned, wide_ref[:, a, :].astype(bf16)).astype(bf16)
         coeff = coeffs_ref[a].astype(f32)
         image = kinetic_of(plane_waves, a) * coeff + dot_nn(along_y, table)
         image_ref[a] = image
@@ -413,7 +422,8 @@
 
 
 def per_device(coeffs, v_local, atom_pos, atom_charge, near_list, live_count):
-    table = cosine_table()
+    cosines = cosine_table()
+    table, turned = jnp.asarray(cosines, bf16), jnp.asarray(cosines.T, bf16)
     coeffs = coeffs[0]
     (own,) = call(
         pick_kernel,
@@ -438,15 +448,17 @@
     )
     rows = jnp.broadcast_to(group.reshape(1, SHARES, 128), (SHARES, SHARES, 128))
     got = exchange(lax.dynamic_update_slice(sections, rows, (0, 64, 0)), "gvec")
-    stats, hot, halved, drawn = call(
+    stats, hot, halved, drawn, local = call(
         stats_kernel,
-        [near_list, live_count, coeffs],
+        [near_list, live_count, coeffs, v_local],
         [
             ((1, 128), f32),
             ((128, ATOMS), bf16),
             ((8, GRID, GRID), f32),
             ((8, GRID, GRID), f32),
+            ((8, GRID, GRID), f32),
         ],
+        [((GRID, 8, GRID), f32)],
     )
     potential, slots, blocks = call(
         potential_kernel,
@@ -456,13 +468,13 @@
     )
     back, density, energy = call(
         field_kernel,
-        [got, v_local, table, potential, stats],
+        [got, local, table, turned, potential, stats],
         [
             ((SHARES, 64, GRID), bf16),
             ((8, GRID, GRID), f32),
             ((1, 128), f32),
         ],
-        [((GRID, 8, GRID), f32), ((SHARES, 64, GRID), f32)],
+        [((SHARES, 64, GRID), f32)],
     )
     returned = exchange(back, "gvec")
     (forces,) = call(
@@ -481,7 +493,7 @@
     )
     ahead, message = call(
         image_kernel,
-        [returned, coeffs, table, forces, energy, halved],
+        [returned, coeffs, table, turned, forces, energy, halved],
         [((8, GRID, GRID), f32), ((OWNERS, 128), f32)],
         [((GRID, 8, GRID), f32), ((8, GRID, GRID), f32)],
     )

time: 81 us -> 80.8 us (level)
  transfers between devices with their start and end apart: 3 -> 3, of which waited for: 3 -> 3; matrix products, arithmetic and copies ran while one was open for 0% -> 0% of each run, Pallas kernels for 11% -> 12%
where the time goes in v7:
time: 80.8 us; the launch traced here: 80.4 us
  starting transfers between devices  21.9 us (27%)
  waiting for transfers between devices  20.8 us (26%)
  Pallas kernels  17.8 us (22%)
  blocking collectives  17.8 us (22%)
  between operations  1.4 us (2%)
    all_to_all x3, starting transfers between devices, exchange(): return lax.all_to_all(block, axes, split_axis=0, concat_axis=0, tiled=True)  21.9 us
    all_to_all x3, waiting for transfers between devices, exchange(): return lax.all_to_all(block, axes, split_axis=0, concat_axis=0, tiled=True)  20.8 us
    pallas_call x8, Pallas kernels, call(): pl.pallas_call(kernel, out_shape=shapes, in_specs=specs, out_specs=[VMEM]...  17.8 us
    all_to_all x1, blocking collectives, exchange(): return lax.all_to_all(block, axes, split_axis=0, concat_axis=0, tiled=True)  17.8 us
  transfers between devices with their start and end apart: 3, of which 3 were waited for; matrix products, arithmetic and copies ran while one was open for 0% of the time, Pallas kernels for 12%

profile of v7, /device:TPU:1, one launch (start us, length us, event | category | flops | bytes accessed | tf_op | source)
XLA Modules:
  0.0 80.4 jit_solution(1994263803496202417)
XLA Ops:
  1.3 0.0 copy-start.1
  1.3 0.0 copy-start.3
  1.3 1.6 %shard_map.120 = bf16[16,1,128]{2,1,0:T(2,128)(2,1)} custom-call(s32[16]{0:T(128)} %near_ref.1, s32[1]{0:T(128)S(6)} %copy.18.count_hbm.count_ref, f32[3,1024]{1,0:T(4,128)} %pos_hbm.1, f32[1,1024]{1,0:T(1,128)} %bitcast.19), custom_call_target="tpu_custom_call" | custom-call | flops 2000000000 | bytes 1000000 | tf_op jit(solution)/shard_map/pallas_call | solution.py:409
  3.0 7.6 %all-to-all-start = ((bf16[16,1,128]{2,1,0:T(2,128)(2,1)}), bf16[16,1,128]{2,1,0:T(2,128)(2,1)S(1)}, u32[]{:S(2)}, u32[]{:S(2)}) async-start(bf16[16,1,128]{2,1,0:T(2,128)(2,1)} %shard_map.120), calls=%async_computation | async-start | bytes 16384 | tf_op jit(solution)/shard_map/all_to_all | solution.py:421
  10.6 0.0 copy-done.1
  10.6 0.0 copy-done.3
  10.6 1.3 %shard_map.119 = bf16[16,80,128]{2,1,0:T(8,128)(2,1)} custom-call(bf16[8,128,128]{2,1,0:T(8,128)(2,1)S(1)} %bitcast.15, bf16[128,128]{1,0:T(8,128)(2,1)S(1)} %copy-done.3), custom_call_target="tpu_custom_call" | custom-call | flops 2000000000 | bytes 1000000 | tf_op jit(solution)/shard_map/pallas_call | solution.py:409
  11.9 5.0 %all-to-all-done = bf16[16,1,128]{2,1,0:T(2,128)(2,1)S(1)} async-done(((bf16[16,1,128]{2,1,0:T(2,128)(2,1)}), bf16[16,1,128]{2,1,0:T(2,128)(2,1)S(1)}, u32[]{:S(2)}, u32[]{:S(2)}) %all-to-all-start) | async-done | bytes 4128 | tf_op jit(solution)/shard_map/all_to_all | solution.py:421
  16.9 0.6 broadcast_dynamic-update-slice_fusion
  17.5 0.0 copy-start
  17.5 0.0 copy-start.2
  17.6 10.7 %all-to-all-start.1 = ((bf16[16,80,128]{2,1,0:T(8,128)(2,1)}), bf16[16,80,128]{2,1,0:T(8,128)(2,1)S(1)}, u32[]{:S(2)}, u32[]{:S(2)}) async-start(bf16[16,80,128]{2,1,0:T(8,128)(2,1)} %broadcast_dynamic-update-slice_fusion), calls=%async_computation.1 | async-start | bytes 655360 | tf_op jit(solution)/shard_map/all_to_all | solution.py:421
  28.3 0.0 copy-done
  28.3 0.0 copy-done.2
  28.3 1.3 %shard_map.121 = (f32[1,128]{1,0:T(1,128)S(1)}, bf16[128,1024]{1,0:T(8,128)(2,1)S(1)}, f32[8,128,128]{2,1,0:T(8,128)S(1)}, f32[8,128,128]{2,1,0:T(8,128)S(1)}, f32[8,128,128]{2,1,0:T(8,128)S(1)}) custom-call(s32[16]{0:T(128)S(1)} %copy-done.2, s32[1]{0:T(128)S(6)} %copy.18.count_hbm.count_ref, bf16[8,128,128]{2,1,0:T(8,128)(2,1)S(1)} %bitcast.16, ...), custom_call_target="tpu_custom_call" | custom-call | flops 2000000000 | bytes 1000000 | tf_op jit(solution)/shard_map/pallas_call | solution.py:409
  29.6 0.0 copy-start.4
  29.6 11.7 %all-to-all-done.1.got_ref = bf16[16,80,128]{2,1,0:T(8,128)(2,1)S(1)} async-done(((bf16[16,80,128]{2,1,0:T(8,128)(2,1)}), bf16[16,80,128]{2,1,0:T(8,128)(2,1)S(1)}, u32[]{:S(2)}, u32[]{:S(2)}) %all-to-all-start.1) | async-done | bytes 327712 | tf_op jit(solution)/shard_map/all_to_all | solution.py:421
  41.3 3.4 %shard_map.122 = (f32[8,128,128]{2,1,0:T(8,128)S(1)}, f32[8,1024]{1,0:T(8,128)S(1)}, f32[256,128]{1,0:T(8,128)S(1)}) custom-call(bf16[16,80,128]{2,1,0:T(8,128)(2,1)S(1)} %all-to-all-done.1.got_ref), custom_call_target="tpu_custom_call" | custom-call | flops 2000000000 | bytes 1000000 | tf_op jit(solution)/shard_map/pallas_call | solution.py:409
  44.8 0.0 copy-done.4
  44.8 1.1 %shard_map.123 = (bf16[16,64,128]{2,1,0:T(8,128)(2,1)}, f32[8,128,128]{2,1,0:T(8,128)S(1)}, f32[1,128]{1,0:T(1,128)S(1)}) custom-call(bf16[16,80,128]{2,1,0:T(8,128)(2,1)S(1)} %all-to-all-done.1.got_ref, f32[8,128,128]{2,1,0:T(8,128)S(1)} %get-tuple-element.23.local_ref, bf16[128,128]{1,0:T(8,128)(2,1)S(1)} %copy-done.3, bf16[128,128]{1,0:T(8,128)(2,1)S(1)} %copy-done.4, ...), custom_call_target="tpu_custom_call" | custom-call | flops 2000000000 | bytes 1000000 | tf_op jit(solution)/shard_map/pallas_call | solution.py:409
  45.9 3.6 %all-to-all-start.2 = ((bf16[16,64,128]{2,1,0:T(8,128)(2,1)}), bf16[16,64,128]{2,1,0:T(8,128)(2,1)S(1)}, u32[]{:S(2)}, u32[]{:S(2)}) async-start(bf16[16,64,128]{2,1,0:T(8,128)(2,1)} %get-tuple-element.26), calls=%async_computation.2 | async-start | bytes 524288 | tf_op jit(solution)/shard_map/all_to_all | solution.py:421
  49.5 6.8 %shard_map.124.force_ref = f32[256,128]{1,0:T(8,128)S(1)} custom-call(f32[256,128]{1,0:T(8,128)S(1)} %get-tuple-element.27.blocks_ref, f32[8,128,128]{2,1,0:T(8,128)S(1)} %get-tuple-element.28.density_ref, f32[8,1024]{1,0:T(8,128)S(1)} %get-tuple-element.29.slots_ref), custom_call_target="tpu_custom_call" | custom-call | flops 2000000000 | bytes 1000000 | tf_op jit(solution)/shard_map/pallas_call | solution.py:409
  56.3 4.1 %all-to-all-done.2.got_ref = bf16[16,64,128]{2,1,0:T(8,128)(2,1)S(1)} async-done(((bf16[16,64,128]{2,1,0:T(8,128)(2,1)}), bf16[16,64,128]{2,1,0:T(8,128)(2,1)S(1)}, u32[]{:S(2)}, u32[]{:S(2)}) %all-to-all-start.2) | async-done | bytes 262176 | tf_op jit(solution)/shard_map/all_to_all | solution.py:421
  60.4 1.1 %shard_map.125 = (f32[8,128,128]{2,1,0:T(8,128)S(1)}, f32[256,128]{1,0:T(8,128)S(1)}) custom-call(bf16[16,64,128]{2,1,0:T(8,128)(2,1)S(1)} %all-to-all-done.2.got_ref, bf16[8,128,128]{2,1,0:T(8,128)(2,1)S(1)} %bitcast.17, bf16[128,128]{1,0:T(8,128)(2,1)S(1)} %copy-done.3, bf16[128,128]{1,0:T(8,128)(2,1)S(1)} %copy-done.4, ...), custom_call_target="tpu_custom_call" | custom-call | flops 2000000000 | bytes 1000000 | tf_op jit(solution)/shard_map/pallas_call | solution.py:409
  61.6 17.8 %all_to_all.20 = f32[256,1,128]{2,1,0:T(1,128)S(1)} all-to-all(f32[256,1,128]{2,1,0:T(1,128)S(1)} %bitcast.14), channel_id=1, replica_groups=mesh['band'=4,'gvec'=16,'dom'=4] {'gvec','band','dom'}, dimensions={0} | all-to-all | bytes 262144 | tf_op jit(solution)/shard_map/all_to_all | solution.py:421
  79.3 1.0 %shard_map.126 = (bf16[8,128,128]{2,1,0:T(8,128)(2,1)}, f32[3,1024]{1,0:T(4,128)}, f32[1,1]{1,0:T(1,128)}, f32[1,1]{1,0:T(1,128)}, f32[1,8]{1,0:T(1,128)}) custom-call(f32[256,128]{1,0:T(8,128)S(1)} %bitcast.13, f32[8,128,128]{2,1,0:T(8,128)S(1)} %get-tuple-element.33.ahead_ref, f32[8,128,128]{2,1,0:T(8,128)S(1)} %get-tuple-element.34.drawn_ref, ...), custom_call_target="tpu_custom_call" | custom-call | flops 2000000000 | bytes 1000000 | tf_op jit(solution)/shard_map/pallas_call | solution.py:409
  (1 shorter events, 0.0 us)
Async XLA Ops:
  1.3 9.3 %copy-start.1 = (bf16[1,8,128,128]{3,2,1,0:T(8,128)(2,1)S(1)}, bf16[1,8,128,128]{3,2,1,0:T(8,128)(2,1)}, u32[]{:S(2)}) copy-start(bf16[1,8,128,128]{3,2,1,0:T(8,128)(2,1)} %param.8) | copy-start | bytes 786436
  1.3 9.3 %copy-start.3 = (bf16[128,128]{1,0:T(8,128)(2,1)S(1)}, bf16[128,128]{1,0:T(8,128)(2,1)}, u32[]{:S(2)}) copy-start(bf16[128,128]{1,0:T(8,128)(2,1)} %constant.8.clone.table_ref) | copy-start | bytes 98308
  3.0 13.9 %all-to-all-start = ((bf16[16,1,128]{2,1,0:T(2,128)(2,1)}), bf16[16,1,128]{2,1,0:T(2,128)(2,1)S(1)}, u32[]{:S(2)}, u32[]{:S(2)}) async-start(bf16[16,1,128]{2,1,0:T(2,128)(2,1)} %shard_map.120), calls=%async_computation | async-start | bytes 16384 | tf_op jit(solution)/shard_map/all_to_all | solution.py:421
  17.5 10.7 %copy-start = (bf16[128,8,128]{2,1,0:T(8,128)(2,1)S(1)}, bf16[128,8,128]{2,1,0:T(8,128)(2,1)}, u32[]{:S(2)}) copy-start(bf16[128,8,128]{2,1,0:T(8,128)(2,1)} %local_ref.1) | copy-start | bytes 786436
  17.5 10.7 %copy-start.2 = (s32[16]{0:T(128)S(1)}, s32[16]{0:T(128)}, u32[]{:S(2)}) copy-start(s32[16]{0:T(128)} %near_ref.1) | copy-start | bytes 196
  17.6 23.8 %all-to-all-start.1 = ((bf16[16,80,128]{2,1,0:T(8,128)(2,1)}), bf16[16,80,128]{2,1,0:T(8,128)(2,1)S(1)}, u32[]{:S(2)}, u32[]{:S(2)}) async-start(bf16[16,80,128]{2,1,0:T(8,128)(2,1)} %broadcast_dynamic-update-slice_fusion), calls=%async_computation.1 | async-start | bytes 655360 | tf_op jit(solution)/shard_map/all_to_all | solution.py:421
  29.6 15.2 %copy-start.4 = (bf16[128,128]{1,0:T(8,128)(2,1)S(1)}, bf16[128,128]{1,0:T(8,128)(2,1)}, u32[]{:S(2)}) copy-start(bf16[128,128]{1,0:T(8,128)(2,1)} %constant.9.clone.turned_ref) | copy-start | bytes 98308
  45.9 14.5 %all-to-all-start.2 = ((bf16[16,64,128]{2,1,0:T(8,128)(2,1)}), bf16[16,64,128]{2,1,0:T(8,128)(2,1)S(1)}, u32[]{:S(2)}, u32[]{:S(2)}) async-start(bf16[16,64,128]{2,1,0:T(8,128)(2,1)} %get-tuple-element.26), calls=%async_computation.2 | async-start | bytes 524288 | tf_op jit(solution)/shard_map/all_to_all | solution.py:421

commit v8 on v7

--- a/solution.py
+++ b/solution.py
@@ -218,14 +218,14 @@
     gy_values = gauss_values(y_points - slots[1:2])
     gz_values = gauss_values(points - slots[2:3])
     for k in range(4):
-        gx_ref[k] = gx_values[k].astype(bf16)
-        depth_ref[k] = gz_values[k] * (slots[3:4] * KERNEL_WEIGHTS[k])
-    for y in range(8):
-        potential = jnp.zeros((GRID, GRID), f32)
-        for k in range(4):
-            plane = (depth_ref[k] * gy_values[k][y : y + 1]).astype(bf16)
-            potential = potential + dot_nt(gx_ref[k], plane)
-        potential_ref[y] = potential
+        gx_ref[k] = gx_values[k]
+        depth_ref[k] = (gz_values[k] * (slots[3:4] * KERNEL_WEIGHTS[k])).astype(bf16)
+    for k in range(4):
+        plane = jnp.concatenate(
+            [(gx_ref[k] * gy_values[k][y : y + 1]).astype(bf16) for y in range(8)], axis=0
+        )
+        part = dot_nt(plane, depth_ref[k]).reshape(8, GRID, GRID)
+        potential_ref[...] = part if k == 0 else potential_ref[...] + part
 
 
 def field_kernel(
@@ -464,7 +464,7 @@
         potential_kernel,
         [got],
         [((8, GRID, GRID), f32), ((8, LIVE), f32), ((OWNERS, 128), f32)],
-        [((4, GRID, LIVE), bf16), ((4, GRID, LIVE), f32)],
+        [((4, GRID, LIVE), f32), ((4, GRID, LIVE), bf16)],
     )
     back, density, energy = call(
         field_kernel,

time: 80.8 us -> 80.6 us (level)
  no operation moved by 1% of the time
where the time goes in v8:
time: 80.6 us; the launch traced here: 80.2 us
  starting transfers between devices  21.9 us (27%)
  waiting for transfers between devices  20.8 us (26%)
  blocking collectives  17.8 us (22%)
  Pallas kernels  17.6 us (22%)
  between operations  1.4 us (2%)
    all_to_all x3, starting transfers between devices, exchange(): return lax.all_to_all(block, axes, split_axis=0, concat_axis=0, tiled=True)  21.9 us
    all_to_all x3, waiting for transfers between devices, exchange(): return lax.all_to_all(block, axes, split_axis=0, concat_axis=0, tiled=True)  20.8 us
    all_to_all x1, blocking collectives, exchange(): return lax.all_to_all(block, axes, split_axis=0, concat_axis=0, tiled=True)  17.8 us
    pallas_call x8, Pallas kernels, call(): pl.pallas_call(kernel, out_shape=shapes, in_specs=specs, out_specs=[VMEM]...  17.6 us
  transfers between devices with their start and end apart: 3, of which 3 were waited for; matrix products, arithmetic and copies ran while one was open for 0% of the time, Pallas kernels for 12%

profile of v8, /device:TPU:1, one launch (start us, length us, event | category | flops | bytes accessed | tf_op | source)
XLA Modules:
  0.0 80.2 jit_solution(14573370413927755525)
XLA Ops:
  1.3 0.0 copy-start.1
  1.3 0.0 copy-start.3
  1.3 1.6 %shard_map.120 = bf16[16,1,128]{2,1,0:T(2,128)(2,1)} custom-call(s32[16]{0:T(128)} %near_ref.1, s32[1]{0:T(128)S(6)} %copy.18.count_hbm.count_ref, f32[3,1024]{1,0:T(4,128)} %pos_hbm.1, f32[1,1024]{1,0:T(1,128)} %bitcast.19), custom_call_target="tpu_custom_call" | custom-call | flops 2000000000 | bytes 1000000 | tf_op jit(solution)/shard_map/pallas_call | solution.py:409
  3.0 7.6 %all-to-all-start = ((bf16[16,1,128]{2,1,0:T(2,128)(2,1)}), bf16[16,1,128]{2,1,0:T(2,128)(2,1)S(1)}, u32[]{:S(2)}, u32[]{:S(2)}) async-start(bf16[16,1,128]{2,1,0:T(2,128)(2,1)} %shard_map.120), calls=%async_computation | async-start | bytes 16384 | tf_op jit(solution)/shard_map/all_to_all | solution.py:421
  10.6 0.0 copy-done.1
  10.6 0.0 copy-done.3
  10.6 1.3 %shard_map.119 = bf16[16,80,128]{2,1,0:T(8,128)(2,1)} custom-call(bf16[8,128,128]{2,1,0:T(8,128)(2,1)S(1)} %bitcast.15, bf16[128,128]{1,0:T(8,128)(2,1)S(1)} %copy-done.3), custom_call_target="tpu_custom_call" | custom-call | flops 2000000000 | bytes 1000000 | tf_op jit(solution)/shard_map/pallas_call | solution.py:409
  11.9 5.0 %all-to-all-done = bf16[16,1,128]{2,1,0:T(2,128)(2,1)S(1)} async-done(((bf16[16,1,128]{2,1,0:T(2,128)(2,1)}), bf16[16,1,128]{2,1,0:T(2,128)(2,1)S(1)}, u32[]{:S(2)}, u32[]{:S(2)}) %all-to-all-start) | async-done | bytes 4128 | tf_op jit(solution)/shard_map/all_to_all | solution.py:421
  16.9 0.6 broadcast_dynamic-update-slice_fusion
  17.5 0.0 copy-start
  17.5 0.0 copy-start.2
  17.6 10.7 %all-to-all-start.1 = ((bf16[16,80,128]{2,1,0:T(8,128)(2,1)}), bf16[16,80,128]{2,1,0:T(8,128)(2,1)S(1)}, u32[]{:S(2)}, u32[]{:S(2)}) async-start(bf16[16,80,128]{2,1,0:T(8,128)(2,1)} %broadcast_dynamic-update-slice_fusion), calls=%async_computation.1 | async-start | bytes 655360 | tf_op jit(solution)/shard_map/all_to_all | solution.py:421
  28.3 0.0 copy-done
  28.3 0.0 copy-done.2
  28.3 1.3 %shard_map.121 = (f32[1,128]{1,0:T(1,128)S(1)}, bf16[128,1024]{1,0:T(8,128)(2,1)S(1)}, f32[8,128,128]{2,1,0:T(8,128)S(1)}, f32[8,128,128]{2,1,0:T(8,128)S(1)}, f32[8,128,128]{2,1,0:T(8,128)S(1)}) custom-call(s32[16]{0:T(128)S(1)} %copy-done.2, s32[1]{0:T(128)S(6)} %copy.18.count_hbm.count_ref, bf16[8,128,128]{2,1,0:T(8,128)(2,1)S(1)} %bitcast.16, ...), custom_call_target="tpu_custom_call" | custom-call | flops 2000000000 | bytes 1000000 | tf_op jit(solution)/shard_map/pallas_call | solution.py:409
  29.6 0.0 copy-start.4
  29.6 11.7 %all-to-all-done.1.got_ref = bf16[16,80,128]{2,1,0:T(8,128)(2,1)S(1)} async-done(((bf16[16,80,128]{2,1,0:T(8,128)(2,1)}), bf16[16,80,128]{2,1,0:T(8,128)(2,1)S(1)}, u32[]{:S(2)}, u32[]{:S(2)}) %all-to-all-start.1) | async-done | bytes 327712 | tf_op jit(solution)/shard_map/all_to_all | solution.py:421
  41.3 3.2 %shard_map.122 = (f32[8,128,128]{2,1,0:T(8,128)S(1)}, f32[8,1024]{1,0:T(8,128)S(1)}, f32[256,128]{1,0:T(8,128)S(1)}) custom-call(bf16[16,80,128]{2,1,0:T(8,128)(2,1)S(1)} %all-to-all-done.1.got_ref), custom_call_target="tpu_custom_call" | custom-call | flops 2000000000 | bytes 1000000 | tf_op jit(solution)/shard_map/pallas_call | solution.py:409
  44.6 0.0 copy-done.4
  44.6 1.1 %shard_map.123 = (bf16[16,64,128]{2,1,0:T(8,128)(2,1)}, f32[8,128,128]{2,1,0:T(8,128)S(1)}, f32[1,128]{1,0:T(1,128)S(1)}) custom-call(bf16[16,80,128]{2,1,0:T(8,128)(2,1)S(1)} %all-to-all-done.1.got_ref, f32[8,128,128]{2,1,0:T(8,128)S(1)} %get-tuple-element.23.local_ref, bf16[128,128]{1,0:T(8,128)(2,1)S(1)} %copy-done.3, bf16[128,128]{1,0:T(8,128)(2,1)S(1)} %copy-done.4, ...), custom_call_target="tpu_custom_call" | custom-call | flops 2000000000 | bytes 1000000 | tf_op jit(solution)/shard_map/pallas_call | solution.py:409
  45.7 3.6 %all-to-all-start.2 = ((bf16[16,64,128]{2,1,0:T(8,128)(2,1)}), bf16[16,64,128]{2,1,0:T(8,128)(2,1)S(1)}, u32[]{:S(2)}, u32[]{:S(2)}) async-start(bf16[16,64,128]{2,1,0:T(8,128)(2,1)} %get-tuple-element.26), calls=%async_computation.2 | async-start | bytes 524288 | tf_op jit(solution)/shard_map/all_to_all | solution.py:421
  49.3 6.8 %shard_map.124.force_ref = f32[256,128]{1,0:T(8,128)S(1)} custom-call(f32[256,128]{1,0:T(8,128)S(1)} %get-tuple-element.27.blocks_ref, f32[8,128,128]{2,1,0:T(8,128)S(1)} %get-tuple-element.28.density_ref, f32[8,1024]{1,0:T(8,128)S(1)} %get-tuple-element.29.slots_ref), custom_call_target="tpu_custom_call" | custom-call | flops 2000000000 | bytes 1000000 | tf_op jit(solution)/shard_map/pallas_call | solution.py:409
  56.1 4.1 %all-to-all-done.2.got_ref = bf16[16,64,128]{2,1,0:T(8,128)(2,1)S(1)} async-done(((bf16[16,64,128]{2,1,0:T(8,128)(2,1)}), bf16[16,64,128]{2,1,0:T(8,128)(2,1)S(1)}, u32[]{:S(2)}, u32[]{:S(2)}) %all-to-all-start.2) | async-done | bytes 262176 | tf_op jit(solution)/shard_map/all_to_all | solution.py:421
  60.2 1.1 %shard_map.125 = (f32[8,128,128]{2,1,0:T(8,128)S(1)}, f32[256,128]{1,0:T(8,128)S(1)}) custom-call(bf16[16,64,128]{2,1,0:T(8,128)(2,1)S(1)} %all-to-all-done.2.got_ref, bf16[8,128,128]{2,1,0:T(8,128)(2,1)S(1)} %bitcast.17, bf16[128,128]{1,0:T(8,128)(2,1)S(1)} %copy-done.3, bf16[128,128]{1,0:T(8,128)(2,1)S(1)} %copy-done.4, ...), custom_call_target="tpu_custom_call" | custom-call | flops 2000000000 | bytes 1000000 | tf_op jit(solution)/shard_map/pallas_call | solution.py:409
  61.4 17.8 %all_to_all.20 = f32[256,1,128]{2,1,0:T(1,128)S(1)} all-to-all(f32[256,1,128]{2,1,0:T(1,128)S(1)} %bitcast.14), channel_id=1, replica_groups=mesh['band'=4,'gvec'=16,'dom'=4] {'gvec','band','dom'}, dimensions={0} | all-to-all | bytes 262144 | tf_op jit(solution)/shard_map/all_to_all | solution.py:421
  79.1 1.0 %shard_map.126 = (bf16[8,128,128]{2,1,0:T(8,128)(2,1)}, f32[3,1024]{1,0:T(4,128)}, f32[1,1]{1,0:T(1,128)}, f32[1,1]{1,0:T(1,128)}, f32[1,8]{1,0:T(1,128)}) custom-call(f32[256,128]{1,0:T(8,128)S(1)} %bitcast.13, f32[8,128,128]{2,1,0:T(8,128)S(1)} %get-tuple-element.33.ahead_ref, f32[8,128,128]{2,1,0:T(8,128)S(1)} %get-tuple-element.34.drawn_ref, ...), custom_call_target="tpu_custom_call" | custom-call | flops 2000000000 | bytes 1000000 | tf_op jit(solution)/shard_map/pallas_call | solution.py:409
  (1 shorter events, 0.0 us)
Async XLA Ops:
  1.3 9.3 %copy-start.1 = (bf16[1,8,128,128]{3,2,1,0:T(8,128)(2,1)S(1)}, bf16[1,8,128,128]{3,2,1,0:T(8,128)(2,1)}, u32[]{:S(2)}) copy-start(bf16[1,8,128,128]{3,2,1,0:T(8,128)(2,1)} %param.8) | copy-start | bytes 786436
  1.3 9.3 %copy-start.3 = (bf16[128,128]{1,0:T(8,128)(2,1)S(1)}, bf16[128,128]{1,0:T(8,128)(2,1)}, u32[]{:S(2)}) copy-start(bf16[128,128]{1,0:T(8,128)(2,1)} %constant.8.clone.table_ref) | copy-start | bytes 98308
  3.0 13.9 %all-to-all-start = ((bf16[16,1,128]{2,1,0:T(2,128)(2,1)}), bf16[16,1,128]{2,1,0:T(2,128)(2,1)S(1)}, u32[]{:S(2)}, u32[]{:S(2)}) async-start(bf16[16,1,128]{2,1,0:T(2,128)(2,1)} %shard_map.120), calls=%async_computation | async-start | bytes 16384 | tf_op jit(solution)/shard_map/all_to_all | solution.py:421
  17.5 10.7 %copy-start = (bf16[128,8,128]{2,1,0:T(8,128)(2,1)S(1)}, bf16[128,8,128]{2,1,0:T(8,128)(2,1)}, u32[]{:S(2)}) copy-start(bf16[128,8,128]{2,1,0:T(8,128)(2,1)} %local_ref.1) | copy-start | bytes 786436
  17.5 10.7 %copy-start.2 = (s32[16]{0:T(128)S(1)}, s32[16]{0:T(128)}, u32[]{:S(2)}) copy-start(s32[16]{0:T(128)} %near_ref.1) | copy-start | bytes 196
  17.6 23.8 %all-to-all-start.1 = ((bf16[16,80,128]{2,1,0:T(8,128)(2,1)}), bf16[16,80,128]{2,1,0:T(8,128)(2,1)S(1)}, u32[]{:S(2)}, u32[]{:S(2)}) async-start(bf16[16,80,128]{2,1,0:T(8,128)(2,1)} %broadcast_dynamic-update-slice_fusion), calls=%async_computation.1 | async-start | bytes 655360 | tf_op jit(solution)/shard_map/all_to_all | solution.py:421
  29.6 15.0 %copy-start.4 = (bf16[128,128]{1,0:T(8,128)(2,1)S(1)}, bf16[128,128]{1,0:T(8,128)(2,1)}, u32[]{:S(2)}) copy-start(bf16[128,128]{1,0:T(8,128)(2,1)} %constant.9.clone.turned_ref) | copy-start | bytes 98308
  45.7 14.5 %all-to-all-start.2 = ((bf16[16,64,128]{2,1,0:T(8,128)(2,1)}), bf16[16,64,128]{2,1,0:T(8,128)(2,1)S(1)}, u32[]{:S(2)}, u32[]{:S(2)}) async-start(bf16[16,64,128]{2,1,0:T(8,128)(2,1)} %get-tuple-element.26), calls=%async_computation.2 | async-start | bytes 524288 | tf_op jit(solution)/shard_map/all_to_all | solution.py:421

commit v9 on v8

--- a/solution.py
+++ b/solution.py
@@ -254,6 +254,18 @@
     energy_ref[...] = stats_ref[...] + jnp.where(lane == SCALAR_LANE + 9, total, 0.0)
 
 
+def slab_kernel(
+    got_ref, local_ref, table_ref, turned_ref, stats_ref,
+    back_ref, density_ref, energy_ref, slots_ref, blocks_ref,
+    gx_ref, depth_ref, potential_ref, back_wide,
+):
+    potential_kernel(got_ref, potential_ref, slots_ref, blocks_ref, gx_ref, depth_ref)
+    field_kernel(
+        got_ref, local_ref, table_ref, turned_ref, potential_ref, stats_ref,
+        back_ref, density_ref, energy_ref, back_wide,
+    )
+
+
 def force_kernel(
     blocks_ref, density_ref, slots_ref, out_ref,
     turned_ref, x_ref, gz_ref, hz_ref, gy_ref, hy_ref, sum_ref,
@@ -460,21 +472,22 @@
         ],
         [((GRID, 8, GRID), f32)],
     )
-    potential, slots, blocks = call(
-        potential_kernel,
-        [got],
-        [((8, GRID, GRID), f32), ((8, LIVE), f32), ((OWNERS, 128), f32)],
-        [((4, GRID, LIVE), f32), ((4, GRID, LIVE), bf16)],
-    )
-    back, density, energy = call(
-        field_kernel,
-        [got, local, table, turned, potential, stats],
+    back, density, energy, slots, blocks = call(
+        slab_kernel,
+        [got, local, table, turned, stats],
         [
             ((SHARES, 64, GRID), bf16),
             ((8, GRID, GRID), f32),
             ((1, 128), f32),
+            ((8, LIVE), f32),
+            ((OWNERS, 128), f32),
         ],
-        [((SHARES, 64, GRID), f32)],
+        [
+            ((4, GRID, LIVE), f32),
+            ((4, GRID, LIVE), bf16),
+            ((8, GRID, GRID), f32),
+            ((SHARES, 64, GRID), f32),
+        ],
     )
     returned = exchange(back, "gvec")
     (forces,) = call(

time: 80.6 us -> 81.3 us (level)
    pallas_call x8 -> x7, Pallas kernels: 17.6 us -> 18.4 us  [call(): pl.pallas_call(kernel, out_shape=shapes, in_specs=specs, out_specs=[VMEM]...]
where the time goes in v9:
time: 81.3 us; the launch traced here: 81 us
  starting transfers between devices  21.9 us (27%)
  waiting for transfers between devices  20.8 us (26%)
  Pallas kernels  18.4 us (23%)
  blocking collectives  17.8 us (22%)
  between operations  1.38 us (2%)
    all_to_all x3, starting transfers between devices, exchange(): return lax.all_to_all(block, axes, split_axis=0, concat_axis=0, tiled=True)  21.9 us
    all_to_all x3, waiting for transfers between devices, exchange(): return lax.all_to_all(block, axes, split_axis=0, concat_axis=0, tiled=True)  20.8 us
    pallas_call x7, Pallas kernels, call(): pl.pallas_call(kernel, out_shape=shapes, in_specs=specs, out_specs=[VMEM]...  18.4 us
    all_to_all x1, blocking collectives, exchange(): return lax.all_to_all(block, axes, split_axis=0, concat_axis=0, tiled=True)  17.8 us
  transfers between devices with their start and end apart: 3, of which 3 were waited for; matrix products, arithmetic and copies ran while one was open for 0% of the time, Pallas kernels for 12%

profile of v9, /device:TPU:1, one launch (start us, length us, event | category | flops | bytes accessed | tf_op | source)
XLA Modules:
  0.0 81.0 jit_solution(5875425704128412514)
XLA Ops:
  1.3 0.0 copy-start.1
  1.3 0.0 copy-start.3
  1.3 1.6 %shard_map.120 = bf16[16,1,128]{2,1,0:T(2,128)(2,1)} custom-call(s32[16]{0:T(128)} %near_ref.1, s32[1]{0:T(128)S(6)} %copy.18.count_hbm.count_ref, f32[3,1024]{1,0:T(4,128)} %pos_hbm.1, f32[1,1024]{1,0:T(1,128)} %bitcast.19), custom_call_target="tpu_custom_call" | custom-call | flops 2000000000 | bytes 1000000 | tf_op jit(solution)/shard_map/pallas_call | solution.py:421
  3.0 7.6 %all-to-all-start = ((bf16[16,1,128]{2,1,0:T(2,128)(2,1)}), bf16[16,1,128]{2,1,0:T(2,128)(2,1)S(1)}, u32[]{:S(2)}, u32[]{:S(2)}) async-start(bf16[16,1,128]{2,1,0:T(2,128)(2,1)} %shard_map.120), calls=%async_computation | async-start | bytes 16384 | tf_op jit(solution)/shard_map/all_to_all | solution.py:433
  10.6 0.0 copy-done.1
  10.6 0.0 copy-done.3
  10.6 1.3 %shard_map.119 = bf16[16,80,128]{2,1,0:T(8,128)(2,1)} custom-call(bf16[8,128,128]{2,1,0:T(8,128)(2,1)S(1)} %bitcast.15, bf16[128,128]{1,0:T(8,128)(2,1)S(1)} %copy-done.3), custom_call_target="tpu_custom_call" | custom-call | flops 2000000000 | bytes 1000000 | tf_op jit(solution)/shard_map/pallas_call | solution.py:421
  11.9 5.0 %all-to-all-done = bf16[16,1,128]{2,1,0:T(2,128)(2,1)S(1)} async-done(((bf16[16,1,128]{2,1,0:T(2,128)(2,1)}), bf16[16,1,128]{2,1,0:T(2,128)(2,1)S(1)}, u32[]{:S(2)}, u32[]{:S(2)}) %all-to-all-start) | async-done | bytes 4128 | tf_op jit(solution)/shard_map/all_to_all | solution.py:433
  16.9 0.6 broadcast_dynamic-update-slice_fusion
  17.5 0.0 copy-start
  17.5 0.0 copy-start.2
  17.6 10.7 %all-to-all-start.1 = ((bf16[16,80,128]{2,1,0:T(8,128)(2,1)}), bf16[16,80,128]{2,1,0:T(8,128)(2,1)S(1)}, u32[]{:S(2)}, u32[]{:S(2)}) async-start(bf16[16,80,128]{2,1,0:T(8,128)(2,1)} %broadcast_dynamic-update-slice_fusion), calls=%async_computation.1 | async-start | bytes 655360 | tf_op jit(solution)/shard_map/all_to_all | solution.py:433
  28.3 0.0 copy-done
  28.3 0.0 copy-done.2
  28.3 0.0 copy-start.4
  28.3 1.3 %shard_map.121 = (f32[1,128]{1,0:T(1,128)S(1)}, bf16[128,1024]{1,0:T(8,128)(2,1)S(1)}, f32[8,128,128]{2,1,0:T(8,128)S(1)}, f32[8,128,128]{2,1,0:T(8,128)S(1)}, f32[8,128,128]{2,1,0:T(8,128)S(1)}) custom-call(s32[16]{0:T(128)S(1)} %copy-done.2, s32[1]{0:T(128)S(6)} %copy.18.count_hbm.count_ref, bf16[8,128,128]{2,1,0:T(8,128)(2,1)S(1)} %bitcast.16, ...), custom_call_target="tpu_custom_call" | custom-call | flops 2000000000 | bytes 1000000 | tf_op jit(solution)/shard_map/pallas_call | solution.py:421
  29.6 11.7 %all-to-all-done.1.got_ref = bf16[16,80,128]{2,1,0:T(8,128)(2,1)S(1)} async-done(((bf16[16,80,128]{2,1,0:T(8,128)(2,1)}), bf16[16,80,128]{2,1,0:T(8,128)(2,1)S(1)}, u32[]{:S(2)}, u32[]{:S(2)}) %all-to-all-start.1) | async-done | bytes 327712 | tf_op jit(solution)/shard_map/all_to_all | solution.py:433
  41.3 0.0 copy-done.4
  41.3 5.2 %shard_map.122 = (bf16[16,64,128]{2,1,0:T(8,128)(2,1)}, f32[8,128,128]{2,1,0:T(8,128)S(1)}, f32[1,128]{1,0:T(1,128)S(1)}, f32[8,1024]{1,0:T(8,128)S(1)}, f32[256,128]{1,0:T(8,128)S(1)}) custom-call(bf16[16,80,128]{2,1,0:T(8,128)(2,1)S(1)} %all-to-all-done.1.got_ref, f32[8,128,128]{2,1,0:T(8,128)S(1)} %get-tuple-element.22.local_ref, ...), custom_call_target="tpu_custom_call" | custom-call | flops 2000000000 | bytes 1000000 | tf_op jit(solution)/shard_map/pallas_call | solution.py:421
  46.5 3.6 %all-to-all-start.2 = ((bf16[16,64,128]{2,1,0:T(8,128)(2,1)}), bf16[16,64,128]{2,1,0:T(8,128)(2,1)S(1)}, u32[]{:S(2)}, u32[]{:S(2)}) async-start(bf16[16,64,128]{2,1,0:T(8,128)(2,1)} %get-tuple-element.24), calls=%async_computation.2 | async-start | bytes 524288 | tf_op jit(solution)/shard_map/all_to_all | solution.py:433
  50.1 6.8 %shard_map.123.force_ref = f32[256,128]{1,0:T(8,128)S(1)} custom-call(f32[256,128]{1,0:T(8,128)S(1)} %get-tuple-element.25.blocks_ref, f32[8,128,128]{2,1,0:T(8,128)S(1)} %get-tuple-element.26.density_ref, f32[8,1024]{1,0:T(8,128)S(1)} %get-tuple-element.27.slots_ref), custom_call_target="tpu_custom_call" | custom-call | flops 2000000000 | bytes 1000000 | tf_op jit(solution)/shard_map/pallas_call | solution.py:421
  56.9 4.1 %all-to-all-done.2.got_ref = bf16[16,64,128]{2,1,0:T(8,128)(2,1)S(1)} async-done(((bf16[16,64,128]{2,1,0:T(8,128)(2,1)}), bf16[16,64,128]{2,1,0:T(8,128)(2,1)S(1)}, u32[]{:S(2)}, u32[]{:S(2)}) %all-to-all-start.2) | async-done | bytes 262176 | tf_op jit(solution)/shard_map/all_to_all | solution.py:433
  61.0 1.1 %shard_map.124 = (f32[8,128,128]{2,1,0:T(8,128)S(1)}, f32[256,128]{1,0:T(8,128)S(1)}) custom-call(bf16[16,64,128]{2,1,0:T(8,128)(2,1)S(1)} %all-to-all-done.2.got_ref, bf16[8,128,128]{2,1,0:T(8,128)(2,1)S(1)} %bitcast.17, bf16[128,128]{1,0:T(8,128)(2,1)S(1)} %copy-done.3, bf16[128,128]{1,0:T(8,128)(2,1)S(1)} %copy-done.4, ...), custom_call_target="tpu_custom_call" | custom-call | flops 2000000000 | bytes 1000000 | tf_op jit(solution)/shard_map/pallas_call | solution.py:421
  62.2 17.8 %all_to_all.20 = f32[256,1,128]{2,1,0:T(1,128)S(1)} all-to-all(f32[256,1,128]{2,1,0:T(1,128)S(1)} %bitcast.14), channel_id=1, replica_groups=mesh['band'=4,'gvec'=16,'dom'=4] {'gvec','band','dom'}, dimensions={0} | all-to-all | bytes 262144 | tf_op jit(solution)/shard_map/all_to_all | solution.py:433
  79.9 1.0 %shard_map.125 = (bf16[8,128,128]{2,1,0:T(8,128)(2,1)}, f32[3,1024]{1,0:T(4,128)}, f32[1,1]{1,0:T(1,128)}, f32[1,1]{1,0:T(1,128)}, f32[1,8]{1,0:T(1,128)}) custom-call(f32[256,128]{1,0:T(8,128)S(1)} %bitcast.13, f32[8,128,128]{2,1,0:T(8,128)S(1)} %get-tuple-element.31.ahead_ref, f32[8,128,128]{2,1,0:T(8,128)S(1)} %get-tuple-element.32.drawn_ref, ...), custom_call_target="tpu_custom_call" | custom-call | flops 2000000000 | bytes 1000000 | tf_op jit(solution)/shard_map/pallas_call | solution.py:421
  (1 shorter events, 0.0 us)
Async XLA Ops:
  1.3 9.3 %copy-start.1 = (bf16[1,8,128,128]{3,2,1,0:T(8,128)(2,1)S(1)}, bf16[1,8,128,128]{3,2,1,0:T(8,128)(2,1)}, u32[]{:S(2)}) copy-start(bf16[1,8,128,128]{3,2,1,0:T(8,128)(2,1)} %param.8) | copy-start | bytes 786436
  1.3 9.3 %copy-start.3 = (bf16[128,128]{1,0:T(8,128)(2,1)S(1)}, bf16[128,128]{1,0:T(8,128)(2,1)}, u32[]{:S(2)}) copy-start(bf16[128,128]{1,0:T(8,128)(2,1)} %constant.8.clone.table_ref) | copy-start | bytes 98308
  3.0 13.9 %all-to-all-start = ((bf16[16,1,128]{2,1,0:T(2,128)(2,1)}), bf16[16,1,128]{2,1,0:T(2,128)(2,1)S(1)}, u32[]{:S(2)}, u32[]{:S(2)}) async-start(bf16[16,1,128]{2,1,0:T(2,128)(2,1)} %shard_map.120), calls=%async_computation | async-start | bytes 16384 | tf_op jit(solution)/shard_map/all_to_all | solution.py:433
  17.5 10.7 %copy-start = (bf16[128,8,128]{2,1,0:T(8,128)(2,1)S(1)}, bf16[128,8,128]{2,1,0:T(8,128)(2,1)}, u32[]{:S(2)}) copy-start(bf16[128,8,128]{2,1,0:T(8,128)(2,1)} %local_ref.1) | copy-start | bytes 786436
  17.5 10.7 %copy-start.2 = (s32[16]{0:T(128)S(1)}, s32[16]{0:T(128)}, u32[]{:S(2)}) copy-start(s32[16]{0:T(128)} %near_ref.1) | copy-start | bytes 196
  17.6 23.8 %all-to-all-start.1 = ((bf16[16,80,128]{2,1,0:T(8,128)(2,1)}), bf16[16,80,128]{2,1,0:T(8,128)(2,1)S(1)}, u32[]{:S(2)}, u32[]{:S(2)}) async-start(bf16[16,80,128]{2,1,0:T(8,128)(2,1)} %broadcast_dynamic-update-slice_fusion), calls=%async_computation.1 | async-start | bytes 655360 | tf_op jit(solution)/shard_map/all_to_all | solution.py:433
  28.3 13.1 %copy-start.4 = (bf16[128,128]{1,0:T(8,128)(2,1)S(1)}, bf16[128,128]{1,0:T(8,128)(2,1)}, u32[]{:S(2)}) copy-start(bf16[128,128]{1,0:T(8,128)(2,1)} %constant.9.clone.turned_ref) | copy-start | bytes 98308
  46.5 14.5 %all-to-all-start.2 = ((bf16[16,64,128]{2,1,0:T(8,128)(2,1)}), bf16[16,64,128]{2,1,0:T(8,128)(2,1)S(1)}, u32[]{:S(2)}, u32[]{:S(2)}) async-start(bf16[16,64,128]{2,1,0:T(8,128)(2,1)} %get-tuple-element.24), calls=%async_computation.2 | async-start | bytes 524288 | tf_op jit(solution)/shard_map/all_to_all | solution.py:433

commit v10 on v8

--- a/solution.py
+++ b/solution.py
@@ -72,35 +72,25 @@
 
 
 def pick_kernel(
-    near_hbm, count_hbm, pos_hbm, charge_hbm, out_ref,
-    near_ref, count_ref, pos_ref, charge_ref, sems,
+    near_hbm, count_ref, pos_hbm, charge_hbm, out_ref, near_ref, pos_ref, charge_ref, sems
 ):
     moves = [
         pltpu.make_async_copy(near_hbm, near_ref, sems.at[0]),
-        pltpu.make_async_copy(count_hbm, count_ref, sems.at[1]),
-        pltpu.make_async_copy(pos_hbm, pos_ref, sems.at[2]),
-        pltpu.make_async_copy(charge_hbm, charge_ref, sems.at[3]),
+        pltpu.make_async_copy(pos_hbm, pos_ref, sems.at[1]),
+        pltpu.make_async_copy(charge_hbm, charge_ref, sems.at[2]),
     ]
     for move in moves:
         move.start()
-    moves[0].wait()
-    slot = iota((1, 128), 1) % CAP
-    wanted = jnp.zeros((1, 128), jnp.int32)
-    for s in range(CAP):
-        wanted = jnp.where(slot == s, near_ref[s], wanted)
-    parts = [
-        jnp.where(iota((128, 128), 0) + 128 * t == wanted, 1.0, 0.0).astype(bf16)
-        for t in range(ATOMS // 128)
-    ]
-    one_hot = jnp.concatenate(parts, axis=0)
-    for move in moves[1:]:
+    for move in moves:
         move.wait()
-    wide = jnp.concatenate([pos_ref[...], charge_ref[...]], axis=0)
-    high, low = halves(wide)
+    one_hot = jnp.where(iota((ATOMS, CAP), 0) == near_ref[...], 1.0, 0.0).astype(bf16)
+    high, low = halves(jnp.concatenate([pos_ref[...], charge_ref[...]], axis=0))
     both = jnp.concatenate([high, low], axis=0).astype(bf16)
-    picked = dot_nn(both, one_hot)
+    picked = dot_nn(both, one_hot).astype(bf16)
     lane = iota((8, 128), 1)
-    row = jnp.sum(jnp.where(lane // CAP == iota((8, 128), 0), picked, 0.0), axis=0, keepdims=True)
+    spread = jnp.where(iota((CAP, 128), 1) % CAP == iota((CAP, 128), 0), 1.0, 0.0).astype(bf16)
+    wide = dot_nn(picked, spread)
+    row = jnp.sum(jnp.where(lane // CAP == iota((8, 128), 0), wide, 0.0), axis=0, keepdims=True)
     lane_row = iota((1, 128), 1)
     dead = (lane_row < CAP) & (lane_row >= count_ref[0])
     row = jnp.where(dead, DEAD_MARK, row)
@@ -427,16 +417,20 @@
     coeffs = coeffs[0]
     (own,) = call(
         pick_kernel,
-        [near_list, live_count, atom_pos, atom_charge.reshape(1, ATOMS)],
+        [near_list.reshape(1, CAP), live_count, atom_pos, atom_charge.reshape(1, ATOMS)],
         [((SHARES, 1, 128), bf16)],
         [
-            pltpu.SMEM((CAP,), jnp.int32),
-            pltpu.SMEM((1,), jnp.int32),
+            ((1, CAP), jnp.int32),
             ((3, ATOMS), f32),
             ((1, ATOMS), f32),
-            pltpu.SemaphoreType.DMA((4,)),
+            pltpu.SemaphoreType.DMA((3,)),
         ],
-        specs=[pl.BlockSpec(memory_space=pl.ANY)] * 4,
+        specs=[
+            pl.BlockSpec(memory_space=pl.ANY),
+            SMEM,
+            pl.BlockSpec(memory_space=pl.ANY),
+            pl.BlockSpec(memory_space=pl.ANY),
+        ],
         room=60,
     )
     group = exchange(own, GROUP)

time: 80.6 us -> 80.6 us (level)
  no operation moved by 1% of the time
where the time goes in v10:
time: 80.6 us; the launch traced here: 80.2 us
  starting transfers between devices  21.9 us (27%)
  waiting for transfers between devices  20.8 us (26%)
  blocking collectives  17.8 us (22%)
  Pallas kernels  17.6 us (22%)
  between operations  1.4 us (2%)
    all_to_all x3, starting transfers between devices, exchange(): return lax.all_to_all(block, axes, split_axis=0, concat_axis=0, tiled=True)  21.9 us
    all_to_all x3, waiting for transfers between devices, exchange(): return lax.all_to_all(block, axes, split_axis=0, concat_axis=0, tiled=True)  20.8 us
    all_to_all x1, blocking collectives, exchange(): return lax.all_to_all(block, axes, split_axis=0, concat_axis=0, tiled=True)  17.8 us
    pallas_call x8, Pallas kernels, call(): pl.pallas_call(kernel, out_shape=shapes, in_specs=specs, out_specs=[VMEM]...  17.6 us
  transfers between devices with their start and end apart: 3, of which 3 were waited for; matrix products, arithmetic and copies ran while one was open for 0% of the time, Pallas kernels for 12%

profile of v10, /device:TPU:1, one launch (start us, length us, event | category | flops | bytes accessed | tf_op | source)
XLA Modules:
  0.0 80.2 jit_solution(10078106054025759958)
XLA Ops:
  1.3 0.0 copy-start.1
  1.3 0.0 copy-start.3
  1.3 1.7 %shard_map.120 = bf16[16,1,128]{2,1,0:T(2,128)(2,1)} custom-call(s32[1,16]{1,0:T(1,128)} %bitcast.19, s32[1]{0:T(128)S(6)} %copy.18.count_ref, f32[3,1024]{1,0:T(4,128)} %pos_hbm.1, f32[1,1024]{1,0:T(1,128)} %bitcast.21), custom_call_target="tpu_custom_call" | custom-call | flops 2000000000 | bytes 1000000 | tf_op jit(solution)/shard_map/pallas_call | solution.py:399
  3.0 7.6 %all-to-all-start = ((bf16[16,1,128]{2,1,0:T(2,128)(2,1)}), bf16[16,1,128]{2,1,0:T(2,128)(2,1)S(1)}, u32[]{:S(2)}, u32[]{:S(2)}) async-start(bf16[16,1,128]{2,1,0:T(2,128)(2,1)} %shard_map.120), calls=%async_computation | async-start | bytes 16384 | tf_op jit(solution)/shard_map/all_to_all | solution.py:411
  10.6 0.0 copy-done.1
  10.6 0.0 copy-done.3
  10.6 1.3 %shard_map.119 = bf16[16,80,128]{2,1,0:T(8,128)(2,1)} custom-call(bf16[8,128,128]{2,1,0:T(8,128)(2,1)S(1)} %bitcast.16, bf16[128,128]{1,0:T(8,128)(2,1)S(1)} %copy-done.3), custom_call_target="tpu_custom_call" | custom-call | flops 2000000000 | bytes 1000000 | tf_op jit(solution)/shard_map/pallas_call | solution.py:399
  12.0 5.0 %all-to-all-done = bf16[16,1,128]{2,1,0:T(2,128)(2,1)S(1)} async-done(((bf16[16,1,128]{2,1,0:T(2,128)(2,1)}), bf16[16,1,128]{2,1,0:T(2,128)(2,1)S(1)}, u32[]{:S(2)}, u32[]{:S(2)}) %all-to-all-start) | async-done | bytes 4128 | tf_op jit(solution)/shard_map/all_to_all | solution.py:411
  16.9 0.6 broadcast_dynamic-update-slice_fusion
  17.6 0.0 copy-start
  17.6 0.0 copy-start.2
  17.6 10.7 %all-to-all-start.1 = ((bf16[16,80,128]{2,1,0:T(8,128)(2,1)}), bf16[16,80,128]{2,1,0:T(8,128)(2,1)S(1)}, u32[]{:S(2)}, u32[]{:S(2)}) async-start(bf16[16,80,128]{2,1,0:T(8,128)(2,1)} %broadcast_dynamic-update-slice_fusion), calls=%async_computation.1 | async-start | bytes 655360 | tf_op jit(solution)/shard_map/all_to_all | solution.py:411
  28.3 0.0 copy-done
  28.3 0.0 copy-done.2
  28.3 1.3 %shard_map.121 = (f32[1,128]{1,0:T(1,128)S(1)}, bf16[128,1024]{1,0:T(8,128)(2,1)S(1)}, f32[8,128,128]{2,1,0:T(8,128)S(1)}, f32[8,128,128]{2,1,0:T(8,128)S(1)}, f32[8,128,128]{2,1,0:T(8,128)S(1)}) custom-call(s32[16]{0:T(128)S(1)} %copy-done.2, s32[1]{0:T(128)S(6)} %copy.18.count_ref, bf16[8,128,128]{2,1,0:T(8,128)(2,1)S(1)} %bitcast.17, ...), custom_call_target="tpu_custom_call" | custom-call | flops 2000000000 | bytes 1000000 | tf_op jit(solution)/shard_map/pallas_call | solution.py:399
  29.6 0.0 copy-start.4
  29.7 11.7 %all-to-all-done.1.got_ref = bf16[16,80,128]{2,1,0:T(8,128)(2,1)S(1)} async-done(((bf16[16,80,128]{2,1,0:T(8,128)(2,1)}), bf16[16,80,128]{2,1,0:T(8,128)(2,1)S(1)}, u32[]{:S(2)}, u32[]{:S(2)}) %all-to-all-start.1) | async-done | bytes 327712 | tf_op jit(solution)/shard_map/all_to_all | solution.py:411
  41.4 3.2 %shard_map.122 = (f32[8,128,128]{2,1,0:T(8,128)S(1)}, f32[8,1024]{1,0:T(8,128)S(1)}, f32[256,128]{1,0:T(8,128)S(1)}) custom-call(bf16[16,80,128]{2,1,0:T(8,128)(2,1)S(1)} %all-to-all-done.1.got_ref), custom_call_target="tpu_custom_call" | custom-call | flops 2000000000 | bytes 1000000 | tf_op jit(solution)/shard_map/pallas_call | solution.py:399
  44.6 0.0 copy-done.4
  44.6 1.1 %shard_map.123 = (bf16[16,64,128]{2,1,0:T(8,128)(2,1)}, f32[8,128,128]{2,1,0:T(8,128)S(1)}, f32[1,128]{1,0:T(1,128)S(1)}) custom-call(bf16[16,80,128]{2,1,0:T(8,128)(2,1)S(1)} %all-to-all-done.1.got_ref, f32[8,128,128]{2,1,0:T(8,128)S(1)} %get-tuple-element.23.local_ref, bf16[128,128]{1,0:T(8,128)(2,1)S(1)} %copy-done.3, bf16[128,128]{1,0:T(8,128)(2,1)S(1)} %copy-done.4, ...), custom_call_target="tpu_custom_call" | custom-call | flops 2000000000 | bytes 1000000 | tf_op jit(solution)/shard_map/pallas_call | solution.py:399
  45.8 3.6 %all-to-all-start.2 = ((bf16[16,64,128]{2,1,0:T(8,128)(2,1)}), bf16[16,64,128]{2,1,0:T(8,128)(2,1)S(1)}, u32[]{:S(2)}, u32[]{:S(2)}) async-start(bf16[16,64,128]{2,1,0:T(8,128)(2,1)} %get-tuple-element.26), calls=%async_computation.2 | async-start | bytes 524288 | tf_op jit(solution)/shard_map/all_to_all | solution.py:411
  49.4 6.8 %shard_map.124.force_ref = f32[256,128]{1,0:T(8,128)S(1)} custom-call(f32[256,128]{1,0:T(8,128)S(1)} %get-tuple-element.27.blocks_ref, f32[8,128,128]{2,1,0:T(8,128)S(1)} %get-tuple-element.28.density_ref, f32[8,1024]{1,0:T(8,128)S(1)} %get-tuple-element.29.slots_ref), custom_call_target="tpu_custom_call" | custom-call | flops 2000000000 | bytes 1000000 | tf_op jit(solution)/shard_map/pallas_call | solution.py:399
  56.2 4.1 %all-to-all-done.2.got_ref = bf16[16,64,128]{2,1,0:T(8,128)(2,1)S(1)} async-done(((bf16[16,64,128]{2,1,0:T(8,128)(2,1)}), bf16[16,64,128]{2,1,0:T(8,128)(2,1)S(1)}, u32[]{:S(2)}, u32[]{:S(2)}) %all-to-all-start.2) | async-done | bytes 262176 | tf_op jit(solution)/shard_map/all_to_all | solution.py:411
  60.3 1.1 %shard_map.125 = (f32[8,128,128]{2,1,0:T(8,128)S(1)}, f32[256,128]{1,0:T(8,128)S(1)}) custom-call(bf16[16,64,128]{2,1,0:T(8,128)(2,1)S(1)} %all-to-all-done.2.got_ref, bf16[8,128,128]{2,1,0:T(8,128)(2,1)S(1)} %bitcast.18, bf16[128,128]{1,0:T(8,128)(2,1)S(1)} %copy-done.3, bf16[128,128]{1,0:T(8,128)(2,1)S(1)} %copy-done.4, ...), custom_call_target="tpu_custom_call" | custom-call | flops 2000000000 | bytes 1000000 | tf_op jit(solution)/shard_map/pallas_call | solution.py:399
  61.4 17.8 %all_to_all.20 = f32[256,1,128]{2,1,0:T(1,128)S(1)} all-to-all(f32[256,1,128]{2,1,0:T(1,128)S(1)} %bitcast.15), channel_id=1, replica_groups=mesh['band'=4,'gvec'=16,'dom'=4] {'gvec','band','dom'}, dimensions={0} | all-to-all | bytes 262144 | tf_op jit(solution)/shard_map/all_to_all | solution.py:411
  79.2 1.0 %shard_map.126 = (bf16[8,128,128]{2,1,0:T(8,128)(2,1)}, f32[3,1024]{1,0:T(4,128)}, f32[1,1]{1,0:T(1,128)}, f32[1,1]{1,0:T(1,128)}, f32[1,8]{1,0:T(1,128)}) custom-call(f32[256,128]{1,0:T(8,128)S(1)} %bitcast.14, f32[8,128,128]{2,1,0:T(8,128)S(1)} %get-tuple-element.33.ahead_ref, f32[8,128,128]{2,1,0:T(8,128)S(1)} %get-tuple-element.34.drawn_ref, ...), custom_call_target="tpu_custom_call" | custom-call | flops 2000000000 | bytes 1000000 | tf_op jit(solution)/shard_map/pallas_call | solution.py:399
  (1 shorter events, 0.0 us)
Async XLA Ops:
  1.3 9.3 %copy-start.1 = (bf16[1,8,128,128]{3,2,1,0:T(8,128)(2,1)S(1)}, bf16[1,8,128,128]{3,2,1,0:T(8,128)(2,1)}, u32[]{:S(2)}) copy-start(bf16[1,8,128,128]{3,2,1,0:T(8,128)(2,1)} %param.8) | copy-start | bytes 786436
  1.3 9.3 %copy-start.3 = (bf16[128,128]{1,0:T(8,128)(2,1)S(1)}, bf16[128,128]{1,0:T(8,128)(2,1)}, u32[]{:S(2)}) copy-start(bf16[128,128]{1,0:T(8,128)(2,1)} %constant.8.clone.table_ref) | copy-start | bytes 98308
  3.0 13.9 %all-to-all-start = ((bf16[16,1,128]{2,1,0:T(2,128)(2,1)}), bf16[16,1,128]{2,1,0:T(2,128)(2,1)S(1)}, u32[]{:S(2)}, u32[]{:S(2)}) async-start(bf16[16,1,128]{2,1,0:T(2,128)(2,1)} %shard_map.120), calls=%async_computation | async-start | bytes 16384 | tf_op jit(solution)/shard_map/all_to_all | solution.py:411
  17.6 10.7 %copy-start = (bf16[128,8,128]{2,1,0:T(8,128)(2,1)S(1)}, bf16[128,8,128]{2,1,0:T(8,128)(2,1)}, u32[]{:S(2)}) copy-start(bf16[128,8,128]{2,1,0:T(8,128)(2,1)} %local_ref.1) | copy-start | bytes 786436
  17.6 10.7 %copy-start.2 = (s32[16]{0:T(128)S(1)}, s32[16]{0:T(128)}, u32[]{:S(2)}) copy-start(s32[16]{0:T(128)} %near_ref.1) | copy-start | bytes 196
  17.6 23.8 %all-to-all-start.1 = ((bf16[16,80,128]{2,1,0:T(8,128)(2,1)}), bf16[16,80,128]{2,1,0:T(8,128)(2,1)S(1)}, u32[]{:S(2)}, u32[]{:S(2)}) async-start(bf16[16,80,128]{2,1,0:T(8,128)(2,1)} %broadcast_dynamic-update-slice_fusion), calls=%async_computation.1 | async-start | bytes 655360 | tf_op jit(solution)/shard_map/all_to_all | solution.py:411
  29.6 15.0 %copy-start.4 = (bf16[128,128]{1,0:T(8,128)(2,1)S(1)}, bf16[128,128]{1,0:T(8,128)(2,1)}, u32[]{:S(2)}) copy-start(bf16[128,128]{1,0:T(8,128)(2,1)} %constant.9.clone.turned_ref) | copy-start | bytes 98308
  45.8 14.5 %all-to-all-start.2 = ((bf16[16,64,128]{2,1,0:T(8,128)(2,1)}), bf16[16,64,128]{2,1,0:T(8,128)(2,1)S(1)}, u32[]{:S(2)}, u32[]{:S(2)}) async-start(bf16[16,64,128]{2,1,0:T(8,128)(2,1)} %get-tuple-element.26), calls=%async_computation.2 | async-start | bytes 524288 | tf_op jit(solution)/shard_map/all_to_all | solution.py:411

commit v11 on v10

--- a/solution.py
+++ b/solution.py
@@ -102,8 +102,12 @@
     along_z = dot_nt(coeffs_ref[...].reshape(1024, GRID), table).astype(bf16)
     for a in range(8):
         wide_ref[:, a, :] = dot_nn(table, along_z[a * GRID : (a + 1) * GRID])
-    out_ref[:, :64, :] = wide_ref[...].reshape(SHARES, 64, GRID).astype(bf16)
-    out_ref[:, 64:, :] = jnp.zeros((SHARES, 16, GRID), bf16)
+    out_ref[...] = wide_ref[...].reshape(SHARES, 64, GRID).astype(bf16)
+
+
+def attach_kernel(sections_ref, group_ref, out_ref):
+    out_ref[:, :64, :] = sections_ref[...]
+    out_ref[:, 64:, :] = jnp.broadcast_to(group_ref[...][None], (SHARES, 16, 128))
 
 
 def stats_kernel(
@@ -437,11 +441,15 @@
     (sections,) = call(
         section_kernel,
         [coeffs, table],
+        [((SHARES, 64, GRID), bf16)],
+        [((GRID, 8, GRID), f32)],
+    )
+    (message,) = call(
+        attach_kernel,
+        [sections, group.reshape(SHARES, 128)],
         [((SHARES, 80, GRID), bf16)],
-        [((GRID, 8, GRID), f32)],
-    )
-    rows = jnp.broadcast_to(group.reshape(1, SHARES, 128), (SHARES, SHARES, 128))
-    got = exchange(lax.dynamic_update_slice(sections, rows, (0, 64, 0)), "gvec")
+    )
+    got = exchange(message, "gvec")
     stats, hot, halved, drawn, local = call(
         stats_kernel,
         [near_list, live_count, coeffs, v_local],

time: 80.6 us -> 80.7 us (level)
    pallas_call x8 -> x9, Pallas kernels: 17.6 us -> 17.7 us  [call(): pl.pallas_call(kernel, out_shape=shapes, in_specs=specs, out_specs=[VMEM]...]
  transfers between devices with their start and end apart: 3 -> 3, of which waited for: 3 -> 3; matrix products, arithmetic and copies ran while one was open for 0% -> 0% of each run, Pallas kernels for 12% -> 11%
where the time goes in v11:
time: 80.7 us; the launch traced here: 80.3 us
  starting transfers between devices  21.9 us (27%)
  waiting for transfers between devices  21.5 us (27%)
  blocking collectives  17.8 us (22%)
  Pallas kernels  17.7 us (22%)
  between operations  1.4 us (2%)
    all_to_all x3, starting transfers between devices, exchange(): return lax.all_to_all(block, axes, split_axis=0, concat_axis=0, tiled=True)  21.9 us
    all_to_all x3, waiting for transfers between devices, exchange(): return lax.all_to_all(block, axes, split_axis=0, concat_axis=0, tiled=True)  21.5 us
    all_to_all x1, blocking collectives, exchange(): return lax.all_to_all(block, axes, split_axis=0, concat_axis=0, tiled=True)  17.8 us
    pallas_call x9, Pallas kernels, call(): pl.pallas_call(kernel, out_shape=shapes, in_specs=specs, out_specs=[VMEM]...  17.7 us
  transfers between devices with their start and end apart: 3, of which 3 were waited for; matrix products, arithmetic and copies ran while one was open for 0% of the time, Pallas kernels for 11%

profile of v11, /device:TPU:1, one launch (start us, length us, event | category | flops | bytes accessed | tf_op | source)
XLA Modules:
  0.0 80.3 jit_solution(2570894108528829731)
XLA Ops:
  1.3 0.0 copy-start.1
  1.3 0.0 copy-start.3
  1.3 1.7 %shard_map.120 = bf16[16,1,128]{2,1,0:T(2,128)(2,1)} custom-call(s32[1,16]{1,0:T(1,128)} %bitcast.20, s32[1]{0:T(128)S(6)} %copy.19.count_ref, f32[3,1024]{1,0:T(4,128)} %pos_hbm.1, f32[1,1024]{1,0:T(1,128)} %bitcast.21), custom_call_target="tpu_custom_call" | custom-call | flops 2000000000 | bytes 1000000 | tf_op jit(solution)/shard_map/pallas_call | solution.py:403
  3.0 7.6 %all-to-all-start = ((bf16[16,1,128]{2,1,0:T(2,128)(2,1)}), bf16[16,1,128]{2,1,0:T(2,128)(2,1)S(1)}, u32[]{:S(2)}, u32[]{:S(2)}) async-start(bf16[16,1,128]{2,1,0:T(2,128)(2,1)} %shard_map.120), calls=%async_computation | async-start | bytes 16384 | tf_op jit(solution)/shard_map/all_to_all | solution.py:415
  10.6 0.0 copy-done.1
  10.6 0.0 copy-done.3
  10.6 0.6 shard_map.119.sections_ref
  11.2 5.7 %all-to-all-done = bf16[16,1,128]{2,1,0:T(2,128)(2,1)S(1)} async-done(((bf16[16,1,128]{2,1,0:T(2,128)(2,1)}), bf16[16,1,128]{2,1,0:T(2,128)(2,1)S(1)}, u32[]{:S(2)}, u32[]{:S(2)}) %all-to-all-start) | async-done | bytes 4128 | tf_op jit(solution)/shard_map/all_to_all | solution.py:415
  16.9 0.7 shard_map.121
  17.7 0.0 copy-start
  17.7 0.0 copy-start.2
  17.7 10.7 %all-to-all-start.1 = ((bf16[16,80,128]{2,1,0:T(8,128)(2,1)}), bf16[16,80,128]{2,1,0:T(8,128)(2,1)S(1)}, u32[]{:S(2)}, u32[]{:S(2)}) async-start(bf16[16,80,128]{2,1,0:T(8,128)(2,1)} %shard_map.121), calls=%async_computation.1 | async-start | bytes 655360 | tf_op jit(solution)/shard_map/all_to_all | solution.py:415
  28.4 0.0 copy-done
  28.4 0.0 copy-done.2
  28.4 1.3 %shard_map.122 = (f32[1,128]{1,0:T(1,128)S(1)}, bf16[128,1024]{1,0:T(8,128)(2,1)S(1)}, f32[8,128,128]{2,1,0:T(8,128)S(1)}, f32[8,128,128]{2,1,0:T(8,128)S(1)}, f32[8,128,128]{2,1,0:T(8,128)S(1)}) custom-call(s32[16]{0:T(128)S(1)} %copy-done.2, s32[1]{0:T(128)S(6)} %copy.19.count_ref, bf16[8,128,128]{2,1,0:T(8,128)(2,1)S(1)} %bitcast.18, ...), custom_call_target="tpu_custom_call" | custom-call | flops 2000000000 | bytes 1000000 | tf_op jit(solution)/shard_map/pallas_call | solution.py:403
  29.7 0.0 copy-start.4
  29.8 11.7 %all-to-all-done.1.got_ref = bf16[16,80,128]{2,1,0:T(8,128)(2,1)S(1)} async-done(((bf16[16,80,128]{2,1,0:T(8,128)(2,1)}), bf16[16,80,128]{2,1,0:T(8,128)(2,1)S(1)}, u32[]{:S(2)}, u32[]{:S(2)}) %all-to-all-start.1) | async-done | bytes 327712 | tf_op jit(solution)/shard_map/all_to_all | solution.py:415
  41.5 3.2 %shard_map.123 = (f32[8,128,128]{2,1,0:T(8,128)S(1)}, f32[8,1024]{1,0:T(8,128)S(1)}, f32[256,128]{1,0:T(8,128)S(1)}) custom-call(bf16[16,80,128]{2,1,0:T(8,128)(2,1)S(1)} %all-to-all-done.1.got_ref), custom_call_target="tpu_custom_call" | custom-call | flops 2000000000 | bytes 1000000 | tf_op jit(solution)/shard_map/pallas_call | solution.py:403
  44.7 0.0 copy-done.4
  44.7 1.1 %shard_map.124 = (bf16[16,64,128]{2,1,0:T(8,128)(2,1)}, f32[8,128,128]{2,1,0:T(8,128)S(1)}, f32[1,128]{1,0:T(1,128)S(1)}) custom-call(bf16[16,80,128]{2,1,0:T(8,128)(2,1)S(1)} %all-to-all-done.1.got_ref, f32[8,128,128]{2,1,0:T(8,128)S(1)} %get-tuple-element.23.local_ref, bf16[128,128]{1,0:T(8,128)(2,1)S(1)} %copy-done.3, bf16[128,128]{1,0:T(8,128)(2,1)S(1)} %copy-done.4, ...), custom_call_target="tpu_custom_call" | custom-call | flops 2000000000 | bytes 1000000 | tf_op jit(solution)/shard_map/pallas_call | solution.py:403
  45.9 3.6 %all-to-all-start.2 = ((bf16[16,64,128]{2,1,0:T(8,128)(2,1)}), bf16[16,64,128]{2,1,0:T(8,128)(2,1)S(1)}, u32[]{:S(2)}, u32[]{:S(2)}) async-start(bf16[16,64,128]{2,1,0:T(8,128)(2,1)} %get-tuple-element.26), calls=%async_computation.2 | async-start | bytes 524288 | tf_op jit(solution)/shard_map/all_to_all | solution.py:415
  49.5 6.8 %shard_map.125.force_ref = f32[256,128]{1,0:T(8,128)S(1)} custom-call(f32[256,128]{1,0:T(8,128)S(1)} %get-tuple-element.27.blocks_ref, f32[8,128,128]{2,1,0:T(8,128)S(1)} %get-tuple-element.28.density_ref, f32[8,1024]{1,0:T(8,128)S(1)} %get-tuple-element.29.slots_ref), custom_call_target="tpu_custom_call" | custom-call | flops 2000000000 | bytes 1000000 | tf_op jit(solution)/shard_map/pallas_call | solution.py:403
  56.3 4.1 %all-to-all-done.2.got_ref = bf16[16,64,128]{2,1,0:T(8,128)(2,1)S(1)} async-done(((bf16[16,64,128]{2,1,0:T(8,128)(2,1)}), bf16[16,64,128]{2,1,0:T(8,128)(2,1)S(1)}, u32[]{:S(2)}, u32[]{:S(2)}) %all-to-all-start.2) | async-done | bytes 262176 | tf_op jit(solution)/shard_map/all_to_all | solution.py:415
  60.4 1.1 %shard_map.126 = (f32[8,128,128]{2,1,0:T(8,128)S(1)}, f32[256,128]{1,0:T(8,128)S(1)}) custom-call(bf16[16,64,128]{2,1,0:T(8,128)(2,1)S(1)} %all-to-all-done.2.got_ref, bf16[8,128,128]{2,1,0:T(8,128)(2,1)S(1)} %bitcast.19, bf16[128,128]{1,0:T(8,128)(2,1)S(1)} %copy-done.3, bf16[128,128]{1,0:T(8,128)(2,1)S(1)} %copy-done.4, ...), custom_call_target="tpu_custom_call" | custom-call | flops 2000000000 | bytes 1000000 | tf_op jit(solution)/shard_map/pallas_call | solution.py:403
  61.5 17.8 %all_to_all.20 = f32[256,1,128]{2,1,0:T(1,128)S(1)} all-to-all(f32[256,1,128]{2,1,0:T(1,128)S(1)} %bitcast.15), channel_id=1, replica_groups=mesh['band'=4,'gvec'=16,'dom'=4] {'gvec','band','dom'}, dimensions={0} | all-to-all | bytes 262144 | tf_op jit(solution)/shard_map/all_to_all | solution.py:415
  79.3 1.0 %shard_map.127 = (bf16[8,128,128]{2,1,0:T(8,128)(2,1)}, f32[3,1024]{1,0:T(4,128)}, f32[1,1]{1,0:T(1,128)}, f32[1,1]{1,0:T(1,128)}, f32[1,8]{1,0:T(1,128)}) custom-call(f32[256,128]{1,0:T(8,128)S(1)} %bitcast.14, f32[8,128,128]{2,1,0:T(8,128)S(1)} %get-tuple-element.33.ahead_ref, f32[8,128,128]{2,1,0:T(8,128)S(1)} %get-tuple-element.34.drawn_ref, ...), custom_call_target="tpu_custom_call" | custom-call | flops 2000000000 | bytes 1000000 | tf_op jit(solution)/shard_map/pallas_call | solution.py:403
  (1 shorter events, 0.0 us)
Async XLA Ops:
  1.3 9.3 %copy-start.1 = (bf16[1,8,128,128]{3,2,1,0:T(8,128)(2,1)S(1)}, bf16[1,8,128,128]{3,2,1,0:T(8,128)(2,1)}, u32[]{:S(2)}) copy-start(bf16[1,8,128,128]{3,2,1,0:T(8,128)(2,1)} %param.8) | copy-start | bytes 786436
  1.3 9.3 %copy-start.3 = (bf16[128,128]{1,0:T(8,128)(2,1)S(1)}, bf16[128,128]{1,0:T(8,128)(2,1)}, u32[]{:S(2)}) copy-start(bf16[128,128]{1,0:T(8,128)(2,1)} %constant.4.clone.table_ref) | copy-start | bytes 98308
  3.0 13.9 %all-to-all-start = ((bf16[16,1,128]{2,1,0:T(2,128)(2,1)}), bf16[16,1,128]{2,1,0:T(2,128)(2,1)S(1)}, u32[]{:S(2)}, u32[]{:S(2)}) async-start(bf16[16,1,128]{2,1,0:T(2,128)(2,1)} %shard_map.120), calls=%async_computation | async-start | bytes 16384 | tf_op jit(solution)/shard_map/all_to_all | solution.py:415
  17.7 10.7 %copy-start = (bf16[128,8,128]{2,1,0:T(8,128)(2,1)S(1)}, bf16[128,8,128]{2,1,0:T(8,128)(2,1)}, u32[]{:S(2)}) copy-start(bf16[128,8,128]{2,1,0:T(8,128)(2,1)} %local_ref.1) | copy-start | bytes 786436
  17.7 10.7 %copy-start.2 = (s32[16]{0:T(128)S(1)}, s32[16]{0:T(128)}, u32[]{:S(2)}) copy-start(s32[16]{0:T(128)} %near_ref.1) | copy-start | bytes 196
  17.7 23.8 %all-to-all-start.1 = ((bf16[16,80,128]{2,1,0:T(8,128)(2,1)}), bf16[16,80,128]{2,1,0:T(8,128)(2,1)S(1)}, u32[]{:S(2)}, u32[]{:S(2)}) async-start(bf16[16,80,128]{2,1,0:T(8,128)(2,1)} %shard_map.121), calls=%async_computation.1 | async-start | bytes 655360 | tf_op jit(solution)/shard_map/all_to_all | solution.py:415
  29.7 15.0 %copy-start.4 = (bf16[128,128]{1,0:T(8,128)(2,1)S(1)}, bf16[128,128]{1,0:T(8,128)(2,1)}, u32[]{:S(2)}) copy-start(bf16[128,128]{1,0:T(8,128)(2,1)} %constant.5.clone.turned_ref) | copy-start | bytes 98308
  45.9 14.5 %all-to-all-start.2 = ((bf16[16,64,128]{2,1,0:T(8,128)(2,1)}), bf16[16,64,128]{2,1,0:T(8,128)(2,1)S(1)}, u32[]{:S(2)}, u32[]{:S(2)}) async-start(bf16[16,64,128]{2,1,0:T(8,128)(2,1)} %get-tuple-element.26), calls=%async_computation.2 | async-start | bytes 524288 | tf_op jit(solution)/shard_map/all_to_all | solution.py:415
